TPU v7x, 32 devices: a whole 2x2x4 slice. The times are simulated.
32 devices in a mesh: section: 2 (over y), dp: 16 (over z, x, core).
Axes of the slice: x: 2, y: 2, z: 4, core: 2. Of those that a mesh axis runs over, the one named last changes fastest.
Arguments:
- section_in: bfloat16 [2, 4096, 768], P('section', 'dp'), may hold values from -6 to 6
- segment_ids: int32 [2, 4096], P(None, 'dp'), may hold values from 0 to 3, as said below
- out_cot: float32 [2, 4096, 1024], P('section', 'dp'), may hold values from -6 to 6
- in_proj: float32 [2, 768, 1024], P('section', 'dp'), may hold values from -0.21875 to 0.21875
- attn_in: float32 [2, 1024, 3072], P('section', 'dp'), may hold values from -0.1875 to 0.1875
- attn_out: float32 [2, 1024, 1024], P('section', 'dp'), may hold values from -1 to 1
- ffn_in: float32 [2, 1024, 4096], P('section', 'dp'), may hold values from -0.1875 to 0.1875
- ffn_out: float32 [2, 4096, 1024], P('section', 'dp'), may hold values from -0.09375 to 0.09375
- norm_gain: float32 [2, 3, 1024], P('section', None, 'dp'), may hold values from 0.5 to 1.5
- norm_bias: float32 [2, 3, 1024], P('section', None, 'dp'), may hold values from -1.75 to 1.75
- cross_in: float32 [1024, 3072], P(('section', 'dp')), may hold values from -0.1875 to 0.1875
- cross_out: float32 [1024, 1024], P(('section', 'dp')), may hold values from -1 to 1
- cross_gain: float32 [1024], P(('section', 'dp')), may hold values from 0.5 to 1.5
- cross_bias: float32 [1024], P(('section', 'dp')), may hold values from -1.75 to 1.75
Outputs:
- section_out: float32 [2, 4096, 1024], P('section', 'dp')
- in_grad: float32 [2, 4096, 768], P('section', 'dp')
- in_proj_grad: float32 [2, 768, 1024], P('section', 'dp')
- attn_in_grad: float32 [2, 1024, 3072], P('section', 'dp')
- attn_out_grad: float32 [2, 1024, 1024], P('section', 'dp')
- ffn_in_grad: float32 [2, 1024, 4096], P('section', 'dp')
- ffn_out_grad: float32 [2, 4096, 1024], P('section', 'dp')
- gain_grad: float32 [2, 3, 1024], P('section', None, 'dp')
- bias_grad: float32 [2, 3, 1024], P('section', None, 'dp')
- cross_in_grad: float32 [1024, 3072], P(('section', 'dp'))
- cross_out_grad: float32 [1024, 1024], P(('section', 'dp'))
- cross_gain_grad: float32 [1024], P(('section', 'dp'))
- cross_bias_grad: float32 [1024], P(('section', 'dp'))
Inputs may be any that keep to these rules, and one draw needn't show every extreme that they name: `segment_ids`: within each row and each sequence of 128 tokens the ids never fall, start at 0 and take every value up to 3.
All inputs are finite; a program needn't handle non-finite values.
Results may differ from a plain program's by a relative error of at most 0.018.
Values may be sent and summed in bfloat16 or wider, within the bound.
No kernel may reach another device: no remote copies, remote signals or barrier semaphores. Data moves between devices by JAX's collectives and lax.ppermute only.
A program may use at most 768 MiB of HBM per device.

v0:
```python
import math

import jax
import jax.numpy as jnp
from jax import lax
from jax.sharding import PartitionSpec as P

HEAD_DIM = 64
SEQ = 128


NEG_FILL = -1000000000.0


def from_behind(value, axis, steps):
    count = lax.axis_size(axis)
    initial, last = (max(0, -steps), min(count, count - steps))
    return lax.ppermute(value, axis, [(source, source + steps) for source in range(initial, last)])


def shortened(x):

    def short(part):
        return part.astype(jnp.bfloat16) if part.dtype == jnp.float32 else part

    return jax.tree.map(short, x)


def matmul_low(left_side, right_side):
    return jnp.dot(left_side, right_side, preferred_element_type=jnp.float32)


def outer_sum(left_side, right_side):
    return jnp.einsum("ti,to->io", left_side, right_side, preferred_element_type=jnp.float32)


def back_project(upstream, weight):
    return jnp.einsum("to,io->ti", upstream, weight, preferred_element_type=jnp.float32)


def norm_forward(values, gain_row, bias_row):
    centre = values - jnp.mean(values, axis=-1, keepdims=True)
    inverse = lax.rsqrt(jnp.mean(centre * centre, axis=-1, keepdims=True) + 1e-05)
    normed = centre * inverse
    return (normed * gain_row + bias_row, normed, inverse)


def norm_backward(upstream, normed, inverse, gain_row):
    scaled = upstream * gain_row
    grad_in = inverse * (
        scaled
        - jnp.mean(scaled, axis=-1, keepdims=True)
        - normed * jnp.mean(scaled * normed, axis=-1, keepdims=True)
    )
    return (grad_in, jnp.sum(upstream * normed, axis=0), jnp.sum(upstream, axis=0))


def split_heads(values):
    return values.reshape(values.shape[0], values.shape[1] // HEAD_DIM, HEAD_DIM)


def attend(queries, key_rows, value_rows, allowed):
    factor = HEAD_DIM ** (-0.5)
    scores = jnp.einsum(
        "qhd,khd->hqk",
        split_heads(queries),
        split_heads(key_rows),
        preferred_element_type=jnp.float32,
    )
    logits = jnp.where(allowed[None], scores * factor, NEG_FILL)
    exponent = jnp.exp(logits - jnp.max(logits, axis=-1, keepdims=True))
    attn_probs = exponent / jnp.sum(exponent, axis=-1, keepdims=True)
    blended = jnp.einsum(
        "hqk,khd->qhd",
        attn_probs.astype(jnp.bfloat16),
        split_heads(value_rows),
        preferred_element_type=jnp.float32,
    )
    return (blended.reshape(queries.shape).astype(jnp.bfloat16), attn_probs)


def attend_back(grad_blended, queries, key_rows, value_rows, attn_probs):
    factor = HEAD_DIM ** (-0.5)
    grad_heads = split_heads(grad_blended)
    grad_probs = jnp.einsum(
        "qhd,khd->hqk", grad_heads, split_heads(value_rows), preferred_element_type=jnp.float32
    )
    grad_values = jnp.einsum(
        "hqk,qhd->khd",
        attn_probs.astype(jnp.bfloat16),
        grad_heads,
        preferred_element_type=jnp.float32,
    )
    centred = jnp.sum(attn_probs * grad_probs, axis=-1, keepdims=True)
    grad_scores = (attn_probs * (grad_probs - centred) * factor).astype(jnp.bfloat16)
    grad_queries = jnp.einsum(
        "hqk,khd->qhd", grad_scores, split_heads(key_rows), preferred_element_type=jnp.float32
    )
    grad_keys = jnp.einsum(
        "hqk,qhd->khd", grad_scores, split_heads(queries), preferred_element_type=jnp.float32
    )
    return (
        grad_queries.reshape(queries.shape),
        grad_keys.reshape(key_rows.shape),
        grad_values.reshape(value_rows.shape),
    )


def layer_forward(tokens_in, own_rows, memory, mem_rows, section_w, cross_w, decoder):
    w_in, w_qkv, w_attn, w_up, w_down, gain_rows, bias_rows = section_w
    gain_rows = gain_rows.astype(jnp.float32)
    bias_rows = bias_rows.astype(jnp.float32)
    width = w_attn.shape[0]
    embedded = matmul_low(tokens_in, w_in)
    first, normed_a, inverse_a = norm_forward(embedded, gain_rows[0], bias_rows[0])
    first_low = first.astype(jnp.bfloat16)
    packed = matmul_low(first_low, w_qkv).astype(jnp.bfloat16)
    allowed = own_rows[:, None] == own_rows[None, :]
    if decoder:
        places = jnp.arange(tokens_in.shape[0])
        allowed = allowed & (places[None, :] <= places[:, None])
    blended, probs_self = attend(
        packed[:, :width], packed[:, width : 2 * width], packed[:, 2 * width :], allowed
    )
    second, normed_b, inverse_b = norm_forward(
        first + matmul_low(blended, w_attn), gain_rows[1], bias_rows[1]
    )
    cache = {
        "normed_a": normed_a,
        "inverse_a": inverse_a,
        "first_low": first_low,
        "packed": packed,
        "probs_self": probs_self,
        "blended": blended,
        "normed_b": normed_b,
        "inverse_b": inverse_b,
    }
    if decoder:
        wc_in, wc_out, cross_gain, cross_bias = cross_w
        second_low = second.astype(jnp.bfloat16)
        cross_q = matmul_low(second_low, wc_in[:, :width]).astype(jnp.bfloat16)
        cross_kv = matmul_low(memory, wc_in[:, width:]).astype(jnp.bfloat16)
        cross_mask = own_rows[:, None] == mem_rows[None, :]
        cross_mix, probs_cross = attend(
            cross_q, cross_kv[:, :width], cross_kv[:, width:], cross_mask
        )
        third, normed_c, inverse_c = norm_forward(
            second + matmul_low(cross_mix, wc_out),
            cross_gain.astype(jnp.float32),
            cross_bias.astype(jnp.float32),
        )
        cache.update(
            {
                "second_low": second_low,
                "cross_q": cross_q,
                "cross_kv": cross_kv,
                "probs_cross": probs_cross,
                "cross_mix": cross_mix,
                "normed_c": normed_c,
                "inverse_c": inverse_c,
            }
        )
    else:
        third = second
    third_low = third.astype(jnp.bfloat16)
    inner = matmul_low(third_low, w_up)
    active = jax.nn.gelu(inner, approximate=False).astype(jnp.bfloat16)
    output, normed_d, inverse_d = norm_forward(
        third + matmul_low(active, w_down), gain_rows[2], bias_rows[2]
    )
    cache.update(
        {
            "third_low": third_low,
            "inner": inner,
            "active": active,
            "normed_d": normed_d,
            "inverse_d": inverse_d,
        }
    )
    return (output, cache)


def layer_backward(grad_output, tokens_in, memory, section_w, cross_w, cache, decoder):
    w_in, w_qkv, w_attn, w_up, w_down, gain_rows, bias_rows = section_w
    gain_rows = gain_rows.astype(jnp.float32)
    width = w_attn.shape[0]
    grad_third, gain_last, bias_last = norm_backward(
        grad_output, cache["normed_d"], cache["inverse_d"], gain_rows[2]
    )
    grad_branch = grad_third.astype(jnp.bfloat16)
    grad_down = outer_sum(cache["active"], grad_branch)
    inner = cache["inner"]
    slope = 0.5 * (1.0 + lax.erf(inner / math.sqrt(2.0))) + inner * jnp.exp(
        -0.5 * inner * inner
    ) / math.sqrt(2.0 * math.pi)
    grad_inner = (back_project(grad_branch, w_down) * slope).astype(jnp.bfloat16)
    grad_up = outer_sum(cache["third_low"], grad_inner)
    grad_third = grad_third + back_project(grad_inner, w_up)
    if decoder:
        wc_in, wc_out, cross_gain, cross_bias = cross_w
        grad_resid, grad_cgain, grad_cbias = norm_backward(
            grad_third, cache["normed_c"], cache["inverse_c"], cross_gain.astype(jnp.float32)
        )
        grad_cbranch = grad_resid.astype(jnp.bfloat16)
        grad_cout = outer_sum(cache["cross_mix"], grad_cbranch)
        grad_cmix = back_project(grad_cbranch, wc_out).astype(jnp.bfloat16)
        cross_kv = cache["cross_kv"]
        grad_cq, grad_ck, grad_cv = attend_back(
            grad_cmix,
            cache["cross_q"],
            cross_kv[:, :width],
            cross_kv[:, width:],
            cache["probs_cross"],
        )
        grad_cq = grad_cq.astype(jnp.bfloat16)
        grad_ckv = jnp.concatenate([grad_ck, grad_cv], axis=1).astype(jnp.bfloat16)
        grad_cin = jnp.concatenate(
            [outer_sum(cache["second_low"], grad_cq), outer_sum(memory, grad_ckv)], axis=1
        )
        grad_memory = back_project(grad_ckv, wc_in[:, width:]).astype(jnp.bfloat16)
        grad_second = grad_resid + back_project(grad_cq, wc_in[:, :width])
        cross_grads = (grad_cin, grad_cout, grad_cgain, grad_cbias)
    else:
        grad_second = grad_third
        grad_memory = jnp.zeros((tokens_in.shape[0], width), jnp.bfloat16)
        cross_grads = tuple((jnp.zeros(item.shape, jnp.float32) for item in cross_w))
    grad_resid_b, gain_mid, bias_mid = norm_backward(
        grad_second, cache["normed_b"], cache["inverse_b"], gain_rows[1]
    )
    grad_abranch = grad_resid_b.astype(jnp.bfloat16)
    grad_attn = outer_sum(cache["blended"], grad_abranch)
    grad_blended = back_project(grad_abranch, w_attn).astype(jnp.bfloat16)
    packed = cache["packed"]
    grad_q, grad_k, grad_v = attend_back(
        grad_blended,
        packed[:, :width],
        packed[:, width : 2 * width],
        packed[:, 2 * width :],
        cache["probs_self"],
    )
    grad_packed = jnp.concatenate([grad_q, grad_k, grad_v], axis=1).astype(jnp.bfloat16)
    grad_qkv = outer_sum(cache["first_low"], grad_packed)
    grad_first = grad_resid_b + back_project(grad_packed, w_qkv)
    grad_embed, gain_first, bias_first = norm_backward(
        grad_first, cache["normed_a"], cache["inverse_a"], gain_rows[0]
    )
    grad_embed_low = grad_embed.astype(jnp.bfloat16)
    grad_in = outer_sum(tokens_in, grad_embed_low)
    grad_tokens = back_project(grad_embed_low, w_in)
    gain_grads = jnp.stack([gain_first, gain_mid, gain_last])
    bias_grads = jnp.stack([bias_first, bias_mid, bias_last])
    section_grads = (grad_in, grad_qkv, grad_attn, grad_up, grad_down, gain_grads, bias_grads)
    return (section_grads + cross_grads, grad_tokens, grad_memory)


def shards(
    section_in,
    segment_ids,
    out_cot,
    in_proj,
    attn_in,
    attn_out,
    ffn_in,
    ffn_out,
    norm_gain,
    norm_bias,
    cross_in,
    cross_out,
    cross_gain,
    cross_bias,
):
    section_id = lax.axis_index("section")
    local_in = in_proj[0].astype(jnp.bfloat16)
    local_qkv = attn_in[0].astype(jnp.bfloat16)
    local_attn = attn_out[0].astype(jnp.bfloat16)
    local_up = ffn_in[0].astype(jnp.bfloat16)
    local_down = ffn_out[0].astype(jnp.bfloat16)
    local_gain = norm_gain[0].astype(jnp.bfloat16)
    local_bias = norm_bias[0].astype(jnp.bfloat16)
    local_cin = cross_in.astype(jnp.bfloat16)
    local_cout = cross_out.astype(jnp.bfloat16)
    local_cgain = cross_gain.astype(jnp.bfloat16)
    local_cbias = cross_bias.astype(jnp.bfloat16)
    section_w = (
        lax.all_gather(local_in, "dp", axis=0, tiled=True),
        lax.all_gather(local_qkv, "dp", axis=0, tiled=True),
        lax.all_gather(local_attn, "dp", axis=0, tiled=True),
        lax.all_gather(local_up, "dp", axis=0, tiled=True),
        lax.all_gather(local_down, "dp", axis=0, tiled=True),
        lax.all_gather(local_gain, "dp", axis=1, tiled=True),
        lax.all_gather(local_bias, "dp", axis=1, tiled=True),
    )
    cross_w = (
        lax.all_gather(local_cin, ("section", "dp"), axis=0, tiled=True),
        lax.all_gather(local_cout, ("section", "dp"), axis=0, tiled=True),
        lax.all_gather(local_cgain, ("section", "dp"), axis=0, tiled=True),
        lax.all_gather(local_cbias, ("section", "dp"), axis=0, tiled=True),
    )
    own_tokens = section_in[0]
    total_rows = own_tokens.shape[0]
    in_width = own_tokens.shape[1]
    batches = total_rows // SEQ
    width = section_w[2].shape[0]
    own_segments = lax.dynamic_index_in_dim(segment_ids, section_id, 0, keepdims=False)
    enc_segments = segment_ids[0]

    def run_spare(tokens_in, own_rows, memory, mem_rows):
        return jnp.zeros((SEQ, width), jnp.float32)

    def run_encoder(tokens_in, own_rows, memory, mem_rows):
        return layer_forward(tokens_in, own_rows, memory, mem_rows, section_w, cross_w, False)[0]

    def run_decoder(tokens_in, own_rows, memory, mem_rows):
        return layer_forward(tokens_in, own_rows, memory, mem_rows, section_w, cross_w, True)[0]

    incoming = jnp.zeros((SEQ, width), jnp.bfloat16)
    memories = jnp.zeros((total_rows, width), jnp.bfloat16)
    outputs = jnp.zeros((total_rows, width), jnp.float32)
    for step in range(batches + 1):
        index = step - section_id
        valid = (index >= 0) & (index < batches)
        start = jnp.clip(index, 0, batches - 1) * SEQ
        tokens_in = lax.dynamic_slice_in_dim(own_tokens, start, SEQ, 0)
        own_rows = lax.dynamic_slice_in_dim(own_segments, start, SEQ, 0)
        mem_rows = lax.dynamic_slice_in_dim(enc_segments, start, SEQ, 0)
        memories = jnp.where(
            valid, lax.dynamic_update_slice_in_dim(memories, incoming, start, 0), memories
        )
        branch = jnp.where(valid, 1 + section_id, 0)
        result = lax.switch(
            branch, (run_spare, run_encoder, run_decoder), tokens_in, own_rows, incoming, mem_rows
        )
        outputs = jnp.where(
            valid, lax.dynamic_update_slice_in_dim(outputs, result, start, 0), outputs
        )
        if step < batches:
            incoming = from_behind(result.astype(jnp.bfloat16), "section", 1)
    section_w = (
        lax.all_gather(local_in, "dp", axis=0, tiled=True),
        lax.all_gather(local_qkv, "dp", axis=0, tiled=True),
        lax.all_gather(local_attn, "dp", axis=0, tiled=True),
        lax.all_gather(local_up, "dp", axis=0, tiled=True),
        lax.all_gather(local_down, "dp", axis=0, tiled=True),
        lax.all_gather(local_gain, "dp", axis=1, tiled=True),
        lax.all_gather(local_bias, "dp", axis=1, tiled=True),
    )
    cross_w = (
        lax.all_gather(local_cin, ("section", "dp"), axis=0, tiled=True),
        lax.all_gather(local_cout, ("section", "dp"), axis=0, tiled=True),
        lax.all_gather(local_cgain, ("section", "dp"), axis=0, tiled=True),
        lax.all_gather(local_cbias, ("section", "dp"), axis=0, tiled=True),
    )

    def back_spare(tokens_in, own_rows, memory, mem_rows, grad_output):
        blank = tuple((jnp.zeros(item.shape, jnp.float32) for item in section_w + cross_w))
        return (
            blank,
            jnp.zeros((SEQ, in_width), jnp.float32),
            jnp.zeros((SEQ, width), jnp.bfloat16),
        )

    def back_encoder(tokens_in, own_rows, memory, mem_rows, grad_output):
        output, cache = layer_forward(
            tokens_in, own_rows, memory, mem_rows, section_w, cross_w, False
        )
        return layer_backward(grad_output, tokens_in, memory, section_w, cross_w, cache, False)

    def back_decoder(tokens_in, own_rows, memory, mem_rows, grad_output):
        output, cache = layer_forward(
            tokens_in, own_rows, memory, mem_rows, section_w, cross_w, True
        )
        return layer_backward(grad_output, tokens_in, memory, section_w, cross_w, cache, True)

    returned = jnp.zeros((SEQ, width), jnp.bfloat16)
    in_grads = jnp.zeros((total_rows, in_width), jnp.float32)
    totals = tuple((jnp.zeros(item.shape, jnp.float32) for item in section_w + cross_w))
    section_parts = tuple(
        (
            jnp.zeros(item.shape, jnp.float32)
            for item in (
                local_in,
                local_qkv,
                local_attn,
                local_up,
                local_down,
                local_gain,
                local_bias,
            )
        )
    )
    cross_parts = tuple(
        (
            jnp.zeros(item.shape, jnp.float32)
            for item in (local_cin, local_cout, local_cgain, local_cbias)
        )
    )
    for step in range(batches + 1):
        index = batches - step - section_id
        valid = (index >= 0) & (index < batches)
        start = jnp.clip(index, 0, batches - 1) * SEQ
        tokens_in = lax.dynamic_slice_in_dim(own_tokens, start, SEQ, 0)
        own_rows = lax.dynamic_slice_in_dim(own_segments, start, SEQ, 0)
        mem_rows = lax.dynamic_slice_in_dim(enc_segments, start, SEQ, 0)
        memory = lax.dynamic_slice_in_dim(memories, start, SEQ, 0)
        grad_output = lax.dynamic_slice_in_dim(out_cot[0], start, SEQ, 0) + returned.astype(
            jnp.float32
        )
        branch = jnp.where(valid, 1 + section_id, 0)
        grads, grad_tokens, grad_memory = lax.switch(
            branch,
            (back_spare, back_encoder, back_decoder),
            tokens_in,
            own_rows,
            memory,
            mem_rows,
            grad_output,
        )
        in_grads = jnp.where(
            valid, lax.dynamic_update_slice_in_dim(in_grads, grad_tokens, start, 0), in_grads
        )
        totals = tuple((held + fresh for held, fresh in zip(totals, grads)))
        if step < batches:
            returned = jax.tree.map(
                lambda part, own: part.astype(own.dtype),
                from_behind(shortened(grad_memory), "section", -1),
                grad_memory,
            )
    section_parts = (
        lax.psum_scatter(totals[0], "dp", scatter_dimension=0, tiled=True),
        lax.psum_scatter(totals[1], "dp", scatter_dimension=0, tiled=True),
        lax.psum_scatter(totals[2], "dp", scatter_dimension=0, tiled=True),
        lax.psum_scatter(totals[3], "dp", scatter_dimension=0, tiled=True),
        lax.psum_scatter(totals[4], "dp", scatter_dimension=0, tiled=True),
        lax.psum_scatter(totals[5], "dp", scatter_dimension=1, tiled=True),
        lax.psum_scatter(totals[6], "dp", scatter_dimension=1, tiled=True),
    )
    cross_parts = (
        lax.psum_scatter(totals[7], ("section", "dp"), scatter_dimension=0, tiled=True),
        lax.psum_scatter(totals[8], ("section", "dp"), scatter_dimension=0, tiled=True),
        lax.psum_scatter(totals[9], ("section", "dp"), scatter_dimension=0, tiled=True),
        lax.psum_scatter(totals[10], ("section", "dp"), scatter_dimension=0, tiled=True),
    )
    return (
        outputs[None],
        in_grads[None],
        section_parts[0][None],
        section_parts[1][None],
        section_parts[2][None],
        section_parts[3][None],
        section_parts[4][None],
        section_parts[5][None],
        section_parts[6][None],
        cross_parts[0],
        cross_parts[1],
        cross_parts[2],
        cross_parts[3],
    )


def solution(mesh):
    placed = (
        P("section", "dp", None),
        P(None, "dp"),
        P("section", "dp", None),
        P("section", "dp", None),
        P("section", "dp", None),
        P("section", "dp", None),
        P("section", "dp", None),
        P("section", "dp", None),
        P("section", None, "dp"),
        P("section", None, "dp"),
        P(("section", "dp"), None),
        P(("section", "dp"), None),
        P(("section", "dp")),
        P(("section", "dp")),
    )
    return jax.shard_map(
        shards,
        mesh=mesh,
        in_specs=placed,
        out_specs=(
            P("section", "dp", None),
            P("section", "dp", None),
            P("section", "dp", None),
            P("section", "dp", None),
            P("section", "dp", None),
            P("section", "dp", None),
            P("section", "dp", None),
            P("section", None, "dp"),
            P("section", None, "dp"),
            P(("section", "dp"), None),
            P(("section", "dp"), None),
            P(("section", "dp")),
            P(("section", "dp")),
        ),
        check_vma=False,
    )
```

profile of v0, /device:TPU:0, one launch (start us, length us, event | category | flops | bytes accessed | tf_op | source)
XLA Modules:
  0.0 2098.0 jit_solution(8215674352097853074)
XLA Ops:
  16.4 24.8 %all-gather.1 = bf16[1,3,1024]{1,0,2:T(2,128)(2,1)S(1)} all-gather(bf16[1,3,64]{1,0,2:T(2,128)(2,1)S(1)} %copy.669), channel_id=3, replica_groups=mesh['section'=2,'dp'=16] {'dp'}, dimensions={2}, use_global_device_ids=true | all-gather | bytes 6528 | tf_op jit(solution)/shard_map/all_gather | solution.py:290
  41.6 19.9 all-gather.2
  62.3 38.8 %all-reduce.5 = (bf16[1024]{0:T(1024)(128)(2,1)S(1)}, bf16[1024]{0:T(1024)(128)(2,1)S(1)}) all-reduce(bf16[1024]{0:T(1024)(128)(2,1)S(1)} %dynamic-update-slice.11, bf16[1024]{0:T(1024)(128)(2,1)S(1)} %dynamic-update-slice.12), channel_id=1, replica_groups=mesh['section'=2,'dp'=16] {'section','dp'}, use_global_device_ids=true, to_apply=%add | all-reduce | flops 2048 | bytes 8192
  102.4 59.5 %all-gather.21.cloned.1.call-done = bf16[1,1024,3072]{2,1,0:T(8,128)(2,1)} async-done(((bf16[1,64,3072]{2,1,0:T(8,128)(2,1)}), bf16[1,1024,3072]{2,1,0:T(8,128)(2,1)}) %all-gather.21.cloned.1.call-update) | async-done | bytes 6291472 | tf_op jit(solution)/shard_map/all_gather | solution.py:286
  161.9 76.1 %all-gather.25.cloned.1.call-done = bf16[1,1024,4096]{2,1,0:T(8,128)(2,1)} async-done(((bf16[1,64,4096]{2,1,0:T(8,128)(2,1)}), bf16[1,1024,4096]{2,1,0:T(8,128)(2,1)}) %all-gather.25.cloned.1.call-update) | async-done | bytes 8388624 | tf_op jit(solution)/shard_map/all_gather | solution.py:288
  238.0 75.8 %all-gather.27.cloned.1.call-done = bf16[1,4096,1024]{2,1,0:T(8,128)(2,1)} async-done(((bf16[1,256,1024]{2,1,0:T(8,128)(2,1)}), bf16[1,4096,1024]{2,1,0:T(8,128)(2,1)}) %all-gather.27.cloned.1.call-update) | async-done | bytes 8388624 | tf_op jit(solution)/shard_map/all_gather | solution.py:289
  313.8 58.0 %all-gather.17.cloned.1.call-done = bf16[1024,1024]{1,0:T(8,128)(2,1)} async-done(((bf16[32,1024]{1,0:T(8,128)(2,1)}), bf16[1024,1024]{1,0:T(8,128)(2,1)}) %all-gather.17.cloned.1.call-update) | async-done | bytes 2097168 | tf_op jit(solution)/shard_map/all_gather | solution.py:295
  371.8 71.9 %all-gather.15.cloned.1.call-done = bf16[1024,3072]{1,0:T(8,128)(2,1)} async-done(((bf16[32,3072]{1,0:T(8,128)(2,1)}), bf16[1024,3072]{1,0:T(8,128)(2,1)}) %all-gather.15.cloned.1.call-update) | async-done | bytes 6291472 | tf_op jit(solution)/shard_map/all_gather | solution.py:294
  443.6 35.5 %conditional.6 = (f32[128,1024]{1,0:T(8,128)}) conditional(s32[]{:T(128)} %clamp.24, () %tuple.77, (bf16[128,768]{1,0:T(8,128)(2,1)}, bf16[768,1024]{1,0:T(8,128)(2,1)}, bf16[3,1024]{1,0:T(4,128)(2,1)S(1)}, bf16[3,1024]{1,0:T(4,128)(2,1)S(1)}, bf16[1024,3072]{1,0:T(8,128)(2,1)}, /*index=5*/s32[128]{0:T(128)}, ...), branch_computations={%region_0.1_spmd, %region_1.10_spmd, %region_10.23_spmd} | conditional | flops 4744092672 | bytes 81724568 | solution.py:330
  458.1 13.6 fusion.1199
  490.6 38.2 %conditional.7 = (f32[128,1024]{1,0:T(8,128)S(1)}) conditional(s32[]{:T(128)} %clamp.25, () %tuple.80, (bf16[128,768]{1,0:T(8,128)(2,1)S(1)}, bf16[768,1024]{1,0:T(8,128)(2,1)}, bf16[3,1024]{1,0:T(4,128)(2,1)S(1)}, bf16[3,1024]{1,0:T(4,128)(2,1)S(1)}, bf16[1024,3072]{1,0:T(8,128)(2,1)}, /*index=5*/s32[128]{0:T(128)S(1)}, ...), branch_computations={%region_23.24_spmd, %region_24.33_spmd, %region_33.46_spmd} | conditional | flops 4744092672 | bytes 67306648 | solution.py:330
  510.4 13.5 fusion.1220
  530.8 14.2 collective-permute-start.1
  551.3 37.5 %conditional.9 = (f32[1024,3072]{1,0:T(8,128)}, f32[1024,1024]{1,0:T(8,128)}, f32[1024,4096]{1,0:T(8,128)S(1)}, f32[4096,1024]{1,0:T(8,128)}, f32[3,1024]{1,0:T(...) conditional(s32[]{:T(128)} %clamp.26, () %tuple.86, ...), branch_computations={%region_69.70_spmd, %region_70.92_spmd, %region_92.123_spmd} | conditional | flops 14143806464 | bytes 359808128 | solution.py:409
  590.1 139.8 %collective-permute-done.2 = bf16[128,1024]{1,0:T(8,128)(2,1)S(1)} collective-permute-done((bf16[128,1024]{1,0:T(8,128)(2,1)}, bf16[128,1024]{1,0:T(8,128)(2,1)S(1)}, u32[]{:S(2)}, u32[]{:S(2)}) %collective-permute-start.2) | collective-permute-done | bytes 262176 | tf_op jit(solution)/shard_map/ppermute | solution.py:18
  731.9 121.5 %conditional.10 = (f32[1024,3072]{1,0:T(8,128)}, f32[1024,1024]{1,0:T(8,128)}, f32[1024,4096]{1,0:T(8,128)}, f32[4096,1024]{1,0:T(8,128)}, f32[3,1024]{1,0:T(4,1...) conditional(s32[]{:T(128)} %clamp.25, () %tuple.89, ...), branch_computations={%region_123.124_spmd, %region_124.146_spmd, %region_146.177_spmd} | conditional | flops 14143806464 | bytes 365096160 | solution.py:409
  809.9 10.1 fusion.881
  854.7 49.9 %collective-permute-done.3 = bf16[128,1024]{1,0:T(8,128)(2,1)S(1)} collective-permute-done((bf16[128,1024]{1,0:T(8,128)(2,1)}, bf16[128,1024]{1,0:T(8,128)(2,1)S(1)}, u32[]{:S(2)}, u32[]{:S(2)}) %collective-permute-start.3) | collective-permute-done | bytes 262176 | tf_op jit(solution)/shard_map/ppermute | solution.py:18
  906.5 118.8 %conditional.11 = (f32[1024,3072]{1,0:T(8,128)}, f32[1024,1024]{1,0:T(8,128)}, f32[1024,4096]{1,0:T(8,128)}, f32[4096,1024]{1,0:T(8,128)}, f32[3,1024]{1,0:T(4,1...) conditional(s32[]{:T(128)} %clamp.24, () %tuple.92, ...), branch_computations={%region_177.178_spmd, %region_178.200_spmd, %region_200.231_spmd} | conditional | flops 13605755904 | bytes 354484384 | solution.py:409
  980.1 10.2 fusion.1056
  1053.4 19.1 add_add_fusion.2
  1072.5 19.0 add_add_fusion.3
  1091.6 24.0 %add_add_fusion = f32[4096,1024]{1,0:T(8,128)} fusion(f32[4096,1024]{1,0:T(8,128)} %get-tuple-element.646, f32[4096,1024]{1,0:T(8,128)} %get-tuple-element.644, f32[4096,1024]{1,0:T(8,128)} %get-tuple-element.645), kind=kLoop, calls=%fused_computation.1656 | loop fusion | flops 8388608 | bytes 67108864 | tf_op jit(solution)/shard_map/add | solution.py:421
  1115.7 23.4 %add_add_fusion.1 = f32[1024,4096]{1,0:T(8,128)} fusion(f32[1024,4096]{1,0:T(8,128)} %get-tuple-element.643, f32[1024,4096]{1,0:T(8,128)} %copy-done.8, f32[1024,4096]{1,0:T(8,128)} %get-tuple-element.642), kind=kLoop, calls=%fused_computation.1657 | loop fusion | flops 8388608 | bytes 67108864 | tf_op jit(solution)/shard_map/add | solution.py:421
  1149.0 39.5 %all-reduce.4 = (f32[1024]{0:T(1024)S(1)}, f32[1024]{0:T(1024)S(1)}) all-reduce(f32[1024]{0:T(1024)S(1)} %add_add_fusion.10, f32[1024]{0:T(1024)S(1)} %add_add_fusion.9), channel_id=18, replica_groups=mesh['section'=2,'dp'=16] {'section','dp'}, use_global_device_ids=true, to_apply=%region_240.241.clone | all-reduce | flops 2048 | bytes 16384
  1193.6 16.5 reduce-scatter.14.cloned.1.call-done
  1210.1 75.8 %reduce-scatter.18.cloned.1.call-done = f32[64,1024]{1,0:T(8,128)} async-done(((f32[1024,1024]{1,0:T(8,128)}), f32[64,1024]{1,0:T(8,128)}) %reduce-scatter.18.cloned.1.call-update) | async-done | bytes 262160 | tf_op jit(solution)/shard_map/reduce_scatter | solution.py:431
  1285.9 143.1 %reduce-scatter.26.cloned.1.call-done = f32[32,1024]{1,0:T(8,128)} async-done(((f32[1024,1024]{1,0:T(8,128)}), f32[32,1024]{1,0:T(8,128)}) %reduce-scatter.26.cloned.1.call-update) | async-done | bytes 131088 | tf_op jit(solution)/shard_map/reduce_scatter | solution.py:439
  1429.0 159.5 %reduce-scatter.24.cloned.1.call-done = f32[32,3072]{1,0:T(8,128)} async-done(((f32[1024,3072]{1,0:T(8,128)}), f32[32,3072]{1,0:T(8,128)}) %reduce-scatter.24.cloned.1.call-update) | async-done | bytes 393232 | tf_op jit(solution)/shard_map/reduce_scatter | solution.py:438
  1588.4 138.4 %reduce-scatter.16.cloned.1.call-done = f32[64,3072]{1,0:T(8,128)} async-done(((f32[1024,3072]{1,0:T(8,128)}), f32[64,3072]{1,0:T(8,128)}) %reduce-scatter.16.cloned.1.call-update) | async-done | bytes 786448 | tf_op jit(solution)/shard_map/reduce_scatter | solution.py:430
  1726.8 182.3 %reduce-scatter.22.cloned.1.call-done = f32[256,1024]{1,0:T(8,128)} async-done(((f32[4096,1024]{1,0:T(8,128)}), f32[256,1024]{1,0:T(8,128)}) %reduce-scatter.22.cloned.1.call-update) | async-done | bytes 1048592 | tf_op jit(solution)/shard_map/reduce_scatter | solution.py:433
  1909.1 182.1 %reduce-scatter.20.cloned.1.call-done = f32[64,4096]{1,0:T(8,128)} async-done(((f32[1024,4096]{1,0:T(8,128)}), f32[64,4096]{1,0:T(8,128)}) %reduce-scatter.20.cloned.1.call-update) | async-done | bytes 1048592 | tf_op jit(solution)/shard_map/reduce_scatter | solution.py:432
  (468 shorter events, 337.5 us)
Async XLA Ops:
  7.2 95.2 %all-gather.19.cloned.1.call-start = ((), (), s32[]{:S(2)}) async-start(), calls=%async_computation.18 | async-start | bytes 1671168 | tf_op jit(solution)/shard_map/all_gather | solution.py:285
  8.9 93.5 %all-gather.23.cloned.1.call-start = ((), (), s32[]{:S(2)}) async-start(), calls=%async_computation.20 | async-start | bytes 2228224 | tf_op jit(solution)/shard_map/all_gather | solution.py:287
  10.7 151.2 %all-gather.21.cloned.1.call-start = ((), (), s32[]{:S(2)}) async-start(), calls=%async_computation.19 | async-start | bytes 6684672 | tf_op jit(solution)/shard_map/all_gather | solution.py:286
  12.7 225.3 %all-gather.25.cloned.1.call-start = ((), (), s32[]{:S(2)}) async-start(), calls=%async_computation.21 | async-start | bytes 8912896 | tf_op jit(solution)/shard_map/all_gather | solution.py:288
  13.7 300.1 %all-gather.27.cloned.1.call-start = ((), (), s32[]{:S(2)}) async-start(), calls=%async_computation.22 | async-start | bytes 8912896 | tf_op jit(solution)/shard_map/all_gather | solution.py:289
  14.6 86.4 %slice-start.12 = ((s32[2,256]{1,0:T(2,128)}), s32[1,256]{1,0:T(1,128)S(1)}, s32[]{:S(2)}) async-start(s32[2,256]{1,0:T(2,128)} %param.33), calls=%async_computation.37 | async-start | bytes 2048 | tf_op jit(solution)/shard_map/slice | solution.py:305
  14.6 87.1 %copy-start.122 = (bf16[1,256,768]{2,1,0:T(8,128)(2,1)S(1)}, bf16[1,256,768]{2,1,0:T(8,128)(2,1)}, u32[]{:S(2)}) copy-start(bf16[1,256,768]{2,1,0:T(8,128)(2,1)} %param.32) | copy-start | bytes 1179652
  14.6 357.1 %all-gather.17.cloned.1.call-start = ((), (), s32[]{:S(2)}) async-start(), calls=%async_computation.10 | async-start | bytes 2162688 | tf_op jit(solution)/shard_map/all_gather | solution.py:295
  15.4 428.3 %all-gather.15.cloned.1.call-start = ((), (), s32[]{:S(2)}) async-start(), calls=%async_computation.9 | async-start | bytes 6488064 | tf_op jit(solution)/shard_map/all_gather | solution.py:294
  16.2 1174.6 %reduce-scatter.30.cloned.1.call-start = ((), (), s32[]{:S(2)}) async-start(), calls=%async_computation.24 | async-start | bytes 557056
  101.0 388.9 %copy-start.191 = (bf16[1024]{0:T(1024)(128)(2,1)}, bf16[1024]{0:T(1024)(128)(2,1)S(1)}, u32[]{:S(2)}) copy-start(bf16[1024]{0:T(1024)(128)(2,1)S(1)} %get-tuple-element.945) | copy-start | bytes 6148
  101.0 388.9 %copy-start.196 = (bf16[1024]{0:T(1024)(128)(2,1)}, bf16[1024]{0:T(1024)(128)(2,1)S(1)}, u32[]{:S(2)}) copy-start(bf16[1024]{0:T(1024)(128)(2,1)S(1)} %get-tuple-element.946) | copy-start | bytes 6148
  101.7 342.0 %copy-start.279 = (s32[128]{0:T(128)}, s32[128]{0:T(128)S(1)}, u32[]{:S(2)}) copy-start(s32[128]{0:T(128)S(1)} %get-tuple-element.1232) | copy-start | bytes 1540
  101.7 388.3 %copy-start.207 = (s32[128]{0:T(128)}, s32[128]{0:T(128)S(1)}, u32[]{:S(2)}) copy-start(s32[128]{0:T(128)S(1)} %get-tuple-element.1233) | copy-start | bytes 1540
  101.7 388.3 %copy-start.281 = (s32[128]{0:T(128)}, s32[128]{0:T(128)S(1)}, u32[]{:S(2)}) copy-start(s32[128]{0:T(128)S(1)} %get-tuple-element.1231) | copy-start | bytes 1540
  102.4 387.6 %copy-start.26 = (bf16[128,768]{1,0:T(8,128)(2,1)}, bf16[128,768]{1,0:T(8,128)(2,1)S(1)}, u32[]{:S(2)}) copy-start(bf16[128,768]{1,0:T(8,128)(2,1)S(1)} %get-tuple-element.1226) | copy-start | bytes 589828
  102.4 448.1 %copy-start.24 = (bf16[128,768]{1,0:T(8,128)(2,1)}, bf16[128,768]{1,0:T(8,128)(2,1)S(1)}, u32[]{:S(2)}) copy-start(bf16[128,768]{1,0:T(8,128)(2,1)S(1)} %get-tuple-element.1224) | copy-start | bytes 589828
  482.4 7.5 collective-permute-start
  530.8 19.6 collective-permute-start.1
  550.5 181.4 %copy-start.27 = (bf16[128,768]{1,0:T(8,128)(2,1)S(1)}, bf16[128,768]{1,0:T(8,128)(2,1)}, u32[]{:S(2)}) copy-start(bf16[128,768]{1,0:T(8,128)(2,1)} %copy-done.26) | copy-start | bytes 589828
  588.8 143.1 %copy-start.8 = (f32[1024,4096]{1,0:T(8,128)}, f32[1024,4096]{1,0:T(8,128)S(1)}, u32[]{:S(2)}) copy-start(f32[1024,4096]{1,0:T(8,128)S(1)} %get-tuple-element.641) | copy-start | bytes 50331652
  588.8 141.1 %collective-permute-start.2 = (bf16[128,1024]{1,0:T(8,128)(2,1)}, bf16[128,1024]{1,0:T(8,128)(2,1)S(1)}, u32[]{:S(2)}, u32[]{:S(2)}) collective-permute-start(bf16[128,1024]{1,0:T(8,128)(2,1)} %get-tuple-element.628), channel_id=1, source_target_pairs={{16,0},{17,1},{18,2},{19,3},{20,4},{21,5},{22,6},{23,7},{24,8},{25... | collective-permute-start | bytes 786440 | tf_op jit(solution)/shard_map/ppermute | solution.py:18
  853.4 51.2 %collective-permute-start.3 = (bf16[128,1024]{1,0:T(8,128)(2,1)}, bf16[128,1024]{1,0:T(8,128)(2,1)S(1)}, u32[]{:S(2)}, u32[]{:S(2)}) collective-permute-start(bf16[128,1024]{1,0:T(8,128)(2,1)} %get-tuple-element.630), channel_id=1, source_target_pairs={{16,0},{17,1},{18,2},{19,3},{20,4},{21,5},{22,6},{23,7},{24,8},{25... | collective-permute-start | bytes 786440 | tf_op jit(solution)/shard_map/ppermute | solution.py:18
  1027.2 165.0 %reduce-scatter.28.cloned.1.call-start = ((), (), s32[]{:S(2)}) async-start(), calls=%async_computation.23 | async-start | bytes 557056
  1029.1 181.1 %reduce-scatter.14.cloned.1.call-start = ((), (), s32[]{:S(2)}) async-start(), calls=%async_computation.11 | async-start | bytes 3342336 | tf_op jit(solution)/shard_map/reduce_scatter | solution.py:429
  1036.0 249.9 %reduce-scatter.18.cloned.1.call-start = ((), (), s32[]{:S(2)}) async-start(), calls=%async_computation.13 | async-start | bytes 4456448 | tf_op jit(solution)/shard_map/reduce_scatter | solution.py:431
  1044.7 384.3 %reduce-scatter.26.cloned.1.call-start = ((), (), s32[]{:S(2)}) async-start(), calls=%async_computation.17 | async-start | bytes 4325376 | tf_op jit(solution)/shard_map/reduce_scatter | solution.py:439
  1053.3 535.1 %reduce-scatter.24.cloned.1.call-start = ((), (), s32[]{:S(2)}) async-start(), calls=%async_computation.16 | async-start | bytes 12976128 | tf_op jit(solution)/shard_map/reduce_scatter | solution.py:438
  1072.5 654.3 %reduce-scatter.16.cloned.1.call-start = ((), (), s32[]{:S(2)}) async-start(), calls=%async_computation.12 | async-start | bytes 13369344 | tf_op jit(solution)/shard_map/reduce_scatter | solution.py:430
  1091.6 817.5 %reduce-scatter.22.cloned.1.call-start = ((), (), s32[]{:S(2)}) async-start(), calls=%async_computation.15 | async-start | bytes 17825792 | tf_op jit(solution)/shard_map/reduce_scatter | solution.py:433
  1115.6 975.5 %reduce-scatter.20.cloned.1.call-start = ((), (), s32[]{:S(2)}) async-start(), calls=%async_computation.14 | async-start | bytes 17825792 | tf_op jit(solution)/shard_map/reduce_scatter | solution.py:432
  1190.7 900.5 %copy-start.123 = (f32[1,256,768]{2,1,0:T(8,128)}, f32[1,256,768]{2,1,0:T(8,128)S(1)}, u32[]{:S(2)}) copy-start(f32[1,256,768]{2,1,0:T(8,128)S(1)} %bitcast_dynamic-update-slice_fusion.1) | copy-start | bytes 2359300
  (90 other events, 868.2 us)
Sparse Core Ops, SparseCore 0:
  10.9 43.9 all-gather.18
  57.6 40.5 all-gather.22
  101.1 60.7 all-gather.20
  164.5 73.4 all-gather.24
  240.6 73.1 all-gather.26
  317.0 54.7 all-gather.16
  375.2 68.3 all-gather.14
  1027.3 54.1 reduce-scatter.29
  1085.5 54.8 reduce-scatter.27
  1144.7 65.4 reduce-scatter.13
  1214.6 71.2 reduce-scatter.17
  1288.7 140.2 reduce-scatter.25
  1436.6 151.7 reduce-scatter.23
  1592.9 133.8 reduce-scatter.15
  1731.3 177.6 reduce-scatter.21
  1913.6 177.5 reduce-scatter.19
where the time goes:
time: 2110 us; the launch traced here: 2100 us
  waiting for transfers between devices  1440 us (68%)
  matrix products  216 us (10%)
  other arithmetic  143 us (7%)
  blocking collectives  123 us (6%)
  local copies, waits for them, and re-layouts  95.1 us (5%)
  loops' own time  50.1 us (2%)
    ppermute x4, waiting for transfers between devices, from_behind(): lax.ppermute(value, axis, [(source, source + steps) for source in range(i...  198 us
    reduce_scatter x1, waiting for transfers between devices, shards(): lax.psum_scatter(totals[4], 'dp', scatter_dimension=0, tiled=True)  182 us
    reduce_scatter x1, waiting for transfers between devices, shards(): lax.psum_scatter(totals[3], 'dp', scatter_dimension=0, tiled=True)  182 us
    reduce_scatter x1, waiting for transfers between devices, shards(): lax.psum_scatter(totals[7], ('section', 'dp'), scatter_dimension=0, tiled...  159 us
    reduce_scatter x1, waiting for transfers between devices, shards(): lax.psum_scatter(totals[8], ('section', 'dp'), scatter_dimension=0, tiled...  143 us
    reduce_scatter x1, waiting for transfers between devices, shards(): lax.psum_scatter(totals[1], 'dp', scatter_dimension=0, tiled=True)  138 us
    add x11, other arithmetic, shards(): totals = tuple((held + fresh for held, fresh in zip(totals, grads)))  112 us
    unnamed x2, blocking collectives  78.3 us
  transfers between devices with their start and end apart: 20, of which 16 were waited for; matrix products, arithmetic and copies ran while one was open for 6% of the time, Pallas kernels for 0%

commit v1 on v0

v1 whole, which is shorter than its diff:
```python
import math

import jax
import jax.numpy as jnp
from jax import lax
from jax.sharding import PartitionSpec as P

HEAD_DIM = 64
SEQ = 128
NEG_FILL = -1000000000.0
BF = jnp.bfloat16
F32 = jnp.float32


def swap_core(x):
    n = lax.axis_size("dp")
    return lax.ppermute(x, "dp", [(i, i ^ 1) for i in range(n)])


def swap_pair(x):
    n = lax.axis_size("dp")
    return lax.ppermute(x, "dp", [(i, i ^ 2) for i in range(n)])


def shift_outer(x):
    n = lax.axis_size("dp")
    return lax.ppermute(x, "dp", [(i, (i + 4) % n) for i in range(n)])


def to_decoder(x):
    return lax.ppermute(x, "section", [(0, 1)])


def to_encoder(x):
    return lax.ppermute(x, "section", [(1, 0)])


def gather(x):
    return lax.all_gather(x, "dp", axis=0, tiled=False)


def relative_blocks(me, n):
    m = n // 4
    blk = jnp.arange(n)
    crel = 1 - blk // (2 * m)
    xrel = 1 - (blk % (2 * m)) // m
    zpos = blk % m
    z = (me // 4 - 1 - zpos) % m
    return z * 4 + ((me // 2) % 2 ^ xrel) * 2 + (me % 2 ^ crel)


def order_matrix(order, block, halves=1):
    n = order.shape[0]
    base = order.reshape(2, 1, n // 2, 1) * block
    src = (
        base
        + jnp.arange(halves).reshape(1, halves, 1, 1) * (n * block)
        + jnp.arange(block).reshape(1, 1, 1, block)
    ).reshape(-1)
    return (jnp.arange(src.shape[0])[:, None] == src[None, :]).astype(BF)


def reordered(a, matrix):
    return jnp.dot(a, matrix, preferred_element_type=F32).astype(BF)


def add_low(a, b):
    return (a.astype(F32) + b.astype(F32)).astype(BF)


def reduce_core(part):
    half = part.shape[0] // 2
    return add_low(part[half:], swap_core(part[:half]))


def reduce_rest(part):
    m = lax.axis_size("dp") // 4
    half = part.shape[0] // 2
    part = add_low(part[half:], swap_pair(part[:half]))
    rows = part.shape[0] // m
    total = part[:rows]
    for k in range(1, m):
        total = shift_outer(total.astype(BF)).astype(F32) + part[k * rows : (k + 1) * rows].astype(
            F32
        )
    return total


def reduce_rel(part):
    return reduce_rest(reduce_core(part))


def mm(a, w):
    return jnp.dot(a, w, preferred_element_type=F32)


def outer_low(a, dy):
    return jnp.einsum("ti,to->io", a, dy, preferred_element_type=F32).astype(BF)


def mm_t(dy, w):
    return jnp.einsum("to,io->ti", dy, w, preferred_element_type=F32)


def norm_forward(values, gain_row, bias_row):
    centre = values - jnp.mean(values, axis=-1, keepdims=True)
    inverse = lax.rsqrt(jnp.mean(centre * centre, axis=-1, keepdims=True) + 1e-05)
    normed = centre * inverse
    return (normed * gain_row + bias_row, normed, inverse)


def norm_backward(upstream, normed, inverse, gain_row):
    scaled = upstream * gain_row
    grad_in = inverse * (
        scaled
        - jnp.mean(scaled, axis=-1, keepdims=True)
        - normed * jnp.mean(scaled * normed, axis=-1, keepdims=True)
    )
    return (grad_in, jnp.sum(upstream * normed, axis=0), jnp.sum(upstream, axis=0))


def heads(values):
    return values.reshape(-1, SEQ, values.shape[1] // HEAD_DIM, HEAD_DIM)


def attend(queries, key_rows, value_rows, allowed):
    factor = HEAD_DIM ** (-0.5)
    scores = jnp.einsum(
        "bqhd,bkhd->bhqk", heads(queries), heads(key_rows), preferred_element_type=F32
    )
    logits = jnp.where(allowed[:, None], scores * factor, NEG_FILL)
    exponent = jnp.exp(logits - jnp.max(logits, axis=-1, keepdims=True))
    probs = exponent / jnp.sum(exponent, axis=-1, keepdims=True)
    blended = jnp.einsum(
        "bhqk,bkhd->bqhd", probs.astype(BF), heads(value_rows), preferred_element_type=F32
    )
    return (blended.reshape(queries.shape).astype(BF), probs)


def attend_back(grad_blended, queries, key_rows, value_rows, probs):
    factor = HEAD_DIM ** (-0.5)
    grad_heads = heads(grad_blended)
    grad_probs = jnp.einsum(
        "bqhd,bkhd->bhqk", grad_heads, heads(value_rows), preferred_element_type=F32
    )
    grad_values = jnp.einsum(
        "bhqk,bqhd->bkhd", probs.astype(BF), grad_heads, preferred_element_type=F32
    )
    centred = jnp.sum(probs * grad_probs, axis=-1, keepdims=True)
    grad_scores = (probs * (grad_probs - centred) * factor).astype(BF)
    grad_queries = jnp.einsum(
        "bhqk,bkhd->bqhd", grad_scores, heads(key_rows), preferred_element_type=F32
    )
    grad_keys = jnp.einsum(
        "bhqk,bqhd->bkhd", grad_scores, heads(queries), preferred_element_type=F32
    )
    shape = queries.shape
    return (
        grad_queries.reshape(shape).astype(BF),
        grad_keys.reshape(shape).astype(BF),
        grad_values.reshape(shape).astype(BF),
    )


def ffn_forward(third, w_up, w_down, gain_row, bias_row):
    third_low = third.astype(BF)
    inner = mm(third_low, w_up)
    erf = lax.erf(inner * (1.0 / math.sqrt(2.0)))
    active = (0.5 * inner * (1.0 + erf)).astype(BF)
    slope = (
        0.5 * (1.0 + erf) + inner * jnp.exp(-0.5 * inner * inner) * (1.0 / math.sqrt(2.0 * math.pi))
    ).astype(BF)
    out, normed, inverse = norm_forward(third + mm(active, w_down), gain_row, bias_row)
    return (out, third_low, active, slope, normed, inverse)


def ffn_backward(cot, normed, inverse, gain_row, slope, w_up, w_down):
    grad, dg, db = norm_backward(cot, normed, inverse, gain_row)
    branch = grad.astype(BF)
    d_inner = (mm_t(branch, w_down) * slope.astype(F32)).astype(BF)
    return (grad + mm_t(d_inner, w_up), branch, d_inner, dg, db)


def shards(
    section_in,
    segment_ids,
    out_cot,
    in_proj,
    attn_in,
    attn_out,
    ffn_in,
    ffn_out,
    norm_gain,
    norm_bias,
    cross_in,
    cross_out,
    cross_gain,
    cross_bias,
):
    n = lax.axis_size("dp")
    me = lax.axis_index("dp")
    core = me % 2
    is_dec = lax.axis_index("section") == 1
    width = attn_out.shape[2]
    inner_width = ffn_in.shape[2]
    d_loc = attn_out.shape[1]
    in_loc = in_proj.shape[1]
    c_loc = cross_in.shape[0]
    in_width = in_loc * n

    params = jnp.concatenate(
        [norm_gain[0].reshape(-1), norm_bias[0].reshape(-1), cross_gain, cross_bias]
    ).astype(BF)
    n_par = params.shape[0]
    tail = jnp.pad(params[None], ((0, d_loc - in_loc - 1), (0, width - n_par)))
    pack1 = jnp.concatenate(
        [
            attn_in[0].astype(BF),
            attn_out[0].astype(BF),
            jnp.concatenate([in_proj[0].astype(BF), tail], axis=0),
        ],
        axis=1,
    )
    q4 = inner_width // width
    pack2 = jnp.concatenate(
        [
            ffn_in[0].astype(BF),
            ffn_out[0].astype(BF).reshape(q4, d_loc, width).transpose(1, 0, 2).reshape(d_loc, -1),
            jnp.concatenate([cross_in, cross_out], axis=1).astype(BF),
        ],
        axis=0,
    )
    all1 = gather(pack1)
    all2 = gather(pack2)

    w_qkv = all1[:, :, : 3 * width].reshape(width, 3 * width)
    w_attn = all1[:, :, 3 * width : 4 * width].reshape(width, width)
    last = all1[:, :, 4 * width :]
    w_in = last[:, :in_loc].reshape(in_width, width)
    pars = last[:, in_loc, :n_par].astype(F32)
    gains = pars[:, : 3 * d_loc].reshape(n, 3, d_loc).transpose(1, 0, 2).reshape(3, width)
    biases = (
        pars[:, 3 * d_loc : 6 * d_loc].reshape(n, 3, d_loc).transpose(1, 0, 2).reshape(3, width)
    )
    w_up = all2[:, :d_loc].reshape(width, inner_width)
    w_down = (
        all2[:, d_loc : 2 * d_loc]
        .reshape(n, d_loc, q4, width)
        .transpose(0, 2, 1, 3)
        .reshape(inner_width, width)
    )
    own_cross = all2[:, 2 * d_loc :].reshape(n * c_loc, 4 * width)
    half = n * c_loc // 2
    mine = to_decoder(lax.dynamic_slice_in_dim(own_cross, core * half, half, 0))
    other = swap_core(mine)
    w_cross = jnp.concatenate(
        [jnp.where(core == 0, mine, other), jnp.where(core == 0, other, mine), own_cross], axis=0
    )
    w_cin, w_cout = w_cross[:, : 3 * width], w_cross[:, 3 * width :]
    own_cpar = pars[:, 6 * d_loc :].astype(BF)
    cpar = jnp.stack([to_decoder(own_cpar), own_cpar]).astype(F32)
    c_gain = cpar[:, :, :c_loc].reshape(width)
    c_bias = cpar[:, :, c_loc:].reshape(width)

    order = relative_blocks(me, n)
    perm_d = order_matrix(order, d_loc)
    perm_in = order_matrix(order, in_loc)
    perm_cross = order_matrix(order, c_loc, 2)

    tokens = section_in[0]
    cot = out_cot[0]
    seqs = tokens.shape[0] // SEQ
    seg = segment_ids.reshape(2, seqs, SEQ)
    own_seg = jnp.where(is_dec, seg[1], seg[0])
    enc_seg = seg[0]
    places = jnp.arange(SEQ)
    causal = (places[None, :] <= places[:, None]) | jnp.logical_not(is_dec)
    self_mask = (own_seg[:, :, None] == own_seg[:, None, :]) & causal[None]
    cross_mask = own_seg[:, :, None] == enc_seg[:, None, :]

    first, xa, ia = norm_forward(mm(tokens, w_in), gains[0], biases[0])
    first_low = first.astype(BF)
    packed = mm(first_low, w_qkv).astype(BF)
    pq, pk, pv = packed[:, :width], packed[:, width : 2 * width], packed[:, 2 * width :]
    blended, probs_self = attend(pq, pk, pv, self_mask)
    second, xb, ib = norm_forward(first + mm(blended, w_attn), gains[1], biases[1])
    second_low = second.astype(BF)

    encoded = ffn_forward(second, w_up, w_down, gains[2], biases[2])[0]
    memory = to_decoder(encoded.astype(BF))

    cross_q = mm(second_low, w_cin[:, :width]).astype(BF)
    cross_kv = mm(memory, w_cin[:, width:]).astype(BF)
    ck, cv = cross_kv[:, :width], cross_kv[:, width:]
    cross_mix, probs_cross = attend(cross_q, ck, cv, cross_mask)
    third_c, xc, ic = norm_forward(second + mm(cross_mix, w_cout), c_gain, c_bias)
    third = jnp.where(is_dec, third_c, second)

    output, third_low, active, slope, xd, idd = ffn_forward(
        third, w_up, w_down, gains[2], biases[2]
    )

    grad_third = ffn_backward(cot, xd, idd, gains[2], slope, w_up, w_down)[0]
    grad_resid, dg_c, db_c = norm_backward(grad_third, xc, ic, c_gain)
    d_cbranch = grad_resid.astype(BF)
    d_cmix = mm_t(d_cbranch, w_cout).astype(BF)
    d_cq, d_ck, d_cv = attend_back(d_cmix, cross_q, ck, cv, probs_cross)
    d_ckv = jnp.concatenate([d_ck, d_cv], axis=1)
    grad_memory = to_encoder(mm_t(d_ckv, w_cin[:, width:]).astype(BF))
    grad_second_dec = grad_resid + mm_t(d_cq, w_cin[:, :width])

    cross_part = jnp.concatenate(
        [
            outer_low(reordered(second_low, perm_cross), d_cq),
            outer_low(reordered(memory, perm_cross), d_ckv),
            outer_low(reordered(cross_mix, perm_cross), d_cbranch),
        ],
        axis=1,
    )
    cross_part = reduce_core(cross_part)
    mid = cross_part.shape[0] // 2
    cross_part = jnp.where(is_dec, cross_part[mid:], to_encoder(cross_part[:mid]))
    cross_total = reduce_rest(cross_part)
    cvec = jnp.stack([dg_c, db_c]).astype(BF).reshape(2, 2, n, c_loc)
    cvec = jnp.where(is_dec, cvec[:, 1], to_encoder(cvec[:, 0])).transpose(1, 0, 2)

    grad_third, branch_d, d_inner, dg_d, db_d = ffn_backward(
        cot + grad_memory.astype(F32), xd, idd, gains[2], slope, w_up, w_down
    )
    blk = inner_width // n
    active_rel = jnp.concatenate(
        [lax.dynamic_slice_in_dim(active, order[k] * blk, blk, 1) for k in range(n)], axis=1
    )
    down_total = reduce_rel(outer_low(active_rel, branch_d))
    up_total = reduce_rel(outer_low(reordered(third_low, perm_d), d_inner))
    grad_second = jnp.where(is_dec, grad_second_dec, grad_third)

    grad_b, dg_b, db_b = norm_backward(grad_second, xb, ib, gains[1])
    branch_b = grad_b.astype(BF)
    attn_total = reduce_rel(outer_low(reordered(blended, perm_d), branch_b))
    d_blended = mm_t(branch_b, w_attn).astype(BF)
    d_q, d_k, d_v = attend_back(d_blended, pq, pk, pv, probs_self)
    d_packed = jnp.concatenate([d_q, d_k, d_v], axis=1)
    qkv_total = reduce_rel(outer_low(reordered(first_low, perm_d), d_packed))
    grad_first = grad_b + mm_t(d_packed, w_qkv)
    grad_embed, dg_a, db_a = norm_backward(grad_first, xa, ia, gains[0])
    d_embed = grad_embed.astype(BF)
    in_grad = mm_t(d_embed, w_in)
    in_part = outer_low(reordered(tokens, perm_in), d_embed).reshape(n, in_loc, width)
    vecs = jnp.stack([dg_a, dg_b, dg_d, db_a, db_b, db_d]).astype(BF)
    vecs = vecs.reshape(6, n, d_loc).transpose(1, 0, 2).reshape(n, 6 * d_loc)
    vecs = jnp.concatenate([vecs, cvec.reshape(n, 2 * c_loc)], axis=1)[order]
    vecs = jnp.pad(vecs[:, None, :], ((0, 0), (0, d_loc - in_loc - 1), (0, width - n_par)))
    in_part = jnp.concatenate([in_part, vecs], axis=1).reshape(n * d_loc, width)
    in_total = reduce_rel(in_part)
    row = in_total[in_loc]
    gain_total = row[: 3 * d_loc].reshape(1, 3, d_loc)
    bias_total = row[3 * d_loc : 6 * d_loc].reshape(1, 3, d_loc)

    return (
        output[None],
        in_grad[None],
        in_total[:in_loc][None],
        qkv_total[None],
        attn_total[None],
        up_total[None],
        down_total[None],
        gain_total,
        bias_total,
        cross_total[:, : 3 * width],
        cross_total[:, 3 * width :],
        row[6 * d_loc : 6 * d_loc + c_loc],
        row[6 * d_loc + c_loc : n_par],
    )


def solution(mesh):
    placed = (
        P("section", "dp", None),
        P(None, "dp"),
        P("section", "dp", None),
        P("section", "dp", None),
        P("section", "dp", None),
        P("section", "dp", None),
        P("section", "dp", None),
        P("section", "dp", None),
        P("section", None, "dp"),
        P("section", None, "dp"),
        P(("section", "dp"), None),
        P(("section", "dp"), None),
        P(("section", "dp")),
        P(("section", "dp")),
    )
    return jax.shard_map(
        shards,
        mesh=mesh,
        in_specs=placed,
        out_specs=(
            P("section", "dp", None),
            P("section", "dp", None),
            P("section", "dp", None),
            P("section", "dp", None),
            P("section", "dp", None),
            P("section", "dp", None),
            P("section", "dp", None),
            P("section", None, "dp"),
            P("section", None, "dp"),
            P(("section", "dp"), None),
            P(("section", "dp"), None),
            P(("section", "dp")),
            P(("section", "dp")),
        ),
        check_vma=False,
    )
```

time: 2110 us -> 808 us (0.38)
  waiting for transfers between devices: 1440 us -> 334 us
  blocking collectives: 123 us -> 0 us
  local copies, waits for them, and re-layouts: 95.1 us -> 168 us
  other arithmetic: 143 us -> 73.5 us
  matrix products: 216 us -> 151 us
  loops' own time: 50.1 us -> 0 us
  starting transfers between devices: 18.7 us -> 43.9 us
    reduce_scatter x7 -> x0, waiting for transfers between devices: 898 us -> none  [the longest x1 182 us: shards(): lax.psum_scatter(totals[4], 'dp', scatter_dimension=0, tiled=True)]
    all_gather x7 -> x2, waiting for transfers between devices: 341 us -> 141 us  [gather(): return lax.all_gather(x, 'dp', axis=0, tiled=False)]
    add x15 -> x7, other arithmetic: 117 us -> 0.39 us  [the longest x4 0.3 us: order_matrix(): base + jnp.arange(halves).reshape(1, halves, 1, 1) * (n * block)]
    unnamed x2 -> x0, blocking collectives: 78.3 us -> none
    dot_general x52 -> x36, matrix products: 209 us -> 143 us  [the longest x9 41.2 us: mm_t(): return jnp.einsum('to,io->ti', dy, w, preferred_element_type=F32)]
    another operation x6 -> x0, loops' own time: 50.1 us -> none  [the longest x3 37 us: shards(): lax.switch(branch, (back_spare, back_encoder, back_decoder), tokens_in, o...]
    another operation x23 -> x10, local copies, waits for them, and re-layouts: 52.9 us -> 4.46 us  [the longest x3 3.99 us: shards(): cvec = jnp.stack([dg_c, db_c]).astype(BF).reshape(2, 2, n, c_loc)]
    reshape x0 -> x24, local copies, waits for them, and re-layouts: none -> 46.6 us  [the longest x16 29.2 us: heads(): return values.reshape(-1, SEQ, values.shape[1] // HEAD_DIM, HEAD_DIM)]
  transfers between devices with their start and end apart: 20 -> 39, of which waited for: 16 -> 21; matrix products, arithmetic and copies ran while one was open for 6% -> 35% of each run, Pallas kernels for 0% -> 0%
where the time goes in v1:
time: 808 us; the launch traced here: 796 us
  waiting for transfers between devices  334 us (41%)
  local copies, waits for them, and re-layouts  168 us (21%)
  matrix products  151 us (19%)
  other arithmetic  73.5 us (9%)
  starting transfers between devices  43.9 us (5%)
  between operations  26.8 us (3%)
    all_gather x2, waiting for transfers between devices, gather(): return lax.all_gather(x, 'dp', axis=0, tiled=False)  141 us
    ppermute x6, waiting for transfers between devices, swap_pair(): return lax.ppermute(x, 'dp', [(i, i ^ 2) for i in range(n)])  106 us
    ppermute x18, waiting for transfers between devices, shift_outer(): return lax.ppermute(x, 'dp', [(i, (i + 4) % n) for i in range(n)])  84 us
    dot_general x9, matrix products, mm_t(): return jnp.einsum('to,io->ti', dy, w, preferred_element_type=F32)  41.2 us
    dot_general x8, matrix products, outer_low(): return jnp.einsum('ti,to->io', a, dy, preferred_element_type=F32).astype(BF)  37.7 us
    dot_general x9, matrix products, mm(): return jnp.dot(a, w, preferred_element_type=F32)  30.8 us
    reshape x16, local copies, waits for them, and re-layouts, heads(): return values.reshape(-1, SEQ, values.shape[1] // HEAD_DIM, HEAD_DIM)  29.2 us
    unnamed x244, local copies, waits for them, and re-layouts  27.8 us
  transfers between devices with their start and end apart: 39, of which 21 were waited for; matrix products, arithmetic and copies ran while one was open for 35% of the time, Pallas kernels for 0%

profile of v1, /device:TPU:0, one launch (start us, length us, event | category | flops | bytes accessed | tf_op | source)
XLA Modules:
  0.0 796.4 jit_solution(7822580357137207479)
XLA Ops:
  32.3 72.2 %all-gather.5.cloned.1.call-done = bf16[1024,5120]{1,0:T(8,128)(2,1)} async-done(((bf16[64,5120]{1,0:T(8,128)(2,1)}), bf16[1024,5120]{1,0:T(8,128)(2,1)}) %all-gather.5.cloned.1.call-update) | async-done | bytes 10485776 | tf_op jit(solution)/shard_map/all_gather | solution.py:39
  107.7 6.0 slice.464
  144.5 68.6 %all-gather.7.cloned.1.call-done = bf16[2560,4096]{1,0:T(8,128)(2,1)} async-done(((bf16[160,4096]{1,0:T(8,128)(2,1)}), bf16[2560,4096]{1,0:T(8,128)(2,1)}) %all-gather.7.cloned.1.call-update) | async-done | bytes 20971536 | tf_op jit(solution)/shard_map/all_gather | solution.py:39
  230.3 11.7 %fusion.230 = (bf16[16,64,4096]{2,1,0:T(8,128)(2,1)}, bf16[16,64,4096]{2,1,0:T(8,128)(2,1)}) fusion(bf16[16,160,4096]{2,1,0:T(8,128)(2,1)} %bitcast.301), kind=kLoop, calls=%fused_computation.421 | loop fusion | bytes 33554432 | tf_op jit(solution)/shard_map/slice | solution.py:245
  242.0 14.5 %reshape.827 = bf16[16,64,4,1024]{3,2,1,0:T(4,128)(2,1)} reshape(bf16[16,64,4096]{2,1,0:T(8,128)(2,1)} %get-tuple-element.79) | data formatting | bytes 16777216 | tf_op jit(solution)/shard_map/reshape | solution.py:248
  256.5 10.1 %copy.134 = bf16[16,4,64,1024]{3,2,1,0:T(8,128)(2,1)} copy(bf16[16,4,64,1024]{3,1,2,0:T(4,128)(2,1)} %bitcast.299) | data formatting | bytes 16777216 | tf_op jit(solution)/shard_map/transpose | solution.py:249
  266.7 11.2 %fusion.242 = (f32[256]{0:T(256)S(1)}, f32[256,1024]{0,1:T(8,128)S(1)}) fusion(bf16[4096,1024]{1,0:T(8,128)(2,1)} %bitcast.310, bf16[1024,4096]{1,0:T(8,128)(2,1)} %bitcast.284, f32[256,1024]{0,1:T(8,128)S(1)} %get-tuple-element.126, f32[1024]{0:T(1024)S(1)} %add.620, f32[1024]{0:T(1024)S(1)} %mul.499, f32[256]{0:T(256)} %add_rsqrt_fusion.3, ...), kind=kOutput, calls=%fused_computation.433 | convolution fusion | flops 4303093760 | bytes 18885632 | tf_op jit(solution)/shard_map/dot_general | solution.py:94
  336.1 15.5 %multiply_reduce_fusion.2 = (bf16[1024]{0:T(1024)(128)(2,1)}, f32[256]{0:T(256)}, f32[256]{0:T(256)}, bf16[1024]{0:T(1024)(128)(2,1)}, f32[256,1024]{0,1:T(8,128)}) fusion(f32[256,1024]{0,1:T(8,128)} %copy-done.20, f32[256]{0:T(256)} %copy-done.78, f32[256]{0:T(256)} %copy-done.73, f32[1024]{0:T(1024)} %mul.516, bf16[1024,4096]{1,0:T(8,128)(2,1)} %bitcast.285, ...), kind=kOutput, calls=%fused_computation.148 | convolution fusion | flops 4314101760 | bytes 25186304 | tf_op jit(solution)/shard_map/to,io->ti/dot_general | solution.py:102
  367.8 5.3 fusion.85
  373.1 5.4 fusion.88
  410.2 5.6 convolution_convert_fusion.4
  436.1 6.8 fusion.5
  452.9 5.1 fusion.94
  466.7 6.3 fusion.106
  490.7 7.0 convolution_convert_fusion.2
  501.9 7.5 convolution_convert_fusion.1
  531.2 10.4 %collective-permute-done.17 = bf16[256,1024]{1,0:T(8,128)(2,1)S(1)} collective-permute-done((bf16[256,1024]{1,0:T(8,128)(2,1)S(1)}, bf16[256,1024]{1,0:T(8,128)(2,1)S(1)}, u32[]{:S(2)}, u32[]{:S(2)}) %collective-permute-start.17) | collective-permute-done | bytes 524320 | tf_op jit(solution)/shard_map/ppermute | solution.py:22
  543.3 5.1 collective-permute-done.8
  548.4 6.7 collective-permute-done.18
  555.2 6.7 collective-permute-done.9
  562.0 7.5 collective-permute-done.19
  569.5 7.6 collective-permute-done.10
  587.7 5.5 add_convert_fusion
  596.1 17.1 %collective-permute-done.12 = bf16[256,3072]{1,0:T(8,128)(2,1)} collective-permute-done((bf16[256,3072]{1,0:T(8,128)(2,1)}, bf16[256,3072]{1,0:T(8,128)(2,1)}, u32[]{:S(2)}, u32[]{:S(2)}) %collective-permute-start.12) | collective-permute-done | bytes 1572896 | tf_op jit(solution)/shard_map/ppermute | solution.py:22
  616.7 5.9 add_convert_fusion.2
  635.5 7.1 collective-permute-done.14
  646.9 28.0 %collective-permute-done.22 = bf16[256,4096]{1,0:T(8,128)(2,1)} collective-permute-done((bf16[256,4096]{1,0:T(8,128)(2,1)}, bf16[256,4096]{1,0:T(8,128)(2,1)}, u32[]{:S(2)}, u32[]{:S(2)}) %collective-permute-start.22) | collective-permute-done | bytes 2097184 | tf_op jit(solution)/shard_map/ppermute | solution.py:22
  678.7 40.9 %collective-permute-done.27 = bf16[1024,1024]{1,0:T(8,128)(2,1)S(1)} collective-permute-done((bf16[1024,1024]{1,0:T(8,128)(2,1)S(1)}, bf16[1024,1024]{1,0:T(8,128)(2,1)S(1)}, u32[]{:S(2)}, u32[]{:S(2)}) %collective-permute-start.27) | collective-permute-done | bytes 2097184 | tf_op jit(solution)/shard_map/ppermute | solution.py:22
  725.4 7.6 collective-permute-done.33
  737.5 14.3 %collective-permute-done.34 = bf16[32,4096]{1,0:T(8,128)(2,1)S(1)} collective-permute-done((bf16[32,4096]{1,0:T(8,128)(2,1)S(1)}, bf16[32,4096]{1,0:T(8,128)(2,1)S(1)}, u32[]{:S(2)}, u32[]{:S(2)}) %collective-permute-start.34) | collective-permute-done | bytes 262176 | tf_op jit(solution)/shard_map/ppermute | solution.py:27
  755.6 13.0 %collective-permute-done.35 = bf16[32,4096]{1,0:T(8,128)(2,1)S(1)} collective-permute-done((bf16[32,4096]{1,0:T(8,128)(2,1)S(1)}, bf16[32,4096]{1,0:T(8,128)(2,1)S(1)}, u32[]{:S(2)}, u32[]{:S(2)}) %collective-permute-start.35) | collective-permute-done | bytes 262176 | tf_op jit(solution)/shard_map/ppermute | solution.py:27
  772.5 9.8 %collective-permute-done.36 = bf16[32,4096]{1,0:T(8,128)(2,1)S(1)} collective-permute-done((bf16[32,4096]{1,0:T(8,128)(2,1)S(1)}, bf16[32,4096]{1,0:T(8,128)(2,1)S(1)}, u32[]{:S(2)}, u32[]{:S(2)}) %collective-permute-start.36) | collective-permute-done | bytes 262176 | tf_op jit(solution)/shard_map/ppermute | solution.py:27
  (538 shorter events, 317.4 us)
Async XLA Ops:
  7.2 97.3 %all-gather.5.cloned.1.call-start = ((), (), s32[]{:S(2)}) async-start(), calls=%async_computation | async-start | bytes 11141120 | tf_op jit(solution)/shard_map/all_gather | solution.py:39
  13.8 199.4 %all-gather.7.cloned.1.call-start = ((), (), s32[]{:S(2)}) async-start(), calls=%async_computation.1 | async-start | bytes 22282240 | tf_op jit(solution)/shard_map/all_gather | solution.py:39
  139.0 87.1 %collective-permute-start.3 = (bf16[16,64]{1,0:T(8,128)(2,1)}, bf16[16,64]{1,0:T(8,128)(2,1)}, u32[]{:S(2)}, u32[]{:S(2)}) collective-permute-start(bf16[16,64]{1,0:T(8,128)(2,1)} %get-tuple-element.97), channel_id=1, source_target_pairs={{0,16},{1,17},{2,18},{3,19},{4,20},{5,21},{6,22},{7,23},{8,24},{9,... | collective-permute-start | bytes 6152 | tf_op jit(solution)/shard_map/ppermute | solution.py:31
  217.7 49.0 %collective-permute-start.1 = (bf16[256,4096]{1,0:T(8,128)(2,1)S(1)}, bf16[256,4096]{1,0:T(8,128)(2,1)}, u32[]{:S(2)}, u32[]{:S(2)}) collective-permute-start(bf16[256,4096]{1,0:T(8,128)(2,1)S(1)} %constant_dynamic-slice_fusion), channel_id=1, source_target_pairs={{0,16},{1,17},{2,18},{3,19},{4,20},{5,21},{6,22},{7,23},{8,24},{9,... | collective-permute-start | bytes 6291464 | tf_op jit(solution)/shard_map/ppermute | solution.py:31
  266.7 15.9 %collective-permute-start.2 = (bf16[256,4096]{1,0:T(8,128)(2,1)}, bf16[256,4096]{1,0:T(8,128)(2,1)}, u32[]{:S(2)}, u32[]{:S(2)}) collective-permute-start(bf16[256,4096]{1,0:T(8,128)(2,1)} %collective-permute-done.1), channel_id=1, source_target_pairs={{0,1},{1,0},{2,3},{3,2},{4,5},{5,4},{6,7},{7,6},{8,9},{9,8},{10,11... | collective-permute-start | bytes 6291464 | tf_op jit(solution)/shard_map/ppermute | solution.py:17
  278.4 16.0 %collective-permute-start = (bf16[256,1024]{0,1:T(8,128)(2,1)S(1)}, bf16[256,1024]{0,1:T(8,128)(2,1)S(1)}, u32[]{:S(2)}, u32[]{:S(2)}) collective-permute-start(bf16[256,1024]{0,1:T(8,128)(2,1)S(1)} %add_convert_fusion.15), channel_id=1, source_target_pairs={{0,16},{1,17},{2,18},{3,19},{4,20},{5,21},{6,22},{7,23},{8,24},{9,... | collective-permute-start | bytes 1572872 | tf_op jit(solution)/shard_map/ppermute | solution.py:31
  385.6 44.8 %collective-permute-start.4 = (bf16[256,1024]{0,1:T(8,128)(2,1)}, bf16[256,1024]{0,1:T(8,128)(2,1)}, u32[]{:S(2)}, u32[]{:S(2)}) collective-permute-start(bf16[256,1024]{0,1:T(8,128)(2,1)} %fusion.78), channel_id=1, source_target_pairs={{16,0},{17,1},{18,2},{19,3},{20,4},{21,5},{22,6},{23,7},{24,8},{25... | collective-permute-start | bytes 1572872 | tf_op jit(solution)/shard_map/ppermute | solution.py:35
  394.8 32.9 %collective-permute-start.5 = (bf16[2,16,32]{2,1,0:T(8,128)(2,1)}, bf16[2,16,32]{2,1,0:T(8,128)(2,1)}, u32[]{:S(2)}, u32[]{:S(2)}) collective-permute-start(bf16[2,16,32]{2,1,0:T(8,128)(2,1)} %slice_bitcast_fusion.1), channel_id=1, source_target_pairs={{16,0},{17,1},{18,2},{19,3},{20,4},{21,5},{22,6},{23,7},{24,8},{25... | collective-permute-start | bytes 6152 | tf_op jit(solution)/shard_map/ppermute | solution.py:35
  425.6 162.1 %collective-permute-start.31 = (bf16[512,4096]{1,0:T(8,128)(2,1)}, bf16[512,4096]{1,0:T(8,128)(2,1)}, u32[]{:S(2)}, u32[]{:S(2)}) collective-permute-start(bf16[512,4096]{1,0:T(8,128)(2,1)} %slice.528), channel_id=1, source_target_pairs={{0,1},{1,0},{2,3},{3,2},{4,5},{5,4},{6,7},{7,6},{8,9},{9,8},{10,11... | collective-permute-start | bytes 12582920 | tf_op jit(solution)/shard_map/ppermute | solution.py:17
  481.3 33.0 %collective-permute-start.6 = (bf16[512,1024]{1,0:T(8,128)(2,1)}, bf16[512,1024]{1,0:T(8,128)(2,1)}, u32[]{:S(2)}, u32[]{:S(2)}) collective-permute-start(bf16[512,1024]{1,0:T(8,128)(2,1)} %bitcast.44), channel_id=1, source_target_pairs={{0,1},{1,0},{2,3},{3,2},{4,5},{5,4},{6,7},{7,6},{8,9},{9,8},{10,11... | collective-permute-start | bytes 3145736 | tf_op jit(solution)/shard_map/ppermute | solution.py:17
  490.5 27.0 %collective-permute-start.16 = (bf16[512,1024]{1,0:T(8,128)(2,1)}, bf16[512,1024]{1,0:T(8,128)(2,1)S(1)}, u32[]{:S(2)}, u32[]{:S(2)}) collective-permute-start(bf16[512,1024]{1,0:T(8,128)(2,1)} %slice.502), channel_id=1, source_target_pairs={{0,1},{1,0},{2,3},{3,2},{4,5},{5,4},{6,7},{7,6},{8,9},{9,8},{10,11... | collective-permute-start | bytes 3145736 | tf_op jit(solution)/shard_map/ppermute | solution.py:17
  501.6 76.2 %collective-permute-start.11 = (bf16[512,3072]{1,0:T(8,128)(2,1)}, bf16[512,3072]{1,0:T(8,128)(2,1)}, u32[]{:S(2)}, u32[]{:S(2)}) collective-permute-start(bf16[512,3072]{1,0:T(8,128)(2,1)} %slice.494), channel_id=1, source_target_pairs={{0,1},{1,0},{2,3},{3,2},{4,5},{5,4},{6,7},{7,6},{8,9},{9,8},{10,11... | collective-permute-start | bytes 9437192 | tf_op jit(solution)/shard_map/ppermute | solution.py:17
  514.1 102.5 %collective-permute-start.21 = (bf16[512,4096]{1,0:T(8,128)(2,1)}, bf16[512,4096]{1,0:T(8,128)(2,1)}, u32[]{:S(2)}, u32[]{:S(2)}) collective-permute-start(bf16[512,4096]{1,0:T(8,128)(2,1)} %slice.510), channel_id=1, source_target_pairs={{0,1},{1,0},{2,3},{3,2},{4,5},{5,4},{6,7},{7,6},{8,9},{9,8},{10,11... | collective-permute-start | bytes 12582920 | tf_op jit(solution)/shard_map/ppermute | solution.py:17
  516.2 14.8 %collective-permute-start.7 = (bf16[256,1024]{1,0:T(8,128)(2,1)S(1)}, bf16[256,1024]{1,0:T(8,128)(2,1)S(1)}, u32[]{:S(2)}, u32[]{:S(2)}) collective-permute-start(bf16[256,1024]{1,0:T(8,128)(2,1)S(1)} %slice.487), channel_id=1, source_target_pairs={{0,2},{1,3},{2,0},{3,1},{4,6},{5,7},{6,4},{7,5},{8,10},{9,11},{10,... | collective-permute-start | bytes 1572872 | tf_op jit(solution)/shard_map/ppermute | solution.py:22
  518.0 23.7 %collective-permute-start.17 = (bf16[256,1024]{1,0:T(8,128)(2,1)S(1)}, bf16[256,1024]{1,0:T(8,128)(2,1)S(1)}, u32[]{:S(2)}, u32[]{:S(2)}) collective-permute-start(bf16[256,1024]{1,0:T(8,128)(2,1)S(1)} %slice.504), channel_id=1, source_target_pairs={{0,2},{1,3},{2,0},{3,1},{4,6},{5,7},{6,4},{7,5},{8,10},{9,11},{10,... | collective-permute-start | bytes 1572872 | tf_op jit(solution)/shard_map/ppermute | solution.py:22
  531.0 98.1 %collective-permute-start.26 = (bf16[2048,1024]{1,0:T(8,128)(2,1)}, bf16[2048,1024]{1,0:T(8,128)(2,1)}, u32[]{:S(2)}, u32[]{:S(2)}) collective-permute-start(bf16[2048,1024]{1,0:T(8,128)(2,1)} %slice.518), channel_id=1, source_target_pairs={{0,1},{1,0},{2,3},{3,2},{4,5},{5,4},{6,7},{7,6},{8,9},{9,8},{10,11... | collective-permute-start | bytes 12582920 | tf_op jit(solution)/shard_map/ppermute | solution.py:17
  583.8 29.4 %collective-permute-start.12 = (bf16[256,3072]{1,0:T(8,128)(2,1)}, bf16[256,3072]{1,0:T(8,128)(2,1)}, u32[]{:S(2)}, u32[]{:S(2)}) collective-permute-start(bf16[256,3072]{1,0:T(8,128)(2,1)} %slice.496), channel_id=1, source_target_pairs={{0,2},{1,3},{2,0},{3,1},{4,6},{5,7},{6,4},{7,5},{8,10},{9,11},{10,... | collective-permute-start | bytes 4718600 | tf_op jit(solution)/shard_map/ppermute | solution.py:22
  594.7 48.1 %collective-permute-start.32 = (bf16[256,4096]{1,0:T(8,128)(2,1)}, bf16[256,4096]{1,0:T(8,128)(2,1)}, u32[]{:S(2)}, u32[]{:S(2)}) collective-permute-start(bf16[256,4096]{1,0:T(8,128)(2,1)} %slice.530), channel_id=1, source_target_pairs={{16,0},{17,1},{18,2},{19,3},{20,4},{21,5},{22,6},{23,7},{24,8},{25... | collective-permute-start | bytes 6291464 | tf_op jit(solution)/shard_map/ppermute | solution.py:35
  626.0 48.9 %collective-permute-start.22 = (bf16[256,4096]{1,0:T(8,128)(2,1)}, bf16[256,4096]{1,0:T(8,128)(2,1)}, u32[]{:S(2)}, u32[]{:S(2)}) collective-permute-start(bf16[256,4096]{1,0:T(8,128)(2,1)} %slice.512), channel_id=1, source_target_pairs={{0,2},{1,3},{2,0},{3,1},{4,6},{5,7},{6,4},{7,5},{8,10},{9,11},{10,... | collective-permute-start | bytes 6291464 | tf_op jit(solution)/shard_map/ppermute | solution.py:22
  629.1 13.5 %collective-permute-start.14 = (bf16[64,3072]{1,0:T(8,128)(2,1)S(1)}, bf16[64,3072]{1,0:T(8,128)(2,1)S(1)}, u32[]{:S(2)}, u32[]{:S(2)}) collective-permute-start(bf16[64,3072]{1,0:T(8,128)(2,1)S(1)} %add_convert_fusion.17), channel_id=1, source_target_pairs={{0,4},{1,5},{2,6},{3,7},{4,8},{5,9},{6,10},{7,11},{8,12},{9,13},{1... | collective-permute-start | bytes 1179656 | tf_op jit(solution)/shard_map/ppermute | solution.py:27
  633.7 86.0 %collective-permute-start.27 = (bf16[1024,1024]{1,0:T(8,128)(2,1)S(1)}, bf16[1024,1024]{1,0:T(8,128)(2,1)S(1)}, u32[]{:S(2)}, u32[]{:S(2)}) collective-permute-start(bf16[1024,1024]{1,0:T(8,128)(2,1)S(1)} %slice.520), channel_id=1, source_target_pairs={{0,2},{1,3},{2,0},{3,1},{4,6},{5,7},{6,4},{7,5},{8,10},{9,11},{10,... | collective-permute-start | bytes 6291464 | tf_op jit(solution)/shard_map/ppermute | solution.py:22
  642.7 35.1 %collective-permute-start.15 = (bf16[64,3072]{1,0:T(8,128)(2,1)S(1)}, bf16[64,3072]{1,0:T(8,128)(2,1)S(1)}, u32[]{:S(2)}, u32[]{:S(2)}) collective-permute-start(bf16[64,3072]{1,0:T(8,128)(2,1)S(1)} %add_convert_fusion.16), channel_id=1, source_target_pairs={{0,4},{1,5},{2,6},{3,7},{4,8},{5,9},{6,10},{7,11},{8,12},{9,13},{1... | collective-permute-start | bytes 1179656 | tf_op jit(solution)/shard_map/ppermute | solution.py:27
  644.9 88.1 %collective-permute-start.33 = (bf16[128,4096]{1,0:T(8,128)(2,1)S(1)}, bf16[128,4096]{1,0:T(8,128)(2,1)S(1)}, u32[]{:S(2)}, u32[]{:S(2)}) collective-permute-start(bf16[128,4096]{1,0:T(8,128)(2,1)S(1)} %slice.532), channel_id=1, source_target_pairs={{0,2},{1,3},{2,0},{3,1},{4,6},{5,7},{6,4},{7,5},{8,10},{9,11},{10,... | collective-permute-start | bytes 3145736 | tf_op jit(solution)/shard_map/ppermute | solution.py:22
  677.3 43.9 %collective-permute-start.23 = (bf16[64,4096]{1,0:T(8,128)(2,1)S(1)}, bf16[64,4096]{1,0:T(8,128)(2,1)S(1)}, u32[]{:S(2)}, u32[]{:S(2)}) collective-permute-start(bf16[64,4096]{1,0:T(8,128)(2,1)S(1)} %slice.513), channel_id=1, source_target_pairs={{0,4},{1,5},{2,6},{3,7},{4,8},{5,9},{6,10},{7,11},{8,12},{9,13},{1... | collective-permute-start | bytes 1572872 | tf_op jit(solution)/shard_map/ppermute | solution.py:27
  720.7 14.2 %collective-permute-start.28 = (bf16[256,1024]{1,0:T(8,128)(2,1)S(1)}, bf16[256,1024]{1,0:T(8,128)(2,1)S(1)}, u32[]{:S(2)}, u32[]{:S(2)}) collective-permute-start(bf16[256,1024]{1,0:T(8,128)(2,1)S(1)} %slice.521), channel_id=1, source_target_pairs={{0,4},{1,5},{2,6},{3,7},{4,8},{5,9},{6,10},{7,11},{8,12},{9,13},{1... | collective-permute-start | bytes 1572872 | tf_op jit(solution)/shard_map/ppermute | solution.py:27
  721.3 31.6 %collective-permute-start.24 = (bf16[64,4096]{1,0:T(8,128)(2,1)S(1)}, bf16[64,4096]{1,0:T(8,128)(2,1)S(1)}, u32[]{:S(2)}, u32[]{:S(2)}) collective-permute-start(bf16[64,4096]{1,0:T(8,128)(2,1)S(1)} %add_convert_fusion.12), channel_id=1, source_target_pairs={{0,4},{1,5},{2,6},{3,7},{4,8},{5,9},{6,10},{7,11},{8,12},{9,13},{1... | collective-permute-start | bytes 1572872 | tf_op jit(solution)/shard_map/ppermute | solution.py:27
  733.3 18.4 %collective-permute-start.34 = (bf16[32,4096]{1,0:T(8,128)(2,1)S(1)}, bf16[32,4096]{1,0:T(8,128)(2,1)S(1)}, u32[]{:S(2)}, u32[]{:S(2)}) collective-permute-start(bf16[32,4096]{1,0:T(8,128)(2,1)S(1)} %slice.533), channel_id=1, source_target_pairs={{0,4},{1,5},{2,6},{3,7},{4,8},{5,9},{6,10},{7,11},{8,12},{9,13},{1... | collective-permute-start | bytes 786440 | tf_op jit(solution)/shard_map/ppermute | solution.py:27
  735.1 34.7 %collective-permute-start.29 = (bf16[256,1024]{1,0:T(8,128)(2,1)S(1)}, bf16[256,1024]{1,0:T(8,128)(2,1)S(1)}, u32[]{:S(2)}, u32[]{:S(2)}) collective-permute-start(bf16[256,1024]{1,0:T(8,128)(2,1)S(1)} %add_convert_fusion.10), channel_id=1, source_target_pairs={{0,4},{1,5},{2,6},{3,7},{4,8},{5,9},{6,10},{7,11},{8,12},{9,13},{1... | collective-permute-start | bytes 1572872 | tf_op jit(solution)/shard_map/ppermute | solution.py:27
  751.8 16.8 %collective-permute-start.35 = (bf16[32,4096]{1,0:T(8,128)(2,1)S(1)}, bf16[32,4096]{1,0:T(8,128)(2,1)S(1)}, u32[]{:S(2)}, u32[]{:S(2)}) collective-permute-start(bf16[32,4096]{1,0:T(8,128)(2,1)S(1)} %add_convert_fusion.19), channel_id=1, source_target_pairs={{0,4},{1,5},{2,6},{3,7},{4,8},{5,9},{6,10},{7,11},{8,12},{9,13},{1... | collective-permute-start | bytes 786440 | tf_op jit(solution)/shard_map/ppermute | solution.py:27
  753.1 30.8 %collective-permute-start.25 = (bf16[64,4096]{1,0:T(8,128)(2,1)S(1)}, bf16[64,4096]{1,0:T(8,128)(2,1)S(1)}, u32[]{:S(2)}, u32[]{:S(2)}) collective-permute-start(bf16[64,4096]{1,0:T(8,128)(2,1)S(1)} %add_convert_fusion.11), channel_id=1, source_target_pairs={{0,4},{1,5},{2,6},{3,7},{4,8},{5,9},{6,10},{7,11},{8,12},{9,13},{1... | collective-permute-start | bytes 1572872 | tf_op jit(solution)/shard_map/ppermute | solution.py:27
  768.7 13.7 %collective-permute-start.36 = (bf16[32,4096]{1,0:T(8,128)(2,1)S(1)}, bf16[32,4096]{1,0:T(8,128)(2,1)S(1)}, u32[]{:S(2)}, u32[]{:S(2)}) collective-permute-start(bf16[32,4096]{1,0:T(8,128)(2,1)S(1)} %add_convert_fusion.18), channel_id=1, source_target_pairs={{0,4},{1,5},{2,6},{3,7},{4,8},{5,9},{6,10},{7,11},{8,12},{9,13},{1... | collective-permute-start | bytes 786440 | tf_op jit(solution)/shard_map/ppermute | solution.py:27
  770.0 18.0 %collective-permute-start.30 = (bf16[256,1024]{1,0:T(8,128)(2,1)S(1)}, bf16[256,1024]{1,0:T(8,128)(2,1)S(1)}, u32[]{:S(2)}, u32[]{:S(2)}) collective-permute-start(bf16[256,1024]{1,0:T(8,128)(2,1)S(1)} %add_convert_fusion.9), channel_id=1, source_target_pairs={{0,4},{1,5},{2,6},{3,7},{4,8},{5,9},{6,10},{7,11},{8,12},{9,13},{1... | collective-permute-start | bytes 1572872 | tf_op jit(solution)/shard_map/ppermute | solution.py:27
  (115 other events, 840.2 us)
Sparse Core Ops, SparseCore 0:
  13.9 90.5 all-gather.4
  106.1 107.0 all-gather.6

commit v2 on v1

v2 whole, which is shorter than its diff:
```python
import math

import jax
import jax.numpy as jnp
from jax import lax
from jax.experimental import pallas as pl
from jax.experimental.pallas import tpu as pltpu
from jax.sharding import PartitionSpec as P

HEAD_DIM = 64
SEQ = 128
NEG_FILL = -1000000000.0
BF = jnp.bfloat16
F32 = jnp.float32


def swap_core(x):
    n = lax.axis_size("dp")
    return lax.ppermute(x, "dp", [(i, i ^ 1) for i in range(n)])


def swap_pair(x):
    n = lax.axis_size("dp")
    return lax.ppermute(x, "dp", [(i, i ^ 2) for i in range(n)])


def spread_outer(x):
    n = lax.axis_size("dp")
    groups = [list(range(at, n, 4)) for at in range(4)]
    x = x.reshape(n // 4, -1, x.shape[1])
    return lax.all_to_all(x, "dp", 0, 0, axis_index_groups=groups)


def to_decoder(x):
    return lax.ppermute(x, "section", [(0, 1)])


def to_encoder(x):
    return lax.ppermute(x, "section", [(1, 0)])


def after(x, *deps):
    return lax.optimization_barrier((x,) + deps)[0]


def relative_blocks(me, n):
    m = n // 4
    blk = jnp.arange(n)
    crel = 1 - blk // (2 * m)
    xrel = 1 - (blk % (2 * m)) // m
    return (blk % m) * 4 + ((me // 2) % 2 ^ xrel) * 2 + (me % 2 ^ crel)


def order_matrix(order, block, halves=1):
    n = order.shape[0]
    base = order.reshape(2, 1, n // 2, 1) * block
    src = (
        base
        + jnp.arange(halves).reshape(1, halves, 1, 1) * (n * block)
        + jnp.arange(block).reshape(1, 1, 1, block)
    ).reshape(-1)
    return (jnp.arange(src.shape[0])[:, None] == src[None, :]).astype(BF)


def reordered(a, matrix):
    return jnp.einsum("tk,kr->rt", a, matrix, preferred_element_type=F32).astype(BF)


class Chain:
    def __init__(self):
        self.last = ()

    def __call__(self, x):
        return after(x, *self.last) if self.last else x

    def mark(self, *outs):
        self.last = outs
        return outs[0]


def add_low(a, b):
    return (a.astype(F32) + b.astype(F32)).astype(BF)


def summed(blocks):
    return jnp.sum(blocks.astype(F32), axis=0)


class Part:
    def __init__(self, chain, a, dy, got=None, picks=(), columns=None):
        self.chain, self.a, self.dy, self.picks, self.columns = chain, a, dy, picks, columns
        self.k = a.shape[-2]
        self.got = got or [swap_core(piece) for piece in self.outer(0, self.k // 2, pieces=True)]

    def outer(self, first, count, *adds, pieces=False):
        dy = self.chain(self.dy)
        kinds = {"picks": self.picks, "pieces": pieces, "columns": self.columns}
        made = outer(self.a, first, count, dy, *adds, **kinds)
        self.chain.mark(*(made if pieces else (made,)))
        return made

    def pair(self, *deps):
        q, mid = self.k // 4, len(self.got) // 2
        half = self.outer(2 * q, q, (self.got[:mid], 0))
        self.pair_got = swap_pair(after(half, *deps) if deps else half)

    def add(self):
        q, mid = self.k // 4, len(self.got) // 2
        self.mine = self.outer(3 * q, q, (self.got[mid:], 0), ((self.pair_got,), 0))

    def spread(self, *deps):
        self.blocks = spread_outer(after(self.mine, *deps) if deps else self.mine)

    def total(self):
        return summed(self.blocks)


VMEM_LIMIT = 58 * 2**20


def dot(a, b):
    return jnp.dot(a, b, preferred_element_type=F32)


def dot_nt(a, b):
    return lax.dot_general(a, b, (((1,), (1,)), ((), ())), preferred_element_type=F32)


def dot_tn(a, b):
    return lax.dot_general(a, b, (((0,), (0,)), ((), ())), preferred_element_type=F32)


SMEM_SPEC = pl.BlockSpec(memory_space=pltpu.SMEM)
VMEM_SPEC = pl.BlockSpec(memory_space=pltpu.VMEM)
ANY_SPEC = pl.BlockSpec(memory_space=pl.ANY)


def shape_of(rows, columns, dtype=F32):
    return jax.ShapeDtypeStruct((rows, columns), dtype)


def kernel_call(body, out_shape, args, specs, out_specs, name, scratch=(), cost=0):
    return pl.pallas_call(
        body,
        in_specs=specs,
        out_specs=out_specs,
        out_shape=out_shape,
        scratch_shapes=scratch,
        compiler_params=pltpu.CompilerParams(vmem_limit_bytes=VMEM_LIMIT),
        cost_estimate=pl.CostEstimate(flops=cost, bytes_accessed=0, transcendentals=0),
        name=name,
    )(*args)


class Rows:
    def __init__(self, d_loc, inner_width, width):
        self.d = d_loc
        self.width = width
        self.ups = inner_width // width
        self.down_rows = self.ups * d_loc
        self.w_in = 0
        self.qkv = d_loc
        self.attn = 4 * d_loc
        self.up = 5 * d_loc
        self.down = self.up + self.ups * d_loc


def fetch(src, row, rows, dst, sem):
    copy = pltpu.make_async_copy(src.at[:, pl.ds(row, rows)], dst, sem)
    copy.start()
    return copy


def whole(ref):
    value = ref[...]
    return value.reshape(value.shape[0] * value.shape[1], value.shape[2])


def halves(x):
    low_half = lax.broadcasted_iota(jnp.int32, x.shape, 1) < HEAD_DIM
    zero = jnp.zeros_like(x)
    return jnp.where(low_half, x, zero), jnp.where(low_half, zero, x)


def joined(a, b):
    return jnp.where(lax.broadcasted_iota(jnp.int32, a.shape, 1) < HEAD_DIM, a, b)


def softmax_t(scores, mask):
    logits = jnp.where(mask, scores, NEG_FILL)
    e = jnp.exp(logits - jnp.max(logits, axis=0, keepdims=True))
    return e * (1.0 / jnp.sum(e, axis=0, keepdims=True))


FACTOR = HEAD_DIM ** (-0.5)


def attend_lanes(q, k, v, mask):
    scaled = q * jnp.asarray(FACTOR, BF)
    scores = [dot_nt(k, part) for part in halves(scaled)]
    probs = [softmax_t(s, mask).astype(BF) for s in scores]
    return joined(*[dot_tn(p, v) for p in probs]).astype(BF)


def attend_back_lanes(g, q, k, v, mask):
    scaled = q * jnp.asarray(FACTOR, BF)
    grads = []
    for q_part, g_part in zip(halves(scaled), halves(g)):
        probs = softmax_t(dot_nt(k, q_part), mask)
        d_probs = dot_nt(v, g_part)
        centred = jnp.sum(probs * d_probs, axis=0, keepdims=True)
        d_s = (probs * (d_probs - centred) * FACTOR).astype(BF)
        grads.append((dot_tn(d_s, k), dot(d_s, q), dot(probs.astype(BF), g)))
    return [joined(a, b).astype(BF) for a, b in zip(*grads)]


def lanes_of(i, offset=0):
    return pl.ds(pl.multiple_of(offset + i * 128, 128), 128)


def attend_all(q_ref, q_at, kv_ref, k_at, v_at, mask_ref, out_ref, width):
    rows = q_ref.shape[0]

    def step(i, carry):
        for b in range(rows // SEQ):
            s = pl.ds(b * SEQ, SEQ)
            out_ref[s, lanes_of(i)] = attend_lanes(
                q_ref[s, lanes_of(i, q_at)],
                kv_ref[s, lanes_of(i, k_at)],
                kv_ref[s, lanes_of(i, v_at)],
                mask_ref[b] > 0,
            )
        return carry

    lax.fori_loop(0, width // 128, step, 0)


def attend_back_all(g_ref, q_ref, q_at, kv_ref, k_at, v_at, mask_ref, out_ref, width):
    rows = g_ref.shape[0]

    def step(i, carry):
        for b in range(rows // SEQ):
            s = pl.ds(b * SEQ, SEQ)
            parts = attend_back_lanes(
                g_ref[s, lanes_of(i)],
                q_ref[s, lanes_of(i, q_at)],
                kv_ref[s, lanes_of(i, k_at)],
                kv_ref[s, lanes_of(i, v_at)],
                mask_ref[b] > 0,
            )
            for at, part in enumerate(parts):
                out_ref[s, lanes_of(i, at * width)] = part
        return carry

    lax.fori_loop(0, width // 128, step, 0)


def norm_values(values, gain, bias):
    centre = values - jnp.mean(values, axis=-1, keepdims=True)
    inverse = lax.rsqrt(jnp.mean(centre * centre, axis=-1, keepdims=True) + 1e-05)
    normed = centre * inverse
    return normed * gain + bias, normed, inverse


def norm_back_values(upstream, normed, inverse, gain):
    scaled = upstream * gain
    return inverse * (
        scaled
        - jnp.mean(scaled, axis=-1, keepdims=True)
        - normed * jnp.mean(scaled * normed, axis=-1, keepdims=True)
    )


def gelu_parts(inner, with_slope):
    erf = 1.0 + lax.erf(inner * (1.0 / math.sqrt(2.0)))
    active = (0.5 * inner * erf).astype(BF)
    if not with_slope:
        return active
    bell = jnp.exp(-0.5 * inner * inner) * (1.0 / math.sqrt(2.0 * math.pi))
    return active, (0.5 * erf + inner * bell).astype(BF)


BLOCK = 512


def column(j, size=BLOCK):
    return pl.ds(pl.multiple_of(j * size, size), size)


def blocks_loop(count, step):
    lax.fori_loop(0, count, lambda j, carry: (step(j), carry)[1], 0)


def front(tokens, mask, weights, rows_of, gains, biases):
    t = tokens.shape[0]
    n, _, width = weights.shape
    d, ups = rows_of.d, rows_of.ups
    inner_width = ups * width

    def kernel(x_ref, mask_ref, g0, g1, g2, b0, b1, b2, w_hbm, *refs):
        xa_hbm, ia_ref, first_hbm, packed_hbm, mix_hbm, second_hbm, xb_hbm, ib_ref, second_low_hbm, memory_ref = refs[:10]
        w_in, w_qkv, w_attn, w_up, w_down, held, normed, low, packed, mix, second_low, total, active = refs[10:23]
        sems, out_sems = refs[23:]
        first_copy = fetch(w_hbm, rows_of.w_in, d, w_in, sems.at[0])
        qkv_copies = [fetch(w_hbm, rows_of.qkv + i * d, d, w_qkv.at[i], sems.at[1 + i]) for i in range(3)]
        attn_copy = fetch(w_hbm, rows_of.attn, d, w_attn, sems.at[4])
        up_copies = [fetch(w_hbm, rows_of.up + i * d, d, w_up.at[i], sems.at[6 + i]) for i in range(ups)]
        down_copy = fetch(w_hbm, rows_of.down, rows_of.down_rows, w_down, sems.at[5])
        outs = []

        def put(src, dst):
            outs.append(pltpu.make_async_copy(src, dst, out_sems.at[len(outs)]))
            outs[-1].start()

        first_copy.wait()
        first, xa, ia = norm_values(dot(x_ref[...], whole(w_in)), g0[...], b0[...])
        held[...] = first
        normed[...] = xa
        ia_ref[...] = ia
        low[...] = first.astype(BF)
        put(normed, xa_hbm)
        put(low, first_hbm)
        for copy in qkv_copies:
            copy.wait()

        def project(j):
            packed[:, column(j, width)] = dot(
                low[...], w_qkv[j].reshape(n * d, width)
            ).astype(BF)

        blocks_loop(3, project)
        put(packed, packed_hbm)
        attend_all(packed, 0, packed, width, 2 * width, mask_ref, mix, width)
        put(mix, mix_hbm)
        attn_copy.wait()
        second, xb, ib = norm_values(held[...] + dot(mix[...], whole(w_attn)), g1[...], b1[...])
        outs[0].wait()
        held[...] = second
        normed[...] = xb
        ib_ref[...] = ib
        second_low[...] = second.astype(BF)
        put(held, second_hbm)
        put(normed, xb_hbm)
        put(second_low, second_low_hbm)
        for copy in up_copies:
            copy.wait()

        def forward(j):
            active[j] = gelu_parts(dot(second_low[...], w_up[j].reshape(n * d, width)), False)

        blocks_loop(ups, forward)
        down_copy.wait()
        total[...] = second

        def forward_down(j):
            rows = pl.ds(j * (n // ups), n // ups)
            total[...] += dot(active[j], w_down[rows].reshape(width, width))

        blocks_loop(ups, forward_down)
        memory_ref[...] = norm_values(total[...], g2[...], b2[...])[0].astype(BF)
        for copy in outs[1:]:
            copy.wait()

    value, low, vector = shape_of(t, width), shape_of(t, width, BF), shape_of(t, 1)
    big = lambda *shape: pltpu.VMEM(shape, BF)
    return kernel_call(
        kernel,
        (value, vector, low, shape_of(t, 3 * width, BF), low, value, value, vector, low, low),
        (tokens, mask, *gains, *biases, weights),
        [VMEM_SPEC] * 8 + [ANY_SPEC],
        (ANY_SPEC, VMEM_SPEC) + (ANY_SPEC,) * 5 + (VMEM_SPEC, ANY_SPEC, VMEM_SPEC),
        "front",
        scratch=[
            big(n, d, width),
            big(3, n, d, width),
            big(n, d, width),
            big(ups, n, d, width),
            big(n, rows_of.down_rows, width),
            pltpu.VMEM((t, width), F32),
            pltpu.VMEM((t, width), F32),
            big(t, width),
            big(t, 3 * width),
            big(t, width),
            big(t, width),
            pltpu.VMEM((t, width), F32),
            big(ups, t, width),
            pltpu.SemaphoreType.DMA((6 + ups,)),
            pltpu.SemaphoreType.DMA((7,)),
        ],
    )


class Cross:
    def __init__(self, weights):
        self.n, rows, self.width = weights.shape
        self.c = rows // 8
        if self.c % 16:
            both = weights.reshape(self.n, 2, 4, self.c, self.width).transpose(2, 1, 0, 3, 4)
            weights = both.reshape(4, 2 * self.n * self.c, self.width)
        self.weights = weights

    @property
    def scratch(self):
        return pltpu.VMEM((4, 2, self.n, self.c, self.width), BF)

    def start(self, ref, dst, sems, groups):
        copies = {}
        for i in groups:
            copies[i] = []
            for s in range(2):
                if self.c % 16:
                    count = self.n * self.c
                    src = ref.at[i, pl.ds(s * count, count)].reshape(self.n, self.c, self.width)
                else:
                    src = ref.at[:, pl.ds((4 * s + i) * self.c, self.c)]
                copies[i].append(pltpu.make_async_copy(src, dst.at[i, s], sems.at[i, s]))
                copies[i][-1].start()
        return copies

    def matrix(self, ref, i):
        return ref[i].reshape(2 * self.n * self.c, self.width)


def cross_query(low, cross):
    t, width = low.shape

    def kernel(low_ref, w_hbm, out_ref, w, sems):
        for copy in cross.start(w_hbm, w, sems, (0,))[0]:
            copy.wait()
        out_ref[...] = dot(low_ref[...], cross.matrix(w, 0)).astype(BF)

    return kernel_call(
        kernel,
        shape_of(t, width, BF),
        (low, cross.weights),
        [VMEM_SPEC, ANY_SPEC],
        VMEM_SPEC,
        "cross_query",
        scratch=[cross.scratch, pltpu.SemaphoreType.DMA((4, 2))],
    )


def cross_query_back(resid, d_cross, cross):
    t, width = resid.shape

    def kernel(resid_ref, d_ref, w_hbm, out_ref, w, sems):
        for copy in cross.start(w_hbm, w, sems, (0,))[0]:
            copy.wait()
        out_ref[...] = resid_ref[...] + dot_nt(d_ref[:, :width], cross.matrix(w, 0))

    return kernel_call(
        kernel,
        shape_of(t, width),
        (resid, d_cross, cross.weights),
        [VMEM_SPEC, VMEM_SPEC, ANY_SPEC],
        VMEM_SPEC,
        "cross_query_back",
        scratch=[cross.scratch, pltpu.SemaphoreType.DMA((4, 2))],
    )


def decoder_middle(info, memory, cross_q, second, cot, mask, weights, rows_of, cross, c_gain, c_bias, gain, bias):
    t, width = second.shape
    n, d, ups = weights.shape[0], rows_of.d, rows_of.ups
    inner_width = ups * width
    block = inner_width // n
    ordered = block % 128 == 0
    per = n // ups

    def kernel(info_ref, memory_ref, q_ref, mask_ref, cg_ref, cb_ref, g_ref, b_ref, second_hbm, cot_hbm, w_hbm, c_hbm, *refs):
        out_hbm, normed_hbm, inv_ref, third_hbm, active_hbm, slope_hbm = refs[:6]
        mix_ref, d_qkv_ref, d_memory_ref, resid_ref, dg_ref, db_ref = refs[6:12]
        w_c, w_up, w_down, kv, third, low, active, slope, out, normed, c_normed, total, cot = refs[12:25]
        d_branch_ref, cross_sems, sems, act_sems = refs[25:]
        is_dec = info_ref[1] == 1
        copies = cross.start(c_hbm, w_c, cross_sems, (1, 2, 3))
        get_second = pltpu.make_async_copy(second_hbm, third, sems.at[0])
        get_cot = pltpu.make_async_copy(cot_hbm, cot, sems.at[1])
        get_second.start()
        up_copies = [fetch(w_hbm, rows_of.up + i * d, d, w_up.at[i], sems.at[8 + i]) for i in range(ups)]
        down_copy = fetch(w_hbm, rows_of.down, rows_of.down_rows, w_down, sems.at[7])
        get_cot.start()
        for i in (1, 2):
            for copy in copies[i]:
                copy.wait()
            kv[:, (i - 1) * width : i * width] = dot(memory_ref[...], cross.matrix(w_c, i)).astype(BF)
        attend_all(q_ref, 0, kv, 0, width, mask_ref, mix_ref, width)
        get_second.wait()
        for copy in copies[3]:
            copy.wait()
        values = third[...] + dot(mix_ref[...], cross.matrix(w_c, 3))
        third_c, normed_c, inverse_c = norm_values(values, cg_ref[...], cb_ref[...])
        c_normed[...] = normed_c
        third[...] = jnp.where(is_dec, third_c, third[...])
        low[...] = third[...].astype(BF)
        outs = [pltpu.make_async_copy(low, third_hbm, sems.at[2])]
        outs[-1].start()
        for copy in up_copies:
            copy.wait()

        def forward(j):
            active[j], slope[j] = gelu_parts(dot(low[...], w_up[j].reshape(n * d, width)), True)

        blocks_loop(ups, forward)
        if not ordered:
            outs.append(pltpu.make_async_copy(active, active_hbm, act_sems.at[0]))
            outs[-1].start()
        for j in range(n if ordered else 0):
            place = info_ref[2 + j]
            outs.append(
                pltpu.make_async_copy(
                    active.at[j // per, :, pl.ds((j % per) * block, block)],
                    active_hbm.at[:, column(place, block)],
                    act_sems.at[j],
                )
            )
            outs[-1].start()
        outs.append(pltpu.make_async_copy(slope, slope_hbm, sems.at[4]))
        outs[-1].start()
        down_copy.wait()
        total[...] = third[...]

        def forward_down(j):
            total[...] += dot(active[j], w_down[pl.ds(j * per, per)].reshape(width, width))

        blocks_loop(ups, forward_down)
        last, normed_d, inverse_d = norm_values(total[...], g_ref[...], b_ref[...])
        out[...] = last
        normed[...] = normed_d
        inv_ref[...] = inverse_d
        outs += [
            pltpu.make_async_copy(out, out_hbm, sems.at[5]),
            pltpu.make_async_copy(normed, normed_hbm, sems.at[6]),
        ]
        outs[-2].start()
        outs[-1].start()
        get_cot.wait()
        grad = norm_back_values(cot[...], normed_d, inverse_d, g_ref[...])
        total[...] = grad
        d_branch_ref[...] = grad.astype(BF)

        def backward(j):
            d_act = dot_nt(d_branch_ref[...], w_down[pl.ds(j * per, per)].reshape(width, width))
            d_inner = (d_act * slope[j].astype(F32)).astype(BF)
            total[...] += dot_nt(d_inner, w_up[j].reshape(n * d, width))

        blocks_loop(ups, backward)
        grad = total[...]
        dg_ref[...] = jnp.sum(grad * c_normed[...], axis=0, keepdims=True)
        db_ref[...] = jnp.sum(grad, axis=0, keepdims=True)
        resid = norm_back_values(grad, c_normed[...], inverse_c, cg_ref[...])
        resid_ref[...] = resid
        d_branch_ref[...] = resid.astype(BF)
        outs[0].wait()
        low[...] = dot_nt(d_branch_ref[...], cross.matrix(w_c, 3)).astype(BF)
        attend_back_all(low, q_ref, 0, kv, 0, width, mask_ref, d_qkv_ref, width)
        d_qkv_ref[:, 3 * width :] = d_branch_ref[...]
        d_memory = dot_nt(d_qkv_ref[:, width : 2 * width], cross.matrix(w_c, 1))
        d_memory_ref[...] = (
            d_memory + dot_nt(d_qkv_ref[:, 2 * width : 3 * width], cross.matrix(w_c, 2))
        ).astype(BF)
        for copy in outs[1:]:
            copy.wait()

    value, low = shape_of(t, width), shape_of(t, width, BF)
    vector, blocked = shape_of(1, width), jax.ShapeDtypeStruct((ups, t, width), BF)
    big = lambda *shape: pltpu.VMEM(shape, BF)
    return kernel_call(
        kernel,
        (value, value, shape_of(t, 1), low)
        + (shape_of(t, inner_width, BF) if ordered else blocked, blocked)
        + (low, shape_of(t, 4 * width, BF), low, value, vector, vector),
        (info, memory, cross_q, mask, c_gain, c_bias, gain, bias, second, cot, weights, cross.weights),
        [SMEM_SPEC] + [VMEM_SPEC] * 7 + [ANY_SPEC] * 4,
        (ANY_SPEC, ANY_SPEC, VMEM_SPEC, ANY_SPEC, ANY_SPEC, ANY_SPEC) + (VMEM_SPEC,) * 6,
        "decoder_middle",
        scratch=[
            cross.scratch,
            big(ups, n, d, width),
            big(n, rows_of.down_rows, width),
            big(t, 2 * width),
            pltpu.VMEM((t, width), F32),
            big(t, width),
            big(ups, t, width),
            big(ups, t, width),
        ]
        + [pltpu.VMEM((t, width), F32)] * 5
        + [
            big(t, width),
            pltpu.SemaphoreType.DMA((4, 2)),
            pltpu.SemaphoreType.DMA((8 + ups,)),
            pltpu.SemaphoreType.DMA((n,)),
        ],
    )


def put_pieces(refs, i, count, value):
    rows, size = value.shape
    value = value.astype(BF)
    side, at = divmod(i, count // 2)
    for h in range(2):
        refs[2 * h + side][:, at * size : (at + 1) * size] = value[h * rows // 2 : (h + 1) * rows // 2]


def norm_backward(cot, more, normed, inverse, gain, active_rel):
    t, width = cot.shape
    half = active_rel.shape[0] // 2

    def kernel(cot_ref, more_ref, n_ref, i_ref, gain_ref, a_hbm, *refs):
        grad_ref, low_ref, dg_ref, db_ref, *sent_refs, a, sem = refs
        copy = pltpu.make_async_copy(a_hbm.at[pl.ds(0, half)], a, sem)
        copy.start()
        g = cot_ref[...] + more_ref[...].astype(F32)
        dg_ref[...] = jnp.sum(g * n_ref[...], axis=0, keepdims=True)
        db_ref[...] = jnp.sum(g, axis=0, keepdims=True)
        grad = norm_back_values(g, n_ref[...], i_ref[...], gain_ref[...])
        grad_ref[...] = grad
        low_ref[...] = grad.astype(BF)
        copy.wait()

        for h in range(2):

            def step(j):
                value = dot(a[column(2 * h + j, half // 4)], low_ref[...]).astype(BF)
                for c in range(2):
                    sent_refs[2 * h + c][column(j, half // 4)] = value[:, c * width // 2 : (c + 1) * width // 2]

            blocks_loop(2, step)

    vector = shape_of(1, width)
    return kernel_call(
        kernel,
        (shape_of(t, width), shape_of(t, width, BF), vector, vector)
        + (shape_of(half // 2, width // 2, BF),) * 4,
        (cot, more, normed, inverse, gain, active_rel),
        [VMEM_SPEC] * 5 + [ANY_SPEC],
        (VMEM_SPEC,) * 8,
        "norm_backward",
        scratch=[pltpu.VMEM((half, t), BF), pltpu.SemaphoreType.DMA],
    )


def ffn_backward(branch, slope, weights, rows_of, third_rel):
    t, width = branch.shape
    n, d, ups = weights.shape[0], rows_of.d, rows_of.ups
    per = n // ups
    half = width // 2

    def kernel(branch_ref, slope_ref, a_ref, w_hbm, out_ref, d_inner_ref, *refs):
        *sent_refs, w_up, w_down, sems = refs
        down_copies = [
            pltpu.make_async_copy(
                w_hbm.at[pl.ds(i * per, per), pl.ds(rows_of.down, rows_of.down_rows)],
                w_down.at[pl.ds(i * per, per)],
                sems.at[i],
            )
            for i in range(ups)
        ]
        for copy in down_copies:
            copy.start()
        up_copies = [fetch(w_hbm, rows_of.up + i * d, d, w_up.at[i], sems.at[ups + i]) for i in range(ups)]
        for i in range(ups):
            cols = slice(i * width, (i + 1) * width)
            down_copies[i].wait()
            d_act = dot_nt(branch_ref[...], w_down[i * per : (i + 1) * per].reshape(width, width))
            d_inner_ref[:, cols] = (d_act * slope_ref[i].astype(F32)).astype(BF)
            put_pieces(sent_refs, i, ups, dot(a_ref[:half], d_inner_ref[:, cols]))
        for i in range(ups):
            up_copies[i].wait()
            part = dot_nt(
                d_inner_ref[:, i * width : (i + 1) * width], w_up[i].reshape(n * d, width)
            )
            if i == 0:
                out_ref[...] = part
            else:
                out_ref[...] += part

    return kernel_call(
        kernel,
        (shape_of(t, width), shape_of(t, ups * width, BF)) + (shape_of(half // 2, ups * width // 2, BF),) * 4,
        (branch, slope, third_rel, weights),
        [VMEM_SPEC, VMEM_SPEC, VMEM_SPEC, ANY_SPEC],
        (VMEM_SPEC,) * 6,
        "ffn_backward",
        scratch=[
            pltpu.VMEM((ups, n, d, width), BF),
            pltpu.VMEM((n, rows_of.down_rows, width), BF),
            pltpu.SemaphoreType.DMA((2 * ups,)),
        ],
    )


def attention_backward(info, from_dec, third, inner, normed, inverse, gain, weights, rows_of, packed, mask, stack):
    t, width = third.shape
    n, d = weights.shape[0], rows_of.d
    half = width // 2

    def kernel(info_ref, dec_ref, third_ref, inner_ref, n_ref, i_ref, gain_ref, packed_ref, mask_ref, a_ref, w_hbm, *refs):
        grad_ref, d_ref, dg_ref, db_ref, *sent_refs, w_attn, blended, sem = refs
        copy = fetch(w_hbm, rows_of.attn, d, w_attn, sem)
        g = jnp.where(info_ref[1] == 1, dec_ref[...], third_ref[...] + inner_ref[...])
        dg_ref[...] = jnp.sum(g * n_ref[...], axis=0, keepdims=True)
        db_ref[...] = jnp.sum(g, axis=0, keepdims=True)
        grad = norm_back_values(g, n_ref[...], i_ref[...], gain_ref[...])
        grad_ref[...] = grad
        d_ref[:, 3 * width :] = grad.astype(BF)
        copy.wait()
        blended[...] = dot_nt(d_ref[:, 3 * width :], whole(w_attn)).astype(BF)
        attend_back_all(
            blended, packed_ref, 0, packed_ref, width, 2 * width, mask_ref, d_ref, width
        )
        for i in range(4):
            cols = slice(i * width, (i + 1) * width)
            put_pieces(sent_refs, i, 4, dot(a_ref[0 if i < 3 else 1, :half], d_ref[:, cols]))

    wide, vector = shape_of(t, 4 * width, BF), shape_of(1, width)
    return kernel_call(
        kernel,
        (shape_of(t, width), wide, vector, vector) + (shape_of(half // 2, 2 * width, BF),) * 4,
        (info, from_dec, third, inner, normed, inverse, gain, packed, mask, stack, weights),
        [SMEM_SPEC] + [VMEM_SPEC] * 8 + [VMEM_SPEC, ANY_SPEC],
        (VMEM_SPEC,) * 8,
        "attention_backward",
        scratch=[
            pltpu.VMEM((n, d, width), BF),
            pltpu.VMEM((t, width), BF),
            pltpu.SemaphoreType.DMA,
        ],
    )


def embed_backward(grad, d_packed, normed, inverse, gain, weights, rows_of):
    t, width = grad.shape
    n, d = weights.shape[0], rows_of.d

    def kernel(grad_ref, dp_ref, n_ref, i_ref, gain_ref, w_hbm, *refs):
        low_ref, tokens_ref, dg_ref, db_ref, w_qkv, w_in, total, sems = refs
        copies = [fetch(w_hbm, rows_of.qkv + i * d, d, w_qkv.at[i], sems.at[i]) for i in range(3)]
        last = fetch(w_hbm, rows_of.w_in, d, w_in, sems.at[3])
        total[...] = grad_ref[...]
        for i in range(3):
            copies[i].wait()
            total[...] += dot_nt(
                dp_ref[:, i * width : (i + 1) * width], w_qkv[i].reshape(n * d, width)
            )
        g = total[...]
        dg_ref[...] = jnp.sum(g * n_ref[...], axis=0, keepdims=True)
        db_ref[...] = jnp.sum(g, axis=0, keepdims=True)
        low_ref[...] = norm_back_values(g, n_ref[...], i_ref[...], gain_ref[...]).astype(BF)
        last.wait()
        tokens_ref[...] = dot_nt(low_ref[...], whole(w_in))

    vector = shape_of(1, width)
    return kernel_call(
        kernel,
        (shape_of(t, width, BF), shape_of(t, n * d), vector, vector),
        (grad, d_packed, normed, inverse, gain, weights),
        [VMEM_SPEC, VMEM_SPEC] + [VMEM_SPEC] * 3 + [ANY_SPEC],
        (VMEM_SPEC,) * 4,
        "embed_backward",
        scratch=[
            pltpu.VMEM((3, n, d, width), BF),
            pltpu.VMEM((n, d, width), BF),
            pltpu.VMEM((t, width), F32),
            pltpu.SemaphoreType.DMA((4,)),
        ],
    )


def outer(a, first, count, dy, *adds, picks=(), pieces=False, columns=None):
    t = dy.shape[0]
    start, width = columns or (0, dy.shape[1])
    block = min(width if columns else width // 2, 1024)
    grid = width // block
    mid = grid // 2
    per = grid // max(len(picks), 1)
    stacked = a.ndim == 3
    low = lambda j: jnp.minimum(j, mid - 1)
    high = lambda j: jnp.maximum(j - mid, 0)

    def kernel(a_ref, dy_ref, *refs):
        j = pl.program_id(0)
        value = dot(a_ref[0] if stacked else a_ref[...], dy_ref[...])
        outs = refs[sum(len(parts) for parts, _ in adds) :]
        for parts, _ in adds:
            terms, refs = [ref[...].astype(F32) for ref in refs[: len(parts)]], refs[len(parts) :]
            value = value + (jnp.where(j < mid, *terms) if len(terms) == 2 else terms[0])
        value = value.astype(BF)
        if not pieces:
            outs[0][...] = value
            return

        @pl.when(j < mid)
        def _():
            outs[0][...] = value[: count // 2]
            outs[2][...] = value[count // 2 :]

        @pl.when(j >= mid)
        def _():
            outs[1][...] = value[: count // 2]
            outs[3][...] = value[count // 2 :]

    if stacked:
        pick = lambda j: sum(jnp.where(j // per == i, at, 0) for i, at in enumerate(picks))
        a_spec = pl.BlockSpec((1, count, t), lambda j: (pick(j), first // count, 0))
    else:
        a_spec = pl.BlockSpec((count, t), lambda j: (first // count, 0))
    specs = [a_spec, pl.BlockSpec((t, block), lambda j: (0, start // block + j))]
    for parts, at in adds:
        for place in (low, high) if len(parts) == 2 else (lambda j: j,):
            specs.append(pl.BlockSpec((count, block), lambda j, at=at, place=place: (at // count, place(j))))
    if pieces:
        out_specs = [pl.BlockSpec((count // 2, block), lambda j, place=place: (0, place(j))) for place in (low, high)] * 2
        out_shape = [jax.ShapeDtypeStruct((count // 2, width // 2), BF)] * 4
    else:
        out_specs = pl.BlockSpec((count, block), lambda j: (0, j))
        out_shape = jax.ShapeDtypeStruct((count, width), BF)
    return pl.pallas_call(
        kernel,
        grid=(grid,),
        in_specs=specs,
        out_specs=out_specs,
        out_shape=out_shape,
        compiler_params=pltpu.CompilerParams(vmem_limit_bytes=VMEM_LIMIT),
        cost_estimate=pl.CostEstimate(flops=0, bytes_accessed=0, transcendentals=0),
        name="outer",
    )(a, dy, *[part for parts, _ in adds for part in parts])


def shards(
    section_in,
    segment_ids,
    out_cot,
    in_proj,
    attn_in,
    attn_out,
    ffn_in,
    ffn_out,
    norm_gain,
    norm_bias,
    cross_in,
    cross_out,
    cross_gain,
    cross_bias,
):
    n = lax.axis_size("dp")
    me = lax.axis_index("dp")
    is_dec = lax.axis_index("section") == 1
    width = attn_out.shape[2]
    inner_width = ffn_in.shape[2]
    d_loc = attn_out.shape[1]
    in_loc = in_proj.shape[1]
    c_loc = cross_in.shape[0]
    m = n // 4
    depth = d_loc * n

    order = relative_blocks(me, n)
    places = jnp.sum(jnp.arange(n)[:, None] * (order[:, None] == jnp.arange(n)[None, :]), axis=0)
    info = jnp.concatenate([jnp.stack([me, lax.axis_index("section")]), places]).astype(jnp.int32)

    rows_of = Rows(d_loc, inner_width, width)
    params = jnp.concatenate(
        [norm_gain[0].reshape(-1), norm_bias[0].reshape(-1), cross_gain, cross_bias]
    )
    n_par = params.shape[0]

    def columns_of(w):
        return [w[:, i * width : (i + 1) * width] for i in range(w.shape[1] // width)]

    pack = [in_proj[0], jnp.pad(params[None], ((0, d_loc - in_loc - 1), (0, width - n_par)))]
    pack += columns_of(attn_in[0]) + [attn_out[0]] + columns_of(ffn_in[0]) + [ffn_out[0]]
    weights = lax.all_gather(jnp.concatenate(pack, axis=0).astype(BF), "dp", axis=0)
    own_cross = jnp.concatenate(columns_of(cross_in) + [cross_out], axis=0).astype(BF)
    cross_pack = jnp.concatenate([to_decoder(own_cross), own_cross], axis=0)
    cross_w = Cross(lax.all_gather(after(cross_pack, weights), "dp", axis=0))

    tokens = section_in[0]
    tokens = tokens.reshape(tokens.shape[0], n, in_loc)
    tokens = jnp.pad(tokens, ((0, 0), (0, 0), (0, d_loc - in_loc))).reshape(-1, depth)
    cot = out_cot[0]
    seqs = tokens.shape[0] // SEQ
    seg = segment_ids.reshape(2, seqs, SEQ)
    own_seg = jnp.where(is_dec, seg[1], seg[0])
    enc_seg = seg[0]
    spots = jnp.arange(SEQ)
    causal = (spots[:, None] <= spots[None, :]) | jnp.logical_not(is_dec)
    self_mask = ((own_seg[:, None, :] == own_seg[:, :, None]) & causal[None]).astype(F32)
    cross_mask = (own_seg[:, None, :] == enc_seg[:, :, None]).astype(F32)
    perm_d = order_matrix(order, d_loc)
    perm_cross = order_matrix(order, c_loc, 2)
    marks = (jnp.arange(depth)[None, :] == (jnp.arange(n) * d_loc + in_loc)[:, None]).astype(BF)
    tokens_rel = reordered(jnp.concatenate([tokens, marks], axis=0), perm_d)

    pars = weights[:, in_loc, :n_par].astype(F32)

    def vectors(at):
        part = pars[:, 3 * at * d_loc : 3 * (at + 1) * d_loc].reshape(n, 3, d_loc)
        part = part.transpose(1, 0, 2).reshape(3, 1, width)
        return [part[i] for i in range(3)]

    gains, biases = vectors(0), vectors(1)
    own_cpar = pars[:, 6 * d_loc :].astype(BF)
    cpar = jnp.stack([to_decoder(own_cpar), own_cpar]).astype(F32)
    c_gain = cpar[:, :, :c_loc].reshape(1, width)
    c_bias = cpar[:, :, c_loc:].reshape(1, width)

    xa, ia, first_low, packed, blended, second, xb, ib, second_low, encoded = front(
        tokens, self_mask, weights, rows_of, gains, biases
    )
    memory = to_decoder(encoded)
    cross_q = cross_query(second_low, cross_w)
    attn_rel = jnp.stack([reordered(first_low, perm_d), reordered(blended, perm_d)])
    second_rel = reordered(second_low, perm_cross)
    cross_q = after(cross_q, attn_rel, second_rel, tokens_rel)

    output, xd, idd, third_low, active_rel, slope, cross_mix, d_cross, d_memory, resid, dg_c, db_c = (
        decoder_middle(
            info,
            memory,
            cross_q,
            second,
            cot,
            cross_mask,
            weights,
            rows_of,
            cross_w,
            c_gain,
            c_bias,
            gains[2],
            biases[2],
        )
    )
    grad_memory = to_encoder(d_memory)
    grad_second_dec = cross_query_back(resid, d_cross, cross_w)
    third_rel = reordered(third_low, perm_d)
    if active_rel.ndim == 3:
        blocks = active_rel.transpose(1, 0, 2).reshape(tokens.shape[0], n, inner_width // n)
        active_rel = blocks[:, order].reshape(tokens.shape[0], inner_width)
    active_rel = active_rel.T
    cross_rel = jnp.stack(
        [second_rel, reordered(memory, perm_cross), reordered(cross_mix, perm_cross)]
    )
    cvec = jnp.concatenate([dg_c, db_c]).astype(BF).reshape(2, 2, n, c_loc)
    cvec_got = to_encoder(cvec[:, 0])
    cot = after(cot, grad_second_dec, third_rel, cross_rel)

    chain = Chain()
    quarter = width // 4
    grad_d, branch_d, dg_d, db_d, *sent = norm_backward(
        cot, grad_memory, xd, idd, gains[2], active_rel
    )
    chain.mark(*sent)
    got = [swap_core(piece) for piece in sent]
    half = width // 2
    down0 = Part(chain, active_rel, branch_d, got[::2], (), (0, half))
    down1 = Part(chain, active_rel, branch_d, got[1::2], (), (half, half))
    cross = Part(chain, cross_rel, d_cross, picks=(0, 1, 1, 2))
    down0.pair()
    grad_inner, d_inner, *sent = ffn_backward(
        chain(branch_d), slope, weights, rows_of, third_rel
    )
    chain.mark(*sent)
    up = Part(chain, third_rel, d_inner, [swap_core(piece) for piece in sent])
    far = cross.outer(2 * quarter, quarter, (cross.got[:2], 0))
    far = to_encoder(after(far, cvec_got))
    down1.pair(down0.pair_got)
    down0.add()
    down0.spread()
    grad_b, d_attn, dg_b, db_b, *sent = attention_backward(
        info,
        grad_second_dec,
        grad_d,
        chain(grad_inner),
        xb,
        ib,
        gains[1],
        weights,
        rows_of,
        packed,
        self_mask,
        attn_rel,
    )
    chain.mark(*sent)
    attn = Part(chain, attn_rel, d_attn, [swap_core(piece) for piece in sent], (0, 0, 0, 1))
    up.pair()
    d_embed, d_tokens, dg_a, db_a = embed_backward(
        grad_b, chain(d_attn), xa, ia, gains[0], weights, rows_of
    )
    chain.mark(d_embed)
    down1.add()
    down1.spread(down0.blocks)
    cvec = jnp.where(is_dec, cvec[:, 1], cvec_got).transpose(1, 0, 2)
    vecs = jnp.concatenate([dg_a, dg_b, dg_d, db_a, db_b, db_d]).astype(BF)
    vecs = vecs.reshape(6, n, d_loc).transpose(1, 0, 2).reshape(n, 6 * d_loc)
    vecs = jnp.concatenate([vecs, cvec.reshape(n, 2 * c_loc)], axis=1)
    vecs = jnp.pad(vecs, ((0, 0), (0, width - n_par)))
    into = Part(chain, tokens_rel, jnp.concatenate([d_embed, vecs], axis=0))
    near = cross.outer(3 * quarter, quarter, (cross.got[2:], 0))
    near = chain.mark(jnp.where(is_dec, near, far))
    cross_pair = swap_pair(near[: quarter // 2])
    attn.pair()
    into.pair()
    up.add()
    up.spread(down1.blocks)
    cross_total = chain.mark(add_low(near[quarter // 2 :], cross_pair))
    cross_blocks = spread_outer(after(cross_total, up.blocks))
    cross_total = summed(cross_blocks)
    attn.add()
    attn.spread(cross_blocks)
    into.add()
    into.spread(attn.blocks)

    in_grad = chain(d_tokens).reshape(-1, n, d_loc)[:, :, :in_loc].reshape(-1, n * in_loc)
    attn_total = attn.total()
    in_total = into.total()
    row = in_total[in_loc]
    gain_total = row[: 3 * d_loc].reshape(1, 3, d_loc)
    bias_total = row[3 * d_loc : 6 * d_loc].reshape(1, 3, d_loc)

    return (
        output[None],
        in_grad[None],
        in_total[:in_loc][None],
        attn_total[None, :, : 3 * width],
        attn_total[None, :, 3 * width :],
        up.total()[None],
        jnp.concatenate([down0.total(), down1.total()], axis=1)[None],
        gain_total,
        bias_total,
        cross_total[:, : 3 * width],
        cross_total[:, 3 * width :],
        row[6 * d_loc : 6 * d_loc + c_loc],
        row[6 * d_loc + c_loc : n_par],
    )


def solution(mesh):
    placed = (
        P("section", "dp", None),
        P(None, "dp"),
        P("section", "dp", None),
        P("section", "dp", None),
        P("section", "dp", None),
        P("section", "dp", None),
        P("section", "dp", None),
        P("section", "dp", None),
        P("section", None, "dp"),
        P("section", None, "dp"),
        P(("section", "dp"), None),
        P(("section", "dp"), None),
        P(("section", "dp")),
        P(("section", "dp")),
    )
    return jax.shard_map(
        shards,
        mesh=mesh,
        in_specs=placed,
        out_specs=(
            P("section", "dp", None),
            P("section", "dp", None),
            P("section", "dp", None),
            P("section", "dp", None),
            P("section", "dp", None),
            P("section", "dp", None),
            P("section", "dp", None),
            P("section", None, "dp"),
            P("section", None, "dp"),
            P(("section", "dp"), None),
            P(("section", "dp"), None),
            P(("section", "dp")),
            P(("section", "dp")),
        ),
        check_vma=False,
    )
```

time: 808 us -> 594 us (0.74)
  Pallas kernels: 0 us -> 174 us
  matrix products: 151 us -> 8.65 us
  local copies, waits for them, and re-layouts: 168 us -> 29.9 us
  other arithmetic: 73.5 us -> 22.5 us
  waiting for transfers between devices: 334 us -> 286 us
  between operations: 26.8 us -> 15.1 us
    pallas_call x0 -> x22, Pallas kernels: none -> 174 us  [the longest x8 117 us: kernel_call(): pl.pallas_call(body, in_specs=specs, out_specs=out_specs, out_shape=out_s...]
    dot_general x36 -> x7, matrix products: 143 us -> 8.65 us  [reordered(): jnp.einsum('tk,kr->rt', a, matrix, preferred_element_type=F32).astype(BF)]
    ppermute x18 -> x0, waiting for transfers between devices: 84 us -> none  [shift_outer(): return lax.ppermute(x, 'dp', [(i, (i + 4) % n) for i in range(n)])]
    all_to_all x0 -> x6, waiting for transfers between devices: none -> 53.4 us  [spread_outer(): return lax.all_to_all(x, 'dp', 0, 0, axis_index_groups=groups)]
    slice x32 -> x7, local copies, waits for them, and re-layouts: 54.1 us -> 2.26 us  [the longest x1 0.95 us: shards(): chain(d_tokens).reshape(-1, n, d_loc)[:, :, :in_loc].reshape(-1, n * in_loc)]
    ppermute x6, waiting for transfers between devices: 106 us -> 55.2 us  [swap_pair(): return lax.ppermute(x, 'dp', [(i, i ^ 2) for i in range(n)])]
    reshape x21 -> x6, local copies, waits for them, and re-layouts: 45.3 us -> 2.58 us  [the longest x1 1 us: shards(): jnp.pad(tokens, ((0, 0), (0, 0), (0, d_loc - in_loc))).reshape(-1, depth)]
    convert_element_type x12 -> x1, other arithmetic: 26.8 us -> 1.24 us  [add_low(): return (a.astype(F32) + b.astype(F32)).astype(BF)]
  transfers between devices with their start and end apart: 39 -> 40, of which waited for: 21 -> 17; matrix products, arithmetic and copies ran while one was open for 35% -> 8% of each run, Pallas kernels for 0% -> 21%
where the time goes in v2:
time: 594 us; the launch traced here: 586 us
  waiting for transfers between devices  286 us (48%)
  Pallas kernels  174 us (29%)
  starting transfers between devices  50.1 us (8%)
  local copies, waits for them, and re-layouts  29.9 us (5%)
  other arithmetic  22.5 us (4%)
  between operations  15.1 us (3%)
  matrix products  8.65 us (1%)
    all_gather x1, waiting for transfers between devices, shards(): lax.all_gather(jnp.concatenate(pack, axis=0).astype(BF), 'dp', axis=0)  131 us
    pallas_call x8, Pallas kernels, kernel_call(): pl.pallas_call(body, in_specs=specs, out_specs=out_specs, out_shape=out_s...  117 us
    pallas_call x14, Pallas kernels, outer(): pl.pallas_call(kernel, grid=(grid,), in_specs=specs, out_specs=out_specs,...  57.3 us
    ppermute x6, waiting for transfers between devices, swap_pair(): return lax.ppermute(x, 'dp', [(i, i ^ 2) for i in range(n)])  55.2 us
    all_to_all x6, waiting for transfers between devices, spread_outer(): return lax.all_to_all(x, 'dp', 0, 0, axis_index_groups=groups)  53.4 us
    all_gather x1, waiting for transfers between devices, shards(): cross_w = Cross(lax.all_gather(after(cross_pack, weights), 'dp', axis=0))  27.5 us
    all_to_all x6, starting transfers between devices, spread_outer(): return lax.all_to_all(x, 'dp', 0, 0, axis_index_groups=groups)  24.5 us
  transfers between devices with their start and end apart: 40, of which 17 were waited for; matrix products, arithmetic and copies ran while one was open for 8% of the time, Pallas kernels for 21%

profile of v2, /device:TPU:0, one launch (start us, length us, event | category | flops | bytes accessed | tf_op | source)
XLA Modules:
  0.0 586.0 jit_solution(18071030124791420818)
XLA Ops:
  14.4 4.9 collective-permute-start.1
  19.3 5.5 collective-permute-done.1
  24.9 130.6 %all-gather.4.cloned.1.call-done.w_hbm = bf16[16,832,1024]{2,1,0:T(8,128)(2,1)} async-done(((bf16[1,832,1024]{2,1,0:T(8,128)(2,1)}), bf16[16,832,1024]{2,1,0:T(8,128)(2,1)}) %all-gather.4.cloned.1.call-update) | async-done | bytes 27262992 | tf_op jit(solution)/shard_map/all_gather | solution.py:872
  166.4 21.2 %front.1 = (f32[256,1024]{1,0:T(8,128)}, f32[256,1]{1,0:T(8,128)}, bf16[256,1024]{1,0:T(8,128)(2,1)}, bf16[256,3072]{1,0:T(8,128)(2,1)}, bf16[256,1024]{1,0:T(8,...) custom-call(bf16[256,1024]{1,0:T(8,128)(2,1)} %copy.68.x_ref, ...), custom_call_target="tpu_custom_call" | custom-call | tf_op jit(solution)/shard_map/front/pallas_call | solution.py:143
  197.3 5.7 collective-permute-done.2
  205.2 27.5 %all-gather.6.cloned.1.call-done = bf16[4096,1024]{1,0:T(8,128)(2,1)} async-done(((bf16[256,1024]{1,0:T(8,128)(2,1)}), bf16[4096,1024]{1,0:T(8,128)(2,1)}) %all-gather.6.cloned.1.call-update) | async-done | bytes 8388624 | tf_op jit(solution)/shard_map/all_gather | solution.py:875
  232.6 4.2 cross_query.1.q_ref
  236.8 41.0 %decoder_middle.1 = (f32[256,1024]{1,0:T(8,128)}, f32[256,1024]{1,0:T(8,128)}, f32[256,1]{1,0:T(8,128)}, bf16[256,1024]{1,0:T(8,128)(2,1)}, bf16[256,4096]{1,0:T...) custom-call(s32[18]{0:T(128)} %pad_add_fusion.info_ref, ...), custom_call_target="tpu_custom_call" | custom-call | tf_op jit(solution)/shard_map/decoder_middle/pallas_call | solution.py:143
  279.4 5.3 cross_query_back.1.dec_ref
  294.8 6.8 %norm_backward.1 = (f32[256,1024]{1,0:T(8,128)}, bf16[256,1024]{1,0:T(8,128)(2,1)}, f32[1,1024]{1,0:T(1,128)}, f32[1,1024]{1,0:T(1,128)}, bf16[1024,512]{1,0:T(8...) custom-call(f32[256,1024]{1,0:T(8,128)} %bitcast.110, ...), custom_call_target="tpu_custom_call" | custom-call | tf_op jit(solution)/shard_map/norm_backward/pallas_call | solution.py:143
  301.8 5.8 outer.14
  313.0 12.4 %ffn_backward.1 = (f32[256,1024]{1,0:T(8,128)}, bf16[256,4096]{1,0:T(8,128)(2,1)}, bf16[256,2048]{1,0:T(8,128)(2,1)}, bf16[256,2048]{1,0:T(8,128)(2,1)}, bf16[25...) custom-call(bf16[256,1024]{1,0:T(8,128)(2,1)} %get-tuple-element.161.dy_ref.branch_ref, ...), custom_call_target="tpu_custom_call" | custom-call | tf_op jit(solution)/shard_map/ffn_backward/pallas_call | solution.py:143
  328.0 5.0 outer.16
  342.1 3.5 all-to-all-start
  346.9 18.0 %attention_backward.1 = (f32[256,1024]{1,0:T(8,128)}, bf16[256,4096]{1,0:T(8,128)(2,1)}, f32[1,1024]{1,0:T(1,128)}, f32[1,1024]{1,0:T(1,128)}, bf16[256,2048]{1,...) custom-call(s32[18]{0:T(128)} %pad_add_fusion.info_ref, ...), custom_call_target="tpu_custom_call" | custom-call | tf_op jit(solution)/shard_map/attention_backward/pallas_call | solution.py:143
  365.0 5.1 outer.19
  372.5 7.9 %embed_backward.1 = (bf16[256,1024]{1,0:T(8,128)(2,1)}, f32[256,1024]{1,0:T(8,128)}, f32[1,1024]{1,0:T(1,128)}, f32[1,1024]{1,0:T(1,128)}) custom-call(f32[256,1024]{1,0:T(8,128)} %get-tuple-element.140.grad_ref, bf16[256,4096]{1,0:T(8,128)(2,1)} %get-tuple-element.171.dp_ref.dy_ref, f32[256,1024]{1,0:T(8,128)} %get-tuple-element.149.n_ref, ...), custom_call_target="tpu_custom_call" | custom-call | tf_op jit(solution)/shard_map/embed_backward/pallas_call | solution.py:143
  384.4 5.2 all-to-all-start.1
  395.2 5.0 outer.22
  403.8 5.0 outer.23
  412.8 6.1 %collective-permute-done.31.refs_2_ = bf16[256,4096]{1,0:T(8,128)(2,1)} collective-permute-done((bf16[256,4096]{1,0:T(8,128)(2,1)}, bf16[256,4096]{1,0:T(8,128)(2,1)}, u32[]{:S(2)}, u32[]{:S(2)}) %collective-permute-start.31) | collective-permute-done | bytes 2097184 | tf_op jit(solution)/shard_map/ppermute | solution.py:24
  419.0 5.5 outer.27
  424.5 5.2 all-to-all-start.2
  431.9 24.1 %collective-permute-done.18 = bf16[128,4096]{1,0:T(8,128)(2,1)S(1)} collective-permute-done((bf16[128,4096]{1,0:T(8,128)(2,1)S(1)}, bf16[128,4096]{1,0:T(8,128)(2,1)S(1)}, u32[]{:S(2)}, u32[]{:S(2)}) %collective-permute-start.18) | collective-permute-done | bytes 1048608 | tf_op jit(solution)/shard_map/ppermute | solution.py:24
  457.2 20.6 %all-to-all-done.2 = bf16[4,64,4096]{2,1,0:T(8,128)(2,1)} async-done(((bf16[4,64,4096]{2,1,0:T(8,128)(2,1)}), bf16[4,64,4096]{2,1,0:T(8,128)(2,1)}, u32[]{:S(2)}, u32[]{:S(2)}) %all-to-all-start.2) | async-done | bytes 2097184 | tf_op jit(solution)/shard_map/all_to_all | solution.py:31
  477.8 3.5 all-to-all-start.3
  485.8 13.6 %collective-permute-done.23.refs_2_ = bf16[256,4096]{1,0:T(8,128)(2,1)} collective-permute-done((bf16[256,4096]{1,0:T(8,128)(2,1)}, bf16[256,4096]{1,0:T(8,128)(2,1)}, u32[]{:S(2)}, u32[]{:S(2)}) %collective-permute-start.23) | collective-permute-done | bytes 2097184 | tf_op jit(solution)/shard_map/ppermute | solution.py:24
  499.4 5.4 outer.24
  507.5 3.6 all-to-all-start.4
  514.7 9.6 %collective-permute-done.28.refs_2_ = bf16[256,1024]{1,0:T(8,128)(2,1)S(1)} collective-permute-done((bf16[256,1024]{1,0:T(8,128)(2,1)}, bf16[256,1024]{1,0:T(8,128)(2,1)S(1)}, u32[]{:S(2)}, u32[]{:S(2)}) %collective-permute-start.28) | collective-permute-done | bytes 524320 | tf_op jit(solution)/shard_map/ppermute | solution.py:24
  539.7 19.0 %all-to-all-done.4 = bf16[4,64,4096]{2,1,0:T(8,128)(2,1)S(1)} async-done(((bf16[4,64,4096]{2,1,0:T(8,128)(2,1)}), bf16[4,64,4096]{2,1,0:T(8,128)(2,1)S(1)}, u32[]{:S(2)}, u32[]{:S(2)}) %all-to-all-start.4) | async-done | bytes 2097184 | tf_op jit(solution)/shard_map/all_to_all | solution.py:31
  564.2 12.0 %all-to-all-done.5 = bf16[4,64,1024]{2,1,0:T(8,128)(2,1)S(1)} async-done(((bf16[4,64,1024]{2,1,0:T(8,128)(2,1)}), bf16[4,64,1024]{2,1,0:T(8,128)(2,1)S(1)}, u32[]{:S(2)}, u32[]{:S(2)}) %all-to-all-start.5) | async-done | bytes 524320 | tf_op jit(solution)/shard_map/all_to_all | solution.py:31
  (277 shorter events, 117.1 us)
Async XLA Ops:
  7.2 148.3 %all-gather.4.cloned.1.call-start = ((), (), s32[]{:S(2)}) async-start(), calls=%async_computation.6 | async-start | bytes 28966912 | tf_op jit(solution)/shard_map/all_gather | solution.py:872
  14.2 218.4 %all-gather.6.cloned.1.call-start = ((), (), s32[]{:S(2)}) async-start(), calls=%async_computation.7 | async-start | bytes 8912896 | tf_op jit(solution)/shard_map/all_gather | solution.py:875
  187.5 16.8 %collective-permute-start = (bf16[256,1024]{1,0:T(8,128)(2,1)}, bf16[256,1024]{1,0:T(8,128)(2,1)S(1)}, u32[]{:S(2)}, u32[]{:S(2)}) collective-permute-start(bf16[256,1024]{1,0:T(8,128)(2,1)} %get-tuple-element.97), channel_id=1, source_target_pairs={{0,16},{1,17},{2,18},{3,19},{4,20},{5,21},{6,22},{7,23},{8,24},{9,... | collective-permute-start | bytes 1572872 | tf_op jit(solution)/shard_map/ppermute | solution.py:35
  191.0 11.9 %collective-permute-start.2 = (bf16[16,64]{1,0:T(8,128)(2,1)S(1)}, bf16[16,64]{1,0:T(8,128)(2,1)S(1)}, u32[]{:S(2)}, u32[]{:S(2)}) collective-permute-start(bf16[16,64]{1,0:T(8,128)(2,1)S(1)} %get-tuple-element.235), channel_id=1, source_target_pairs={{0,16},{1,17},{2,18},{3,19},{4,20},{5,21},{6,22},{7,23},{8,24},{9,... | collective-permute-start | bytes 6152 | tf_op jit(solution)/shard_map/ppermute | solution.py:35
  277.9 16.2 %collective-permute-start.3 = (bf16[256,1024]{1,0:T(8,128)(2,1)}, bf16[256,1024]{1,0:T(8,128)(2,1)S(1)}, u32[]{:S(2)}, u32[]{:S(2)}) collective-permute-start(bf16[256,1024]{1,0:T(8,128)(2,1)} %get-tuple-element.110), channel_id=1, source_target_pairs={{16,0},{17,1},{18,2},{19,3},{20,4},{21,5},{22,6},{23,7},{24,8},{25... | collective-permute-start | bytes 1572872 | tf_op jit(solution)/shard_map/ppermute | solution.py:39
  307.5 17.9 %collective-permute-start.5 = (bf16[256,2048]{1,0:T(8,128)(2,1)}, bf16[256,2048]{1,0:T(8,128)(2,1)S(1)}, u32[]{:S(2)}, u32[]{:S(2)}) collective-permute-start(bf16[256,2048]{1,0:T(8,128)(2,1)} %get-tuple-element.121), channel_id=1, source_target_pairs={{0,1},{1,0},{2,3},{3,2},{4,5},{5,4},{6,7},{7,6},{8,9},{9,8},{10,11... | collective-permute-start | bytes 3145736 | tf_op jit(solution)/shard_map/ppermute | solution.py:19
  308.0 18.3 %collective-permute-start.6 = (bf16[256,2048]{1,0:T(8,128)(2,1)}, bf16[256,2048]{1,0:T(8,128)(2,1)S(1)}, u32[]{:S(2)}, u32[]{:S(2)}) collective-permute-start(bf16[256,2048]{1,0:T(8,128)(2,1)} %get-tuple-element.122), channel_id=1, source_target_pairs={{0,1},{1,0},{2,3},{3,2},{4,5},{5,4},{6,7},{7,6},{8,9},{9,8},{10,11... | collective-permute-start | bytes 3145736 | tf_op jit(solution)/shard_map/ppermute | solution.py:19
  308.1 24.9 %collective-permute-start.7 = (bf16[1024,512]{1,0:T(8,128)(2,1)}, bf16[1024,512]{1,0:T(8,128)(2,1)}, u32[]{:S(2)}, u32[]{:S(2)}) collective-permute-start(bf16[1024,512]{1,0:T(8,128)(2,1)} %get-tuple-element.117), channel_id=1, source_target_pairs={{0,1},{1,0},{2,3},{3,2},{4,5},{5,4},{6,7},{7,6},{8,9},{9,8},{10,11... | collective-permute-start | bytes 3145736 | tf_op jit(solution)/shard_map/ppermute | solution.py:19
  312.4 25.3 %collective-permute-start.9 = (bf16[1024,512]{1,0:T(8,128)(2,1)}, bf16[1024,512]{1,0:T(8,128)(2,1)S(1)}, u32[]{:S(2)}, u32[]{:S(2)}) collective-permute-start(bf16[1024,512]{1,0:T(8,128)(2,1)} %outer.15), channel_id=1, source_target_pairs={{0,2},{1,3},{2,0},{3,1},{4,6},{5,7},{6,4},{7,5},{8,10},{9,11},{10,... | collective-permute-start | bytes 3145736 | tf_op jit(solution)/shard_map/ppermute | solution.py:24
  313.0 25.3 %collective-permute-start.8 = (bf16[1024,512]{1,0:T(8,128)(2,1)}, bf16[1024,512]{1,0:T(8,128)(2,1)}, u32[]{:S(2)}, u32[]{:S(2)}) collective-permute-start(bf16[1024,512]{1,0:T(8,128)(2,1)} %get-tuple-element.118), channel_id=1, source_target_pairs={{0,1},{1,0},{2,3},{3,2},{4,5},{5,4},{6,7},{7,6},{8,9},{9,8},{10,11... | collective-permute-start | bytes 3145736 | tf_op jit(solution)/shard_map/ppermute | solution.py:19
  325.4 20.2 %collective-permute-start.10 = (bf16[256,2048]{1,0:T(8,128)(2,1)}, bf16[256,2048]{1,0:T(8,128)(2,1)}, u32[]{:S(2)}, u32[]{:S(2)}) collective-permute-start(bf16[256,2048]{1,0:T(8,128)(2,1)} %get-tuple-element.129), channel_id=1, source_target_pairs={{0,1},{1,0},{2,3},{3,2},{4,5},{5,4},{6,7},{7,6},{8,9},{9,8},{10,11... | collective-permute-start | bytes 3145736 | tf_op jit(solution)/shard_map/ppermute | solution.py:19
  326.3 11.5 %collective-permute-start.12 = (bf16[2,16,32]{2,0,1:T(2,128)(2,1)S(1)}, bf16[2,16,32]{2,0,1:T(2,128)(2,1)S(1)}, u32[]{:S(2)}, u32[]{:S(2)}) collective-permute-start(bf16[2,16,32]{2,0,1:T(2,128)(2,1)S(1)} %fusion.70), channel_id=1, source_target_pairs={{16,0},{17,1},{18,2},{19,3},{20,4},{21,5},{22,6},{23,7},{24,8},{25... | collective-permute-start | bytes 6152 | tf_op jit(solution)/shard_map/ppermute | solution.py:39
  333.0 32.0 %collective-permute-start.11 = (bf16[256,2048]{1,0:T(8,128)(2,1)}, bf16[256,2048]{1,0:T(8,128)(2,1)}, u32[]{:S(2)}, u32[]{:S(2)}) collective-permute-start(bf16[256,2048]{1,0:T(8,128)(2,1)} %get-tuple-element.130), channel_id=1, source_target_pairs={{0,1},{1,0},{2,3},{3,2},{4,5},{5,4},{6,7},{7,6},{8,9},{9,8},{10,11... | collective-permute-start | bytes 3145736 | tf_op jit(solution)/shard_map/ppermute | solution.py:19
  337.7 32.4 %collective-permute-start.13 = (bf16[1024,512]{1,0:T(8,128)(2,1)}, bf16[1024,512]{1,0:T(8,128)(2,1)}, u32[]{:S(2)}, u32[]{:S(2)}) collective-permute-start(bf16[1024,512]{1,0:T(8,128)(2,1)} %get-tuple-element.119), channel_id=1, source_target_pairs={{0,1},{1,0},{2,3},{3,2},{4,5},{5,4},{6,7},{7,6},{8,9},{9,8},{10,11... | collective-permute-start | bytes 3145736 | tf_op jit(solution)/shard_map/ppermute | solution.py:19
  337.8 32.8 %collective-permute-start.15 = (bf16[256,2048]{1,0:T(8,128)(2,1)}, bf16[256,2048]{1,0:T(8,128)(2,1)}, u32[]{:S(2)}, u32[]{:S(2)}) collective-permute-start(bf16[256,2048]{1,0:T(8,128)(2,1)} %get-tuple-element.123), channel_id=1, source_target_pairs={{0,1},{1,0},{2,3},{3,2},{4,5},{5,4},{6,7},{7,6},{8,9},{9,8},{10,11... | collective-permute-start | bytes 3145736 | tf_op jit(solution)/shard_map/ppermute | solution.py:19
  338.3 32.4 %collective-permute-start.14 = (bf16[1024,512]{1,0:T(8,128)(2,1)}, bf16[1024,512]{1,0:T(8,128)(2,1)}, u32[]{:S(2)}, u32[]{:S(2)}) collective-permute-start(bf16[1024,512]{1,0:T(8,128)(2,1)} %outer.17), channel_id=1, source_target_pairs={{0,2},{1,3},{2,0},{3,1},{4,6},{5,7},{6,4},{7,5},{8,10},{9,11},{10,... | collective-permute-start | bytes 3145736 | tf_op jit(solution)/shard_map/ppermute | solution.py:24
  342.1 42.3 %all-to-all-start = ((bf16[4,256,512]{2,1,0:T(8,128)(2,1)}), bf16[4,256,512]{2,1,0:T(8,128)(2,1)S(1)}, u32[]{:S(2)}, u32[]{:S(2)}) async-start(bf16[4,256,512]{2,1,0:T(8,128)(2,1)} %bitcast.112), calls=%async_computation | async-start | bytes 2097152 | tf_op jit(solution)/shard_map/all_to_all | solution.py:31
  345.6 54.6 %collective-permute-start.17 = (bf16[256,4096]{1,0:T(8,128)(2,1)}, bf16[256,4096]{1,0:T(8,128)(2,1)S(1)}, u32[]{:S(2)}, u32[]{:S(2)}) collective-permute-start(bf16[256,4096]{1,0:T(8,128)(2,1)} %outer.16), channel_id=1, source_target_pairs={{16,0},{17,1},{18,2},{19,3},{20,4},{21,5},{22,6},{23,7},{24,8},{25... | collective-permute-start | bytes 6291464 | tf_op jit(solution)/shard_map/ppermute | solution.py:39
  365.0 30.1 %collective-permute-start.16 = (bf16[256,2048]{1,0:T(8,128)(2,1)}, bf16[256,2048]{1,0:T(8,128)(2,1)}, u32[]{:S(2)}, u32[]{:S(2)}) collective-permute-start(bf16[256,2048]{1,0:T(8,128)(2,1)} %get-tuple-element.124), channel_id=1, source_target_pairs={{0,1},{1,0},{2,3},{3,2},{4,5},{5,4},{6,7},{7,6},{8,9},{9,8},{10,11... | collective-permute-start | bytes 3145736 | tf_op jit(solution)/shard_map/ppermute | solution.py:19
  370.1 30.6 %collective-permute-start.21 = (bf16[256,2048]{1,0:T(8,128)(2,1)}, bf16[256,2048]{1,0:T(8,128)(2,1)}, u32[]{:S(2)}, u32[]{:S(2)}) collective-permute-start(bf16[256,2048]{1,0:T(8,128)(2,1)} %get-tuple-element.143), channel_id=1, source_target_pairs={{0,1},{1,0},{2,3},{3,2},{4,5},{5,4},{6,7},{7,6},{8,9},{9,8},{10,11... | collective-permute-start | bytes 3145736 | tf_op jit(solution)/shard_map/ppermute | solution.py:19
  370.6 30.2 %collective-permute-start.22 = (bf16[256,2048]{1,0:T(8,128)(2,1)}, bf16[256,2048]{1,0:T(8,128)(2,1)}, u32[]{:S(2)}, u32[]{:S(2)}) collective-permute-start(bf16[256,2048]{1,0:T(8,128)(2,1)} %get-tuple-element.144), channel_id=1, source_target_pairs={{0,1},{1,0},{2,3},{3,2},{4,5},{5,4},{6,7},{7,6},{8,9},{9,8},{10,11... | collective-permute-start | bytes 3145736 | tf_op jit(solution)/shard_map/ppermute | solution.py:19
  370.7 48.3 %collective-permute-start.31 = (bf16[256,4096]{1,0:T(8,128)(2,1)}, bf16[256,4096]{1,0:T(8,128)(2,1)}, u32[]{:S(2)}, u32[]{:S(2)}) collective-permute-start(bf16[256,4096]{1,0:T(8,128)(2,1)} %outer.19), channel_id=1, source_target_pairs={{0,2},{1,3},{2,0},{3,1},{4,6},{5,7},{6,4},{7,5},{8,10},{9,11},{10,... | collective-permute-start | bytes 6291464 | tf_op jit(solution)/shard_map/ppermute | solution.py:24
  384.4 40.1 %all-to-all-start.1 = ((bf16[4,256,512]{2,1,0:T(8,128)(2,1)}), bf16[4,256,512]{2,1,0:T(8,128)(2,1)}, u32[]{:S(2)}, u32[]{:S(2)}) async-start(bf16[4,256,512]{2,1,0:T(8,128)(2,1)} %bitcast.111), calls=%async_computation.1 | async-start | bytes 2097152 | tf_op jit(solution)/shard_map/all_to_all | solution.py:31
  395.1 17.7 %collective-permute-start.29 = (bf16[256,2048]{1,0:T(8,128)(2,1)}, bf16[256,2048]{1,0:T(8,128)(2,1)S(1)}, u32[]{:S(2)}, u32[]{:S(2)}) collective-permute-start(bf16[256,2048]{1,0:T(8,128)(2,1)} %get-tuple-element.131), channel_id=1, source_target_pairs={{0,1},{1,0},{2,3},{3,2},{4,5},{5,4},{6,7},{7,6},{8,9},{9,8},{10,11... | collective-permute-start | bytes 3145736 | tf_op jit(solution)/shard_map/ppermute | solution.py:19
  400.2 12.6 %collective-permute-start.30 = (bf16[256,2048]{1,0:T(8,128)(2,1)}, bf16[256,2048]{1,0:T(8,128)(2,1)S(1)}, u32[]{:S(2)}, u32[]{:S(2)}) collective-permute-start(bf16[256,2048]{1,0:T(8,128)(2,1)} %get-tuple-element.132), channel_id=1, source_target_pairs={{0,1},{1,0},{2,3},{3,2},{4,5},{5,4},{6,7},{7,6},{8,9},{9,8},{10,11... | collective-permute-start | bytes 3145736 | tf_op jit(solution)/shard_map/ppermute | solution.py:19
  424.5 53.3 %all-to-all-start.2 = ((bf16[4,64,4096]{2,1,0:T(8,128)(2,1)}), bf16[4,64,4096]{2,1,0:T(8,128)(2,1)}, u32[]{:S(2)}, u32[]{:S(2)}) async-start(bf16[4,64,4096]{2,1,0:T(8,128)(2,1)} %bitcast.107), calls=%async_computation.2 | async-start | bytes 4194304 | tf_op jit(solution)/shard_map/all_to_all | solution.py:31
  429.8 26.2 %collective-permute-start.18 = (bf16[128,4096]{1,0:T(8,128)(2,1)S(1)}, bf16[128,4096]{1,0:T(8,128)(2,1)S(1)}, u32[]{:S(2)}, u32[]{:S(2)}) collective-permute-start(bf16[128,4096]{1,0:T(8,128)(2,1)S(1)} %slice.212), channel_id=1, source_target_pairs={{0,2},{1,3},{2,0},{3,1},{4,6},{5,7},{6,4},{7,5},{8,10},{9,11},{10,... | collective-permute-start | bytes 3145736 | tf_op jit(solution)/shard_map/ppermute | solution.py:24
  431.4 68.0 %collective-permute-start.23 = (bf16[256,4096]{1,0:T(8,128)(2,1)}, bf16[256,4096]{1,0:T(8,128)(2,1)}, u32[]{:S(2)}, u32[]{:S(2)}) collective-permute-start(bf16[256,4096]{1,0:T(8,128)(2,1)} %outer.23), channel_id=1, source_target_pairs={{0,2},{1,3},{2,0},{3,1},{4,6},{5,7},{6,4},{7,5},{8,10},{9,11},{10,... | collective-permute-start | bytes 6291464 | tf_op jit(solution)/shard_map/ppermute | solution.py:24
  477.8 28.7 %all-to-all-start.3 = ((bf16[4,32,4096]{2,1,0:T(8,128)(2,1)}), bf16[4,32,4096]{2,1,0:T(8,128)(2,1)S(1)}, u32[]{:S(2)}, u32[]{:S(2)}) async-start(bf16[4,32,4096]{2,1,0:T(8,128)(2,1)} %bitcast.39), calls=%async_computation.3 | async-start | bytes 2097152 | tf_op jit(solution)/shard_map/all_to_all | solution.py:31
  507.5 51.3 %all-to-all-start.4 = ((bf16[4,64,4096]{2,1,0:T(8,128)(2,1)}), bf16[4,64,4096]{2,1,0:T(8,128)(2,1)S(1)}, u32[]{:S(2)}, u32[]{:S(2)}) async-start(bf16[4,64,4096]{2,1,0:T(8,128)(2,1)} %bitcast.108), calls=%async_computation.4 | async-start | bytes 4194304 | tf_op jit(solution)/shard_map/all_to_all | solution.py:31
  511.1 13.2 %collective-permute-start.28 = (bf16[256,1024]{1,0:T(8,128)(2,1)}, bf16[256,1024]{1,0:T(8,128)(2,1)S(1)}, u32[]{:S(2)}, u32[]{:S(2)}) collective-permute-start(bf16[256,1024]{1,0:T(8,128)(2,1)} %outer.25), channel_id=1, source_target_pairs={{0,2},{1,3},{2,0},{3,1},{4,6},{5,7},{6,4},{7,5},{8,10},{9,11},{10,... | collective-permute-start | bytes 1572872 | tf_op jit(solution)/shard_map/ppermute | solution.py:24
  558.8 17.4 %all-to-all-start.5 = ((bf16[4,64,1024]{2,1,0:T(8,128)(2,1)}), bf16[4,64,1024]{2,1,0:T(8,128)(2,1)S(1)}, u32[]{:S(2)}, u32[]{:S(2)}) async-start(bf16[4,64,1024]{2,1,0:T(8,128)(2,1)} %bitcast.41), calls=%async_computation.5 | async-start | bytes 1048576 | tf_op jit(solution)/shard_map/all_to_all | solution.py:31
  (50 other events, 626.4 us)
Sparse Core Ops, SparseCore 0:
  14.3 141.1 all-gather.3
  157.7 74.9 all-gather.5

commit v3 on v2

--- a/solution.py
+++ b/solution.py
@@ -29,6 +29,20 @@
     groups = [list(range(at, n, 4)) for at in range(4)]
     x = x.reshape(n // 4, -1, x.shape[1])
     return lax.all_to_all(x, "dp", 0, 0, axis_index_groups=groups)
+
+
+def shift_outer(x):
+    n = lax.axis_size("dp")
+    return lax.ppermute(x, "dp", [(i, (i + 4) % n) for i in range(n)])
+
+
+def gather_by_steps(x):
+    pieces = [x]
+    for _ in range(lax.axis_size("dp") // 4 - 1):
+        pieces.append(shift_outer(pieces[-1]))
+    own = jnp.stack(pieces)
+    pair = swap_pair(own)
+    return jnp.stack([own, pair], axis=1), jnp.stack([to_decoder(own), to_decoder(pair)], axis=1)
 
 
 def to_decoder(x):
@@ -182,36 +196,44 @@
     return jnp.where(low_half, x, zero), jnp.where(low_half, zero, x)
 
 
-def joined(a, b):
-    return jnp.where(lax.broadcasted_iota(jnp.int32, a.shape, 1) < HEAD_DIM, a, b)
+def joined(x):
+    rows = x.shape[0] // 2
+    low_half = lax.broadcasted_iota(jnp.int32, (rows, x.shape[1]), 1) < HEAD_DIM
+    return jnp.where(low_half, x[:rows], x[rows:])
+
+
+def stacked_heads(x):
+    return jnp.concatenate(halves(x), axis=0)
 
 
 def softmax_t(scores, mask):
-    logits = jnp.where(mask, scores, NEG_FILL)
-    e = jnp.exp(logits - jnp.max(logits, axis=0, keepdims=True))
-    return e * (1.0 / jnp.sum(e, axis=0, keepdims=True))
+    logits = jnp.where(mask[None], scores, NEG_FILL)
+    e = jnp.exp(logits - jnp.max(logits, axis=1, keepdims=True))
+    return e * (1.0 / jnp.sum(e, axis=1, keepdims=True))
 
 
 FACTOR = HEAD_DIM ** (-0.5)
 
 
+def probabilities(q, k_stack, mask):
+    scores = dot_nt(k_stack, q * jnp.asarray(FACTOR, BF))
+    return softmax_t(scores.reshape((2,) + mask.shape), mask)
+
+
 def attend_lanes(q, k, v, mask):
-    scaled = q * jnp.asarray(FACTOR, BF)
-    scores = [dot_nt(k, part) for part in halves(scaled)]
-    probs = [softmax_t(s, mask).astype(BF) for s in scores]
-    return joined(*[dot_tn(p, v) for p in probs]).astype(BF)
+    probs = probabilities(q, stacked_heads(k), mask).astype(BF)
+    return dot_tn(probs.reshape(2 * SEQ, SEQ), stacked_heads(v)).astype(BF)
 
 
 def attend_back_lanes(g, q, k, v, mask):
-    scaled = q * jnp.asarray(FACTOR, BF)
-    grads = []
-    for q_part, g_part in zip(halves(scaled), halves(g)):
-        probs = softmax_t(dot_nt(k, q_part), mask)
-        d_probs = dot_nt(v, g_part)
-        centred = jnp.sum(probs * d_probs, axis=0, keepdims=True)
-        d_s = (probs * (d_probs - centred) * FACTOR).astype(BF)
-        grads.append((dot_tn(d_s, k), dot(d_s, q), dot(probs.astype(BF), g)))
-    return [joined(a, b).astype(BF) for a, b in zip(*grads)]
+    k_stack = stacked_heads(k)
+    probs = probabilities(q, k_stack, mask)
+    d_probs = dot_nt(stacked_heads(v), g).reshape(probs.shape)
+    centred = jnp.sum(probs * d_probs, axis=1, keepdims=True)
+    d_s = (probs * (d_probs - centred) * FACTOR).astype(BF).reshape(2 * SEQ, SEQ)
+    d_v = joined(dot(probs.astype(BF).reshape(2 * SEQ, SEQ), g))
+    d_k = joined(dot(d_s, q))
+    return [part.astype(BF) for part in (dot_tn(d_s, k_stack), d_k, d_v)]
 
 
 def lanes_of(i, offset=0):
@@ -232,7 +254,7 @@
             )
         return carry
 
-    lax.fori_loop(0, width // 128, step, 0)
+    lax.fori_loop(0, width // 128, step, 0, unroll=4)
 
 
 def attend_back_all(g_ref, q_ref, q_at, kv_ref, k_at, v_at, mask_ref, out_ref, width):
@@ -252,7 +274,7 @@
                 out_ref[s, lanes_of(i, at * width)] = part
         return carry
 
-    lax.fori_loop(0, width // 128, step, 0)
+    lax.fori_loop(0, width // 128, step, 0, unroll=4)
 
 
 def norm_values(values, gain, bias):
@@ -390,72 +412,96 @@
     )
 
 
+def arrivals(me, m):
+    z, x, core = me // 4, lax.rem(me // 2, 2), lax.rem(me, 2)
+    for h in range(2):
+        for k in range(m):
+            for xrel in range(2):
+                outer_pair = lax.rem(z - k + m, m) * 4 + lax.rem(x + xrel, 2) * 2
+                yield h, k, xrel, outer_pair + lax.rem(core + h, 2)
+
+
 class Cross:
-    def __init__(self, weights):
-        self.n, rows, self.width = weights.shape
-        self.c = rows // 8
+    def __init__(self, far, own, me):
+        m, _, _, self.c, self.width = own.shape
+        self.m, self.n = m, 4 * m
+        self.arrays = (far, swap_core(far), own, swap_core(own))
         if self.c % 16:
-            both = weights.reshape(self.n, 2, 4, self.c, self.width).transpose(2, 1, 0, 3, 4)
-            weights = both.reshape(4, 2 * self.n * self.c, self.width)
-        self.weights = weights
+            index = jnp.stack([j for *_, j in arrivals(me, self.m)])
+            back = jnp.sum((index[:, None] == jnp.arange(self.n)) * jnp.arange(self.n)[:, None], axis=0)
+            sections = []
+            for one, other in (self.arrays[:2], self.arrays[2:]):
+                both = jnp.stack([one, other]).reshape(self.n, 4, self.c, self.width)
+                sections.append(both[back])
+            self.arrays = (jnp.stack(sections).transpose(2, 0, 1, 3, 4),)
+
+    @property
+    def specs(self):
+        return [ANY_SPEC] * len(self.arrays)
 
     @property
     def scratch(self):
-        return pltpu.VMEM((4, 2, self.n, self.c, self.width), BF)
-
-    def start(self, ref, dst, sems, groups):
-        copies = {}
-        for i in groups:
-            copies[i] = []
-            for s in range(2):
-                if self.c % 16:
-                    count = self.n * self.c
-                    src = ref.at[i, pl.ds(s * count, count)].reshape(self.n, self.c, self.width)
-                else:
-                    src = ref.at[:, pl.ds((4 * s + i) * self.c, self.c)]
-                copies[i].append(pltpu.make_async_copy(src, dst.at[i, s], sems.at[i, s]))
-                copies[i][-1].start()
+        return [pltpu.VMEM((4, 2, self.n, self.c, self.width), BF), pltpu.SemaphoreType.DMA((2, 2, self.n))]
+
+    def start(self, refs, dst, sems, me, first, count):
+        groups = pl.ds(first, count)
+        if len(refs) == 1:
+            copies = [pltpu.make_async_copy(refs[0].at[groups], dst.at[groups], sems.at[0, 0])]
+        else:
+            copies = [
+                pltpu.make_async_copy(
+                    refs[2 * s + h].at[k, xrel, groups], dst.at[groups, s, j], sems.at[s, i]
+                )
+                for i, (h, k, xrel, j) in enumerate(arrivals(me, self.m))
+                for s in range(2)
+            ]
+        for copy in copies:
+            copy.start()
         return copies
 
     def matrix(self, ref, i):
         return ref[i].reshape(2 * self.n * self.c, self.width)
 
 
-def cross_query(low, cross):
+def cross_query(info, low, cross):
     t, width = low.shape
-
-    def kernel(low_ref, w_hbm, out_ref, w, sems):
-        for copy in cross.start(w_hbm, w, sems, (0,))[0]:
+    count = len(cross.arrays)
+
+    def kernel(info_ref, low_ref, *refs):
+        out_ref, w, sems = refs[count:]
+        for copy in cross.start(refs[:count], w, sems.at[0], info_ref[0], 0, 1):
             copy.wait()
         out_ref[...] = dot(low_ref[...], cross.matrix(w, 0)).astype(BF)
 
     return kernel_call(
         kernel,
         shape_of(t, width, BF),
-        (low, cross.weights),
-        [VMEM_SPEC, ANY_SPEC],
+        (info, low, *cross.arrays),
+        [SMEM_SPEC, VMEM_SPEC] + cross.specs,
         VMEM_SPEC,
         "cross_query",
-        scratch=[cross.scratch, pltpu.SemaphoreType.DMA((4, 2))],
-    )
-
-
-def cross_query_back(resid, d_cross, cross):
+        scratch=cross.scratch,
+    )
+
+
+def cross_query_back(info, resid, d_cross, cross):
     t, width = resid.shape
-
-    def kernel(resid_ref, d_ref, w_hbm, out_ref, w, sems):
-        for copy in cross.start(w_hbm, w, sems, (0,))[0]:
+    count = len(cross.arrays)
+
+    def kernel(info_ref, resid_ref, d_ref, *refs):
+        out_ref, w, sems = refs[count:]
+        for copy in cross.start(refs[:count], w, sems.at[0], info_ref[0], 0, 1):
             copy.wait()
         out_ref[...] = resid_ref[...] + dot_nt(d_ref[:, :width], cross.matrix(w, 0))
 
     return kernel_call(
         kernel,
         shape_of(t, width),
-        (resid, d_cross, cross.weights),
-        [VMEM_SPEC, VMEM_SPEC, ANY_SPEC],
+        (info, resid, d_cross, *cross.arrays),
+        [SMEM_SPEC, VMEM_SPEC, VMEM_SPEC] + cross.specs,
         VMEM_SPEC,
         "cross_query_back",
-        scratch=[cross.scratch, pltpu.SemaphoreType.DMA((4, 2))],
+        scratch=cross.scratch,
     )
 
 
@@ -465,28 +511,31 @@
     inner_width = ups * width
     block = inner_width // n
     ordered = block % 128 == 0
+    count = len(cross.arrays)
     per = n // ups
 
-    def kernel(info_ref, memory_ref, q_ref, mask_ref, cg_ref, cb_ref, g_ref, b_ref, second_hbm, cot_hbm, w_hbm, c_hbm, *refs):
+    def kernel(info_ref, memory_ref, q_ref, mask_ref, cg_ref, cb_ref, g_ref, b_ref, second_hbm, cot_hbm, w_hbm, *refs):
+        c_refs, refs = refs[:count], refs[count:]
         out_hbm, normed_hbm, inv_ref, third_hbm, active_hbm, slope_hbm = refs[:6]
         mix_ref, d_qkv_ref, d_memory_ref, resid_ref, dg_ref, db_ref = refs[6:12]
-        w_c, w_up, w_down, kv, third, low, active, slope, out, normed, c_normed, total, cot = refs[12:25]
-        d_branch_ref, cross_sems, sems, act_sems = refs[25:]
+        w_c, cross_sems, w_up, w_down, kv, third, low, active, slope, out, normed, c_normed, total, cot = refs[12:26]
+        d_branch_ref, sems, act_sems = refs[26:]
         is_dec = info_ref[1] == 1
-        copies = cross.start(c_hbm, w_c, cross_sems, (1, 2, 3))
+        copies = cross.start(c_refs, w_c, cross_sems.at[0], info_ref[0], 1, 2)
         get_second = pltpu.make_async_copy(second_hbm, third, sems.at[0])
         get_cot = pltpu.make_async_copy(cot_hbm, cot, sems.at[1])
         get_second.start()
+        last_copies = cross.start(c_refs, w_c, cross_sems.at[1], info_ref[0], 3, 1)
         up_copies = [fetch(w_hbm, rows_of.up + i * d, d, w_up.at[i], sems.at[8 + i]) for i in range(ups)]
         down_copy = fetch(w_hbm, rows_of.down, rows_of.down_rows, w_down, sems.at[7])
         get_cot.start()
+        for copy in copies:
+            copy.wait()
         for i in (1, 2):
-            for copy in copies[i]:
-                copy.wait()
             kv[:, (i - 1) * width : i * width] = dot(memory_ref[...], cross.matrix(w_c, i)).astype(BF)
         attend_all(q_ref, 0, kv, 0, width, mask_ref, mix_ref, width)
         get_second.wait()
-        for copy in copies[3]:
+        for copy in last_copies:
             copy.wait()
         values = third[...] + dot(mix_ref[...], cross.matrix(w_c, 3))
         third_c, normed_c, inverse_c = norm_values(values, cg_ref[...], cb_ref[...])
@@ -570,12 +619,12 @@
         (value, value, shape_of(t, 1), low)
         + (shape_of(t, inner_width, BF) if ordered else blocked, blocked)
         + (low, shape_of(t, 4 * width, BF), low, value, vector, vector),
-        (info, memory, cross_q, mask, c_gain, c_bias, gain, bias, second, cot, weights, cross.weights),
-        [SMEM_SPEC] + [VMEM_SPEC] * 7 + [ANY_SPEC] * 4,
+        (info, memory, cross_q, mask, c_gain, c_bias, gain, bias, second, cot, weights, *cross.arrays),
+        [SMEM_SPEC] + [VMEM_SPEC] * 7 + [ANY_SPEC] * 3 + cross.specs,
         (ANY_SPEC, ANY_SPEC, VMEM_SPEC, ANY_SPEC, ANY_SPEC, ANY_SPEC) + (VMEM_SPEC,) * 6,
         "decoder_middle",
-        scratch=[
-            cross.scratch,
+        scratch=cross.scratch
+        + [
             big(ups, n, d, width),
             big(n, rows_of.down_rows, width),
             big(t, 2 * width),
@@ -587,7 +636,6 @@
         + [pltpu.VMEM((t, width), F32)] * 5
         + [
             big(t, width),
-            pltpu.SemaphoreType.DMA((4, 2)),
             pltpu.SemaphoreType.DMA((8 + ups,)),
             pltpu.SemaphoreType.DMA((n,)),
         ],
@@ -867,12 +915,12 @@
     def columns_of(w):
         return [w[:, i * width : (i + 1) * width] for i in range(w.shape[1] // width)]
 
-    pack = [in_proj[0], jnp.pad(params[None], ((0, d_loc - in_loc - 1), (0, width - n_par)))]
+    pack = [in_proj[0], jnp.zeros((d_loc - in_loc, width), F32)]
     pack += columns_of(attn_in[0]) + [attn_out[0]] + columns_of(ffn_in[0]) + [ffn_out[0]]
     weights = lax.all_gather(jnp.concatenate(pack, axis=0).astype(BF), "dp", axis=0)
-    own_cross = jnp.concatenate(columns_of(cross_in) + [cross_out], axis=0).astype(BF)
-    cross_pack = jnp.concatenate([to_decoder(own_cross), own_cross], axis=0)
-    cross_w = Cross(lax.all_gather(after(cross_pack, weights), "dp", axis=0))
+    own_cross = jnp.stack(columns_of(cross_in) + [cross_out]).astype(BF)
+    own_cross, far_cross = gather_by_steps(own_cross)
+    cross_w = Cross(far_cross, own_cross, me)
 
     tokens = section_in[0]
     tokens = tokens.reshape(tokens.shape[0], n, in_loc)
@@ -891,24 +939,33 @@
     marks = (jnp.arange(depth)[None, :] == (jnp.arange(n) * d_loc + in_loc)[:, None]).astype(BF)
     tokens_rel = reordered(jnp.concatenate([tokens, marks], axis=0), perm_d)
 
-    pars = weights[:, in_loc, :n_par].astype(F32)
+    own_pars, far_pars = gather_by_steps(params.astype(BF)[None])
+    pars = jnp.stack([far_pars, own_pars]).reshape(2, n // 2, n_par)
+    pars = jnp.concatenate([pars, swap_core(pars)], axis=1)
+    index = jnp.stack([j for *_, j in arrivals(me, m)])
+    place = (jnp.arange(n)[:, None] == index[None, :]).astype(BF)
+    pars = jnp.stack([dot(place, pars[0]), dot(place, pars[1])])
 
     def vectors(at):
-        part = pars[:, 3 * at * d_loc : 3 * (at + 1) * d_loc].reshape(n, 3, d_loc)
+        part = pars[1, :, 3 * at * d_loc : 3 * (at + 1) * d_loc].reshape(n, 3, d_loc)
         part = part.transpose(1, 0, 2).reshape(3, 1, width)
         return [part[i] for i in range(3)]
 
     gains, biases = vectors(0), vectors(1)
-    own_cpar = pars[:, 6 * d_loc :].astype(BF)
-    cpar = jnp.stack([to_decoder(own_cpar), own_cpar]).astype(F32)
+    cpar = pars[:, :, 6 * d_loc :]
     c_gain = cpar[:, :, :c_loc].reshape(1, width)
     c_bias = cpar[:, :, c_loc:].reshape(1, width)
 
     xa, ia, first_low, packed, blended, second, xb, ib, second_low, encoded = front(
-        tokens, self_mask, weights, rows_of, gains, biases
+        after(tokens, *cross_w.arrays, c_gain, c_bias, perm_d, perm_cross),
+        self_mask,
+        weights,
+        rows_of,
+        gains,
+        biases,
     )
     memory = to_decoder(encoded)
-    cross_q = cross_query(second_low, cross_w)
+    cross_q = cross_query(info, second_low, cross_w)
     attn_rel = jnp.stack([reordered(first_low, perm_d), reordered(blended, perm_d)])
     second_rel = reordered(second_low, perm_cross)
     cross_q = after(cross_q, attn_rel, second_rel, tokens_rel)
@@ -931,7 +988,7 @@
         )
     )
     grad_memory = to_encoder(d_memory)
-    grad_second_dec = cross_query_back(resid, d_cross, cross_w)
+    grad_second_dec = cross_query_back(info, resid, d_cross, cross_w)
     third_rel = reordered(third_low, perm_d)
     if active_rel.ndim == 3:
         blocks = active_rel.transpose(1, 0, 2).reshape(tokens.shape[0], n, inner_width // n)
@@ -966,6 +1023,7 @@
     down1.pair(down0.pair_got)
     down0.add()
     down0.spread()
+    up.pair()
     grad_b, d_attn, dg_b, db_b, *sent = attention_backward(
         info,
         grad_second_dec,
@@ -982,13 +1040,12 @@
     )
     chain.mark(*sent)
     attn = Part(chain, attn_rel, d_attn, [swap_core(piece) for piece in sent], (0, 0, 0, 1))
-    up.pair()
+    down1.add()
+    down1.spread(down0.blocks)
     d_embed, d_tokens, dg_a, db_a = embed_backward(
         grad_b, chain(d_attn), xa, ia, gains[0], weights, rows_of
     )
     chain.mark(d_embed)
-    down1.add()
-    down1.spread(down0.blocks)
     cvec = jnp.where(is_dec, cvec[:, 1], cvec_got).transpose(1, 0, 2)
     vecs = jnp.concatenate([dg_a, dg_b, dg_d, db_a, db_b, db_d]).astype(BF)
     vecs = vecs.reshape(6, n, d_loc).transpose(1, 0, 2).reshape(n, 6 * d_loc)

time: 594 us -> 559 us (0.941)
  waiting for transfers between devices: 286 us -> 234 us
  starting transfers between devices: 50.1 us -> 66.6 us
  Pallas kernels: 174 us -> 159 us
  local copies, waits for them, and re-layouts: 29.9 us -> 36.2 us
    all_gather x1, waiting for transfers between devices: 131 us -> 10.7 us  [shards(): lax.all_gather(jnp.concatenate(pack, axis=0).astype(BF), 'dp', axis=0)]
    ppermute x0 -> x6, waiting for transfers between devices: none -> 50.4 us  [shift_outer(): return lax.ppermute(x, 'dp', [(i, (i + 4) % n) for i in range(n)])]
    ppermute x6 -> x8, waiting for transfers between devices: 55.2 us -> 94.6 us  [swap_pair(): return lax.ppermute(x, 'dp', [(i, i ^ 2) for i in range(n)])]
    all_gather x1 -> x0, waiting for transfers between devices: 27.5 us -> none  [shards(): cross_w = Cross(lax.all_gather(after(cross_pack, weights), 'dp', axis=0))]
    pallas_call x8, Pallas kernels: 117 us -> 102 us  [kernel_call(): pl.pallas_call(body, in_specs=specs, out_specs=out_specs, out_shape=out_s...]
    ppermute x3 -> x5, starting transfers between devices: 9.8 us -> 18.7 us  [to_decoder(): return lax.ppermute(x, 'section', [(0, 1)])]
    ppermute x3 -> x5, waiting for transfers between devices: 11.2 us -> 18.2 us  [to_decoder(): return lax.ppermute(x, 'section', [(0, 1)])]
  transfers between devices with their start and end apart: 40 -> 52, of which waited for: 17 -> 24; matrix products, arithmetic and copies ran while one was open for 8% -> 10% of each run, Pallas kernels for 21% -> 18%
where the time goes in v3:
time: 559 us; the launch traced here: 548 us
  waiting for transfers between devices  234 us (42%)
  Pallas kernels  159 us (28%)
  starting transfers between devices  66.6 us (12%)
  local copies, waits for them, and re-layouts  36.2 us (6%)
  other arithmetic  27.2 us (5%)
  between operations  15.5 us (3%)
  matrix products  10 us (2%)
    pallas_call x8, Pallas kernels, kernel_call(): pl.pallas_call(body, in_specs=specs, out_specs=out_specs, out_shape=out_s...  102 us
    ppermute x8, waiting for transfers between devices, swap_pair(): return lax.ppermute(x, 'dp', [(i, i ^ 2) for i in range(n)])  94.6 us
    pallas_call x14, Pallas kernels, outer(): pl.pallas_call(kernel, grid=(grid,), in_specs=specs, out_specs=out_specs,...  57.4 us
    all_to_all x6, waiting for transfers between devices, spread_outer(): return lax.all_to_all(x, 'dp', 0, 0, axis_index_groups=groups)  53.4 us
    ppermute x6, waiting for transfers between devices, shift_outer(): return lax.ppermute(x, 'dp', [(i, (i + 4) % n) for i in range(n)])  50.4 us
    all_to_all x6, starting transfers between devices, spread_outer(): return lax.all_to_all(x, 'dp', 0, 0, axis_index_groups=groups)  25.6 us
    ppermute x5, starting transfers between devices, to_decoder(): return lax.ppermute(x, 'section', [(0, 1)])  18.7 us
    ppermute x5, waiting for transfers between devices, to_decoder(): return lax.ppermute(x, 'section', [(0, 1)])  18.2 us
  transfers between devices with their start and end apart: 52, of which 24 were waited for; matrix products, arithmetic and copies ran while one was open for 10% of the time, Pallas kernels for 18%

profile of v3, /device:TPU:0, one launch (start us, length us, event | category | flops | bytes accessed | tf_op | source)
XLA Modules:
  0.0 548.5 jit_solution(131921897082414843)
XLA Ops:
  14.5 8.3 %collective-permute-done = bf16[4,32,1024]{2,1,0:T(8,128)(2,1)S(1)} collective-permute-done((bf16[4,32,1024]{2,1,0:T(8,128)(2,1)S(1)}, bf16[4,32,1024]{2,1,0:T(8,128)(2,1)S(1)}, u32[]{:S(2)}, u32[]{:S(2)}) %collective-permute-start) | collective-permute-done | bytes 262176 | tf_op jit(solution)/shard_map/ppermute | solution.py:36
  22.9 16.0 %collective-permute-done.1 = bf16[4,32,1024]{2,1,0:T(8,128)(2,1)S(1)} collective-permute-done((bf16[4,32,1024]{2,1,0:T(8,128)(2,1)S(1)}, bf16[4,32,1024]{2,1,0:T(8,128)(2,1)S(1)}, u32[]{:S(2)}, u32[]{:S(2)}) %collective-permute-start.1) | collective-permute-done | bytes 262176 | tf_op jit(solution)/shard_map/ppermute | solution.py:36
  39.0 15.5 %collective-permute-done.2 = bf16[4,32,1024]{2,1,0:T(8,128)(2,1)S(1)} collective-permute-done((bf16[4,32,1024]{2,1,0:T(8,128)(2,1)S(1)}, bf16[4,32,1024]{2,1,0:T(8,128)(2,1)S(1)}, u32[]{:S(2)}, u32[]{:S(2)}) %collective-permute-start.2) | collective-permute-done | bytes 262176 | tf_op jit(solution)/shard_map/ppermute | solution.py:36
  61.6 41.7 %collective-permute-done.4 = bf16[4,4,32,1024]{3,2,1,0:T(8,128)(2,1)} collective-permute-done((bf16[4,4,32,1024]{3,2,1,0:T(8,128)(2,1)}, bf16[4,4,32,1024]{3,2,1,0:T(8,128)(2,1)}, u32[]{:S(2)}, u32[]{:S(2)}) %collective-permute-start.4) | collective-permute-done | bytes 1048608 | tf_op jit(solution)/shard_map/ppermute | solution.py:24
  112.5 13.2 %collective-permute-done.5 = bf16[4,4,32,1024]{3,2,1,0:T(8,128)(2,1)} collective-permute-done((bf16[4,4,32,1024]{3,2,1,0:T(8,128)(2,1)}, bf16[4,4,32,1024]{3,2,1,0:T(8,128)(2,1)}, u32[]{:S(2)}, u32[]{:S(2)}) %collective-permute-start.5) | collective-permute-done | bytes 1048608 | tf_op jit(solution)/shard_map/ppermute | solution.py:49
  129.0 5.4 collective-permute-done.9
  134.6 5.2 collective-permute-done.10
  164.1 10.7 %all-gather.2.cloned.1.call-done.w_hbm = bf16[16,832,1024]{2,1,0:T(8,128)(2,1)} async-done(((bf16[1,832,1024]{2,1,0:T(8,128)(2,1)}), bf16[16,832,1024]{2,1,0:T(8,128)(2,1)}) %all-gather.2.cloned.1.call-update) | async-done | bytes 27262992 | tf_op jit(solution)/shard_map/all_gather | solution.py:920
  174.8 17.4 %front.1 = (f32[256,1024]{1,0:T(8,128)}, f32[256,1]{1,0:T(8,128)}, bf16[256,1024]{1,0:T(8,128)(2,1)}, bf16[256,3072]{1,0:T(8,128)(2,1)}, bf16[256,1024]{1,0:T(8,...) custom-call(bf16[256,1024]{1,0:T(8,128)(2,1)} %copy.104.x_ref, ...), custom_call_target="tpu_custom_call" | custom-call | tf_op jit(solution)/shard_map/front/pallas_call | solution.py:157
  197.9 4.8 cross_query.1.q_ref
  209.9 33.6 %decoder_middle.1 = (f32[256,1024]{1,0:T(8,128)}, f32[256,1024]{1,0:T(8,128)}, f32[256,1]{1,0:T(8,128)}, bf16[256,1024]{1,0:T(8,128)(2,1)}, bf16[256,4096]{1,0:T...) custom-call(s32[18]{0:T(128)} %pad_add_fusion.info_ref, ...), custom_call_target="tpu_custom_call" | custom-call | tf_op jit(solution)/shard_map/decoder_middle/pallas_call | solution.py:157
  246.8 5.8 %cross_query_back.1.dec_ref = f32[256,1024]{1,0:T(8,128)} custom-call(s32[18]{0:T(128)} %pad_add_fusion.info_ref, f32[256,1024]{1,0:T(8,128)} %get-tuple-element.105.resid_ref, bf16[256,4096]{1,0:T(8,128)(2,1)} %get-tuple-element.168.d_ref.dy_ref, bf16[4,2,4,32,1024]{4,3,2,1,0:T(8,128)(2,1)} %copy.105.refs_0_, bf16[4,2,4,32,1024]{4,3,2,1,0:T(8,128)(2,1)} %copy.106.refs_1_, ...), custom_call_target="tpu_custom_call" | custom-call | tf_op jit(solution)/shard_map/cross_query_back/pallas_call | solution.py:157
  261.4 6.8 %norm_backward.1 = (f32[256,1024]{1,0:T(8,128)}, bf16[256,1024]{1,0:T(8,128)(2,1)}, f32[1,1024]{1,0:T(1,128)}, f32[1,1024]{1,0:T(1,128)}, bf16[1024,512]{1,0:T(8...) custom-call(f32[256,1024]{1,0:T(8,128)} %bitcast.174, ...), custom_call_target="tpu_custom_call" | custom-call | tf_op jit(solution)/shard_map/norm_backward/pallas_call | solution.py:157
  268.3 5.8 %outer.14 = (bf16[256,2048]{1,0:T(8,128)(2,1)}, bf16[256,2048]{1,0:T(8,128)(2,1)}, bf16[256,2048]{1,0:T(8,128)(2,1)}, bf16[256,2048]{1,0:T(8,128)(2,1)}) custom-call(bf16[3,1024,256]{2,1,0:T(8,128)(2,1)} %pad_maximum_fusion.2.a_ref, bf16[256,4096]{1,0:T(8,128)(2,1)} %get-tuple-element.168.d_ref.dy_ref), custom_call_target="tpu_custom_call" | custom-call | tf_op jit(solution)/shard_map/outer/pallas_call | solution.py:866
  279.8 12.4 %ffn_backward.1 = (f32[256,1024]{1,0:T(8,128)}, bf16[256,4096]{1,0:T(8,128)(2,1)}, bf16[256,2048]{1,0:T(8,128)(2,1)}, bf16[256,2048]{1,0:T(8,128)(2,1)}, bf16[25...) custom-call(bf16[256,1024]{1,0:T(8,128)(2,1)} %get-tuple-element.148.dy_ref.branch_ref, ...), custom_call_target="tpu_custom_call" | custom-call | tf_op jit(solution)/shard_map/ffn_backward/pallas_call | solution.py:157
  294.7 5.0 outer.16
  309.0 4.5 all-to-all-start
  314.9 5.1 outer.19
  320.0 12.8 %attention_backward.1 = (f32[256,1024]{1,0:T(8,128)}, bf16[256,4096]{1,0:T(8,128)(2,1)}, f32[1,1024]{1,0:T(1,128)}, f32[1,1024]{1,0:T(1,128)}, bf16[256,2048]{1,...) custom-call(s32[18]{0:T(128)} %pad_add_fusion.info_ref, ...), custom_call_target="tpu_custom_call" | custom-call | tf_op jit(solution)/shard_map/attention_backward/pallas_call | solution.py:157
  339.3 5.4 all-to-all-start.1
  344.9 7.9 %embed_backward.1 = (bf16[256,1024]{1,0:T(8,128)(2,1)}, f32[256,1024]{1,0:T(8,128)}, f32[1,1024]{1,0:T(1,128)}, f32[1,1024]{1,0:T(1,128)}) custom-call(f32[256,1024]{1,0:T(8,128)} %get-tuple-element.142.grad_ref, bf16[256,4096]{1,0:T(8,128)(2,1)} %get-tuple-element.171.dp_ref.dy_ref, f32[256,1024]{1,0:T(8,128)} %get-tuple-element.151.n_ref, ...), custom_call_target="tpu_custom_call" | custom-call | tf_op jit(solution)/shard_map/embed_backward/pallas_call | solution.py:157
  359.6 5.0 outer.22
  368.2 5.0 outer.23
  381.2 5.6 %outer.27 = bf16[256,4096]{1,0:T(8,128)(2,1)} custom-call(bf16[1024,256]{1,0:T(8,128)(2,1)} %fusion.29.a_ref, bf16[256,4096]{1,0:T(8,128)(2,1)} %get-tuple-element.175.dy_ref, bf16[256,2048]{1,0:T(8,128)(2,1)} %copy-done.8, bf16[256,2048]{1,0:T(8,128)(2,1)} %copy-done.10, bf16[256,4096]{1,0:T(8,128)(2,1)} %collective-permute-done.44.refs_2_), custom_call_target="tpu_custom_call" | custom-call | tf_op jit(solution)/shard_map/outer/pallas_call | solution.py:866
  386.8 5.1 all-to-all-start.2
  394.1 24.1 %collective-permute-done.31 = bf16[128,4096]{1,0:T(8,128)(2,1)S(1)} collective-permute-done((bf16[128,4096]{1,0:T(8,128)(2,1)S(1)}, bf16[128,4096]{1,0:T(8,128)(2,1)S(1)}, u32[]{:S(2)}, u32[]{:S(2)}) %collective-permute-start.31) | collective-permute-done | bytes 1048608 | tf_op jit(solution)/shard_map/ppermute | solution.py:24
  419.4 20.7 %all-to-all-done.2 = bf16[4,64,4096]{2,1,0:T(8,128)(2,1)} async-done(((bf16[4,64,4096]{2,1,0:T(8,128)(2,1)}), bf16[4,64,4096]{2,1,0:T(8,128)(2,1)}, u32[]{:S(2)}, u32[]{:S(2)}) %all-to-all-start.2) | async-done | bytes 2097184 | tf_op jit(solution)/shard_map/all_to_all | solution.py:31
  448.0 13.6 %collective-permute-done.36.refs_2_ = bf16[256,4096]{1,0:T(8,128)(2,1)} collective-permute-done((bf16[256,4096]{1,0:T(8,128)(2,1)}, bf16[256,4096]{1,0:T(8,128)(2,1)}, u32[]{:S(2)}, u32[]{:S(2)}) %collective-permute-start.36) | collective-permute-done | bytes 2097184 | tf_op jit(solution)/shard_map/ppermute | solution.py:24
  461.6 5.5 outer.24
  477.1 9.5 %collective-permute-done.41.refs_2_ = bf16[256,1024]{1,0:T(8,128)(2,1)S(1)} collective-permute-done((bf16[256,1024]{1,0:T(8,128)(2,1)}, bf16[256,1024]{1,0:T(8,128)(2,1)S(1)}, u32[]{:S(2)}, u32[]{:S(2)}) %collective-permute-start.41) | collective-permute-done | bytes 524320 | tf_op jit(solution)/shard_map/ppermute | solution.py:24
  502.0 19.0 %all-to-all-done.4 = bf16[4,64,4096]{2,1,0:T(8,128)(2,1)S(1)} async-done(((bf16[4,64,4096]{2,1,0:T(8,128)(2,1)}), bf16[4,64,4096]{2,1,0:T(8,128)(2,1)S(1)}, u32[]{:S(2)}, u32[]{:S(2)}) %all-to-all-start.4) | async-done | bytes 2097184 | tf_op jit(solution)/shard_map/all_to_all | solution.py:31
  526.5 12.0 %all-to-all-done.5 = bf16[4,64,1024]{2,1,0:T(8,128)(2,1)S(1)} async-done(((bf16[4,64,1024]{2,1,0:T(8,128)(2,1)}), bf16[4,64,1024]{2,1,0:T(8,128)(2,1)S(1)}, u32[]{:S(2)}, u32[]{:S(2)}) %all-to-all-start.5) | async-done | bytes 524320 | tf_op jit(solution)/shard_map/all_to_all | solution.py:31
  (318 shorter events, 164.8 us)
Async XLA Ops:
  7.2 167.6 %all-gather.2.cloned.1.call-start = ((), (), s32[]{:S(2)}) async-start(), calls=%async_computation.6 | async-start | bytes 28966912 | tf_op jit(solution)/shard_map/all_gather | solution.py:920
  22.8 16.0 %collective-permute-start.1 = (bf16[4,32,1024]{2,1,0:T(8,128)(2,1)S(1)}, bf16[4,32,1024]{2,1,0:T(8,128)(2,1)S(1)}, u32[]{:S(2)}, u32[]{:S(2)}) collective-permute-start(bf16[4,32,1024]{2,1,0:T(8,128)(2,1)S(1)} %collective-permute-done), channel_id=1, source_target_pairs={{0,4},{1,5},{2,6},{3,7},{4,8},{5,9},{6,10},{7,11},{8,12},{9,13},{1... | collective-permute-start | bytes 786440 | tf_op jit(solution)/shard_map/ppermute | solution.py:36
  55.6 47.6 %collective-permute-start.4 = (bf16[4,4,32,1024]{3,2,1,0:T(8,128)(2,1)}, bf16[4,4,32,1024]{3,2,1,0:T(8,128)(2,1)}, u32[]{:S(2)}, u32[]{:S(2)}) collective-permute-start(bf16[4,4,32,1024]{3,2,1,0:T(8,128)(2,1)} %pad_maximum_fusion.3), channel_id=1, source_target_pairs={{0,2},{1,3},{2,0},{3,1},{4,6},{5,7},{6,4},{7,5},{8,10},{9,11},{10,... | collective-permute-start | bytes 3145736 | tf_op jit(solution)/shard_map/ppermute | solution.py:24
  57.0 72.0 %collective-permute-start.8 = (bf16[1,448]{1,0:T(2,128)(2,1)S(1)}, bf16[1,448]{1,0:T(2,128)(2,1)S(1)}, u32[]{:S(2)}, u32[]{:S(2)}) collective-permute-start(bf16[1,448]{1,0:T(2,128)(2,1)S(1)} %pad_maximum_fusion.14), channel_id=1, source_target_pairs={{0,4},{1,5},{2,6},{3,7},{4,8},{5,9},{6,10},{7,11},{8,12},{9,13},{1... | collective-permute-start | bytes 2696 | tf_op jit(solution)/shard_map/ppermute | solution.py:36
  57.2 55.2 %collective-permute-start.3 = (bf16[4,4,32,1024]{3,2,1,0:T(8,128)(2,1)}, bf16[4,4,32,1024]{3,2,1,0:T(8,128)(2,1)}, u32[]{:S(2)}, u32[]{:S(2)}) collective-permute-start(bf16[4,4,32,1024]{3,2,1,0:T(8,128)(2,1)} %pad_maximum_fusion.3), channel_id=1, source_target_pairs={{0,16},{1,17},{2,18},{3,19},{4,20},{5,21},{6,22},{7,23},{8,24},{9,... | collective-permute-start | bytes 3145736 | tf_op jit(solution)/shard_map/ppermute | solution.py:49
  103.3 22.4 %collective-permute-start.5 = (bf16[4,4,32,1024]{3,2,1,0:T(8,128)(2,1)}, bf16[4,4,32,1024]{3,2,1,0:T(8,128)(2,1)}, u32[]{:S(2)}, u32[]{:S(2)}) collective-permute-start(bf16[4,4,32,1024]{3,2,1,0:T(8,128)(2,1)} %collective-permute-done.4), channel_id=1, source_target_pairs={{0,16},{1,17},{2,18},{3,19},{4,20},{5,21},{6,22},{7,23},{8,24},{9,... | collective-permute-start | bytes 3145736 | tf_op jit(solution)/shard_map/ppermute | solution.py:49
  112.4 47.6 %collective-permute-start.7 = (bf16[4,2,4,32,1024]{4,3,2,1,0:T(8,128)(2,1)S(1)}, bf16[4,2,4,32,1024]{4,3,2,1,0:T(8,128)(2,1)}, u32[]{:S(2)}, u32[]{:S(2)}) collective-permute-start(bf16[4,2,4,32,1024]{4,3,2,1,0:T(8,128)(2,1)S(1)} %pad_maximum_fusion.1.refs_2_), channel_id=1, source_target_pairs={{0,1},{1,0},{2,3},{3,2},{4,5},{5,4},{6,7},{7,6},{8,9},{9,8},{10,11... | collective-permute-start | bytes 6291464 | tf_op jit(solution)/shard_map/ppermute | solution.py:19
  128.8 31.1 %collective-permute-start.6 = (bf16[4,2,4,32,1024]{4,3,2,0,1:T(8,128)(2,1)}, bf16[4,2,4,32,1024]{4,3,2,0,1:T(8,128)(2,1)}, u32[]{:S(2)}, u32[]{:S(2)}) collective-permute-start(bf16[4,2,4,32,1024]{4,3,2,0,1:T(8,128)(2,1)} %pad_maximum_fusion), channel_id=1, source_target_pairs={{0,1},{1,0},{2,3},{3,2},{4,5},{5,4},{6,7},{7,6},{8,9},{9,8},{10,11... | collective-permute-start | bytes 6291464 | tf_op jit(solution)/shard_map/ppermute | solution.py:19
  274.2 18.1 %collective-permute-start.18 = (bf16[256,2048]{1,0:T(8,128)(2,1)}, bf16[256,2048]{1,0:T(8,128)(2,1)S(1)}, u32[]{:S(2)}, u32[]{:S(2)}) collective-permute-start(bf16[256,2048]{1,0:T(8,128)(2,1)} %get-tuple-element.121), channel_id=1, source_target_pairs={{0,1},{1,0},{2,3},{3,2},{4,5},{5,4},{6,7},{7,6},{8,9},{9,8},{10,11... | collective-permute-start | bytes 3145736 | tf_op jit(solution)/shard_map/ppermute | solution.py:19
  274.6 18.5 %collective-permute-start.19 = (bf16[256,2048]{1,0:T(8,128)(2,1)}, bf16[256,2048]{1,0:T(8,128)(2,1)S(1)}, u32[]{:S(2)}, u32[]{:S(2)}) collective-permute-start(bf16[256,2048]{1,0:T(8,128)(2,1)} %get-tuple-element.122), channel_id=1, source_target_pairs={{0,1},{1,0},{2,3},{3,2},{4,5},{5,4},{6,7},{7,6},{8,9},{9,8},{10,11... | collective-permute-start | bytes 3145736 | tf_op jit(solution)/shard_map/ppermute | solution.py:19
  274.7 19.9 %collective-permute-start.20 = (bf16[1024,512]{1,0:T(8,128)(2,1)}, bf16[1024,512]{1,0:T(8,128)(2,1)}, u32[]{:S(2)}, u32[]{:S(2)}) collective-permute-start(bf16[1024,512]{1,0:T(8,128)(2,1)} %get-tuple-element.117), channel_id=1, source_target_pairs={{0,1},{1,0},{2,3},{3,2},{4,5},{5,4},{6,7},{7,6},{8,9},{9,8},{10,11... | collective-permute-start | bytes 3145736 | tf_op jit(solution)/shard_map/ppermute | solution.py:19
  279.0 25.3 %collective-permute-start.22 = (bf16[1024,512]{1,0:T(8,128)(2,1)}, bf16[1024,512]{1,0:T(8,128)(2,1)S(1)}, u32[]{:S(2)}, u32[]{:S(2)}) collective-permute-start(bf16[1024,512]{1,0:T(8,128)(2,1)} %outer.15), channel_id=1, source_target_pairs={{0,2},{1,3},{2,0},{3,1},{4,6},{5,7},{6,4},{7,5},{8,10},{9,11},{10,... | collective-permute-start | bytes 3145736 | tf_op jit(solution)/shard_map/ppermute | solution.py:24
  279.8 25.0 %collective-permute-start.21 = (bf16[1024,512]{1,0:T(8,128)(2,1)}, bf16[1024,512]{1,0:T(8,128)(2,1)}, u32[]{:S(2)}, u32[]{:S(2)}) collective-permute-start(bf16[1024,512]{1,0:T(8,128)(2,1)} %get-tuple-element.118), channel_id=1, source_target_pairs={{0,1},{1,0},{2,3},{3,2},{4,5},{5,4},{6,7},{7,6},{8,9},{9,8},{10,11... | collective-permute-start | bytes 3145736 | tf_op jit(solution)/shard_map/ppermute | solution.py:19
  292.3 21.2 %collective-permute-start.23 = (bf16[256,2048]{1,0:T(8,128)(2,1)}, bf16[256,2048]{1,0:T(8,128)(2,1)}, u32[]{:S(2)}, u32[]{:S(2)}) collective-permute-start(bf16[256,2048]{1,0:T(8,128)(2,1)} %get-tuple-element.130), channel_id=1, source_target_pairs={{0,1},{1,0},{2,3},{3,2},{4,5},{5,4},{6,7},{7,6},{8,9},{9,8},{10,11... | collective-permute-start | bytes 3145736 | tf_op jit(solution)/shard_map/ppermute | solution.py:19
  294.6 20.2 %collective-permute-start.24 = (bf16[256,2048]{1,0:T(8,128)(2,1)}, bf16[256,2048]{1,0:T(8,128)(2,1)}, u32[]{:S(2)}, u32[]{:S(2)}) collective-permute-start(bf16[256,2048]{1,0:T(8,128)(2,1)} %get-tuple-element.131), channel_id=1, source_target_pairs={{0,1},{1,0},{2,3},{3,2},{4,5},{5,4},{6,7},{7,6},{8,9},{9,8},{10,11... | collective-permute-start | bytes 3145736 | tf_op jit(solution)/shard_map/ppermute | solution.py:19
  304.3 28.5 %collective-permute-start.25 = (bf16[1024,512]{1,0:T(8,128)(2,1)}, bf16[1024,512]{1,0:T(8,128)(2,1)}, u32[]{:S(2)}, u32[]{:S(2)}) collective-permute-start(bf16[1024,512]{1,0:T(8,128)(2,1)} %get-tuple-element.119), channel_id=1, source_target_pairs={{0,1},{1,0},{2,3},{3,2},{4,5},{5,4},{6,7},{7,6},{8,9},{9,8},{10,11... | collective-permute-start | bytes 3145736 | tf_op jit(solution)/shard_map/ppermute | solution.py:19
  304.3 30.1 %collective-permute-start.28 = (bf16[256,2048]{1,0:T(8,128)(2,1)}, bf16[256,2048]{1,0:T(8,128)(2,1)}, u32[]{:S(2)}, u32[]{:S(2)}) collective-permute-start(bf16[256,2048]{1,0:T(8,128)(2,1)} %get-tuple-element.123), channel_id=1, source_target_pairs={{0,1},{1,0},{2,3},{3,2},{4,5},{5,4},{6,7},{7,6},{8,9},{9,8},{10,11... | collective-permute-start | bytes 3145736 | tf_op jit(solution)/shard_map/ppermute | solution.py:19
  304.9 29.8 %collective-permute-start.26 = (bf16[1024,512]{1,0:T(8,128)(2,1)}, bf16[1024,512]{1,0:T(8,128)(2,1)}, u32[]{:S(2)}, u32[]{:S(2)}) collective-permute-start(bf16[1024,512]{1,0:T(8,128)(2,1)} %outer.17), channel_id=1, source_target_pairs={{0,2},{1,3},{2,0},{3,1},{4,6},{5,7},{6,4},{7,5},{8,10},{9,11},{10,... | collective-permute-start | bytes 3145736 | tf_op jit(solution)/shard_map/ppermute | solution.py:24
  309.0 30.3 %all-to-all-start = ((bf16[4,256,512]{2,1,0:T(8,128)(2,1)}), bf16[4,256,512]{2,1,0:T(8,128)(2,1)S(1)}, u32[]{:S(2)}, u32[]{:S(2)}) async-start(bf16[4,256,512]{2,1,0:T(8,128)(2,1)} %bitcast.176), calls=%async_computation | async-start | bytes 2097152 | tf_op jit(solution)/shard_map/all_to_all | solution.py:31
  313.5 51.1 %collective-permute-start.30 = (bf16[256,4096]{1,0:T(8,128)(2,1)}, bf16[256,4096]{1,0:T(8,128)(2,1)S(1)}, u32[]{:S(2)}, u32[]{:S(2)}) collective-permute-start(bf16[256,4096]{1,0:T(8,128)(2,1)} %outer.16), channel_id=1, source_target_pairs={{16,0},{17,1},{18,2},{19,3},{20,4},{21,5},{22,6},{23,7},{24,8},{25... | collective-permute-start | bytes 6291464 | tf_op jit(solution)/shard_map/ppermute | solution.py:53
  314.8 44.7 %collective-permute-start.29 = (bf16[256,2048]{1,0:T(8,128)(2,1)}, bf16[256,2048]{1,0:T(8,128)(2,1)}, u32[]{:S(2)}, u32[]{:S(2)}) collective-permute-start(bf16[256,2048]{1,0:T(8,128)(2,1)} %get-tuple-element.124), channel_id=1, source_target_pairs={{0,1},{1,0},{2,3},{3,2},{4,5},{5,4},{6,7},{7,6},{8,9},{9,8},{10,11... | collective-permute-start | bytes 3145736 | tf_op jit(solution)/shard_map/ppermute | solution.py:19
  332.9 48.4 %collective-permute-start.44 = (bf16[256,4096]{1,0:T(8,128)(2,1)}, bf16[256,4096]{1,0:T(8,128)(2,1)}, u32[]{:S(2)}, u32[]{:S(2)}) collective-permute-start(bf16[256,4096]{1,0:T(8,128)(2,1)} %outer.19), channel_id=1, source_target_pairs={{0,2},{1,3},{2,0},{3,1},{4,6},{5,7},{6,4},{7,5},{8,10},{9,11},{10,... | collective-permute-start | bytes 6291464 | tf_op jit(solution)/shard_map/ppermute | solution.py:24
  334.5 30.7 %collective-permute-start.34 = (bf16[256,2048]{1,0:T(8,128)(2,1)}, bf16[256,2048]{1,0:T(8,128)(2,1)}, u32[]{:S(2)}, u32[]{:S(2)}) collective-permute-start(bf16[256,2048]{1,0:T(8,128)(2,1)} %get-tuple-element.144), channel_id=1, source_target_pairs={{0,1},{1,0},{2,3},{3,2},{4,5},{5,4},{6,7},{7,6},{8,9},{9,8},{10,11... | collective-permute-start | bytes 3145736 | tf_op jit(solution)/shard_map/ppermute | solution.py:19
  334.7 30.6 %collective-permute-start.35 = (bf16[256,2048]{1,0:T(8,128)(2,1)}, bf16[256,2048]{1,0:T(8,128)(2,1)}, u32[]{:S(2)}, u32[]{:S(2)}) collective-permute-start(bf16[256,2048]{1,0:T(8,128)(2,1)} %get-tuple-element.145), channel_id=1, source_target_pairs={{0,1},{1,0},{2,3},{3,2},{4,5},{5,4},{6,7},{7,6},{8,9},{9,8},{10,11... | collective-permute-start | bytes 3145736 | tf_op jit(solution)/shard_map/ppermute | solution.py:19
  339.3 47.5 %all-to-all-start.1 = ((bf16[4,256,512]{2,1,0:T(8,128)(2,1)}), bf16[4,256,512]{2,1,0:T(8,128)(2,1)}, u32[]{:S(2)}, u32[]{:S(2)}) async-start(bf16[4,256,512]{2,1,0:T(8,128)(2,1)} %bitcast.175), calls=%async_computation.1 | async-start | bytes 2097152 | tf_op jit(solution)/shard_map/all_to_all | solution.py:31
  359.5 17.7 %collective-permute-start.42 = (bf16[256,2048]{1,0:T(8,128)(2,1)}, bf16[256,2048]{1,0:T(8,128)(2,1)S(1)}, u32[]{:S(2)}, u32[]{:S(2)}) collective-permute-start(bf16[256,2048]{1,0:T(8,128)(2,1)} %get-tuple-element.132), channel_id=1, source_target_pairs={{0,1},{1,0},{2,3},{3,2},{4,5},{5,4},{6,7},{7,6},{8,9},{9,8},{10,11... | collective-permute-start | bytes 3145736 | tf_op jit(solution)/shard_map/ppermute | solution.py:19
  386.8 53.3 %all-to-all-start.2 = ((bf16[4,64,4096]{2,1,0:T(8,128)(2,1)}), bf16[4,64,4096]{2,1,0:T(8,128)(2,1)}, u32[]{:S(2)}, u32[]{:S(2)}) async-start(bf16[4,64,4096]{2,1,0:T(8,128)(2,1)} %bitcast.171), calls=%async_computation.2 | async-start | bytes 4194304 | tf_op jit(solution)/shard_map/all_to_all | solution.py:31
  392.0 26.2 %collective-permute-start.31 = (bf16[128,4096]{1,0:T(8,128)(2,1)S(1)}, bf16[128,4096]{1,0:T(8,128)(2,1)S(1)}, u32[]{:S(2)}, u32[]{:S(2)}) collective-permute-start(bf16[128,4096]{1,0:T(8,128)(2,1)S(1)} %slice.206), channel_id=1, source_target_pairs={{0,2},{1,3},{2,0},{3,1},{4,6},{5,7},{6,4},{7,5},{8,10},{9,11},{10,... | collective-permute-start | bytes 3145736 | tf_op jit(solution)/shard_map/ppermute | solution.py:24
  393.6 68.0 %collective-permute-start.36 = (bf16[256,4096]{1,0:T(8,128)(2,1)}, bf16[256,4096]{1,0:T(8,128)(2,1)}, u32[]{:S(2)}, u32[]{:S(2)}) collective-permute-start(bf16[256,4096]{1,0:T(8,128)(2,1)} %outer.23), channel_id=1, source_target_pairs={{0,2},{1,3},{2,0},{3,1},{4,6},{5,7},{6,4},{7,5},{8,10},{9,11},{10,... | collective-permute-start | bytes 6291464 | tf_op jit(solution)/shard_map/ppermute | solution.py:24
  440.1 28.7 %all-to-all-start.3 = ((bf16[4,32,4096]{2,1,0:T(8,128)(2,1)}), bf16[4,32,4096]{2,1,0:T(8,128)(2,1)S(1)}, u32[]{:S(2)}, u32[]{:S(2)}) async-start(bf16[4,32,4096]{2,1,0:T(8,128)(2,1)} %bitcast.83), calls=%async_computation.3 | async-start | bytes 2097152 | tf_op jit(solution)/shard_map/all_to_all | solution.py:31
  469.8 51.3 %all-to-all-start.4 = ((bf16[4,64,4096]{2,1,0:T(8,128)(2,1)}), bf16[4,64,4096]{2,1,0:T(8,128)(2,1)S(1)}, u32[]{:S(2)}, u32[]{:S(2)}) async-start(bf16[4,64,4096]{2,1,0:T(8,128)(2,1)} %bitcast.172), calls=%async_computation.4 | async-start | bytes 4194304 | tf_op jit(solution)/shard_map/all_to_all | solution.py:31
  521.0 17.4 %all-to-all-start.5 = ((bf16[4,64,1024]{2,1,0:T(8,128)(2,1)}), bf16[4,64,1024]{2,1,0:T(8,128)(2,1)S(1)}, u32[]{:S(2)}, u32[]{:S(2)}) async-start(bf16[4,64,1024]{2,1,0:T(8,128)(2,1)} %bitcast.85), calls=%async_computation.5 | async-start | bytes 1048576 | tf_op jit(solution)/shard_map/all_to_all | solution.py:31
  (66 other events, 593.5 us)
Sparse Core Ops, SparseCore 0:
  11.4 163.4 all-gather.1

commit v4 on v3

--- a/solution.py
+++ b/solution.py
@@ -310,7 +310,7 @@
 
 
 def blocks_loop(count, step):
-    lax.fori_loop(0, count, lambda j, carry: (step(j), carry)[1], 0)
+    lax.fori_loop(0, count, lambda j, carry: (step(j), carry)[1], 0, unroll=1 if count % 2 else 2)
 
 
 def front(tokens, mask, weights, rows_of, gains, biases):

time: 559 us -> 552 us (0.987)
  transfers between devices with their start and end apart: 52 -> 52, of which waited for: 24 -> 24; matrix products, arithmetic and copies ran while one was open for 10% -> 10% of each run, Pallas kernels for 18% -> 19%
where the time goes in v4:
time: 552 us; the launch traced here: 545 us
  waiting for transfers between devices  234 us (42%)
  Pallas kernels  156 us (28%)
  starting transfers between devices  66.9 us (12%)
  local copies, waits for them, and re-layouts  36.2 us (7%)
  other arithmetic  27.2 us (5%)
  between operations  15.2 us (3%)
  matrix products  10 us (2%)
    pallas_call x8, Pallas kernels, kernel_call(): pl.pallas_call(body, in_specs=specs, out_specs=out_specs, out_shape=out_s...  98.6 us
    ppermute x8, waiting for transfers between devices, swap_pair(): return lax.ppermute(x, 'dp', [(i, i ^ 2) for i in range(n)])  94.5 us
    pallas_call x14, Pallas kernels, outer(): pl.pallas_call(kernel, grid=(grid,), in_specs=specs, out_specs=out_specs,...  57.4 us
    all_to_all x6, waiting for transfers between devices, spread_outer(): return lax.all_to_all(x, 'dp', 0, 0, axis_index_groups=groups)  53.4 us
    ppermute x6, waiting for transfers between devices, shift_outer(): return lax.ppermute(x, 'dp', [(i, (i + 4) % n) for i in range(n)])  50.4 us
    all_to_all x6, starting transfers between devices, spread_outer(): return lax.all_to_all(x, 'dp', 0, 0, axis_index_groups=groups)  25.5 us
    ppermute x5, starting transfers between devices, to_decoder(): return lax.ppermute(x, 'section', [(0, 1)])  18.9 us
    ppermute x5, waiting for transfers between devices, to_decoder(): return lax.ppermute(x, 'section', [(0, 1)])  18 us
  transfers between devices with their start and end apart: 52, of which 24 were waited for; matrix products, arithmetic and copies ran while one was open for 10% of the time, Pallas kernels for 19%

profile of v4, /device:TPU:0, one launch (start us, length us, event | category | flops | bytes accessed | tf_op | source)
XLA Modules:
  0.0 545.2 jit_solution(17749722334009527877)
XLA Ops:
  14.5 8.3 %collective-permute-done = bf16[4,32,1024]{2,1,0:T(8,128)(2,1)S(1)} collective-permute-done((bf16[4,32,1024]{2,1,0:T(8,128)(2,1)S(1)}, bf16[4,32,1024]{2,1,0:T(8,128)(2,1)S(1)}, u32[]{:S(2)}, u32[]{:S(2)}) %collective-permute-start) | collective-permute-done | bytes 262176 | tf_op jit(solution)/shard_map/ppermute | solution.py:36
  22.9 16.0 %collective-permute-done.1 = bf16[4,32,1024]{2,1,0:T(8,128)(2,1)S(1)} collective-permute-done((bf16[4,32,1024]{2,1,0:T(8,128)(2,1)S(1)}, bf16[4,32,1024]{2,1,0:T(8,128)(2,1)S(1)}, u32[]{:S(2)}, u32[]{:S(2)}) %collective-permute-start.1) | collective-permute-done | bytes 262176 | tf_op jit(solution)/shard_map/ppermute | solution.py:36
  39.0 15.5 %collective-permute-done.2 = bf16[4,32,1024]{2,1,0:T(8,128)(2,1)S(1)} collective-permute-done((bf16[4,32,1024]{2,1,0:T(8,128)(2,1)S(1)}, bf16[4,32,1024]{2,1,0:T(8,128)(2,1)S(1)}, u32[]{:S(2)}, u32[]{:S(2)}) %collective-permute-start.2) | collective-permute-done | bytes 262176 | tf_op jit(solution)/shard_map/ppermute | solution.py:36
  61.6 41.7 %collective-permute-done.4 = bf16[4,4,32,1024]{3,2,1,0:T(8,128)(2,1)} collective-permute-done((bf16[4,4,32,1024]{3,2,1,0:T(8,128)(2,1)}, bf16[4,4,32,1024]{3,2,1,0:T(8,128)(2,1)}, u32[]{:S(2)}, u32[]{:S(2)}) %collective-permute-start.4) | collective-permute-done | bytes 1048608 | tf_op jit(solution)/shard_map/ppermute | solution.py:24
  112.5 13.2 %collective-permute-done.5 = bf16[4,4,32,1024]{3,2,1,0:T(8,128)(2,1)} collective-permute-done((bf16[4,4,32,1024]{3,2,1,0:T(8,128)(2,1)}, bf16[4,4,32,1024]{3,2,1,0:T(8,128)(2,1)}, u32[]{:S(2)}, u32[]{:S(2)}) %collective-permute-start.5) | collective-permute-done | bytes 1048608 | tf_op jit(solution)/shard_map/ppermute | solution.py:49
  129.0 5.4 collective-permute-done.9
  134.6 5.2 collective-permute-done.10
  164.1 10.7 %all-gather.2.cloned.1.call-done.w_hbm = bf16[16,832,1024]{2,1,0:T(8,128)(2,1)} async-done(((bf16[1,832,1024]{2,1,0:T(8,128)(2,1)}), bf16[16,832,1024]{2,1,0:T(8,128)(2,1)}) %all-gather.2.cloned.1.call-update) | async-done | bytes 27262992 | tf_op jit(solution)/shard_map/all_gather | solution.py:920
  174.8 16.8 %front.1 = (f32[256,1024]{1,0:T(8,128)}, f32[256,1]{1,0:T(8,128)}, bf16[256,1024]{1,0:T(8,128)(2,1)}, bf16[256,3072]{1,0:T(8,128)(2,1)}, bf16[256,1024]{1,0:T(8,...) custom-call(bf16[256,1024]{1,0:T(8,128)(2,1)} %copy.104.x_ref, ...), custom_call_target="tpu_custom_call" | custom-call | tf_op jit(solution)/shard_map/front/pallas_call | solution.py:157
  196.9 4.8 cross_query.1.q_ref
  209.2 32.5 %decoder_middle.1 = (f32[256,1024]{1,0:T(8,128)}, f32[256,1024]{1,0:T(8,128)}, f32[256,1]{1,0:T(8,128)}, bf16[256,1024]{1,0:T(8,128)(2,1)}, bf16[256,4096]{1,0:T...) custom-call(s32[18]{0:T(128)} %pad_add_fusion.info_ref, ...), custom_call_target="tpu_custom_call" | custom-call | tf_op jit(solution)/shard_map/decoder_middle/pallas_call | solution.py:157
  245.2 5.8 %cross_query_back.1.dec_ref = f32[256,1024]{1,0:T(8,128)} custom-call(s32[18]{0:T(128)} %pad_add_fusion.info_ref, f32[256,1024]{1,0:T(8,128)} %get-tuple-element.105.resid_ref, bf16[256,4096]{1,0:T(8,128)(2,1)} %get-tuple-element.168.d_ref.dy_ref, bf16[4,2,4,32,1024]{4,3,2,1,0:T(8,128)(2,1)} %copy.105.refs_0_, bf16[4,2,4,32,1024]{4,3,2,1,0:T(8,128)(2,1)} %copy.106.refs_1_, ...), custom_call_target="tpu_custom_call" | custom-call | tf_op jit(solution)/shard_map/cross_query_back/pallas_call | solution.py:157
  259.7 5.6 %norm_backward.1 = (f32[256,1024]{1,0:T(8,128)}, bf16[256,1024]{1,0:T(8,128)(2,1)}, f32[1,1024]{1,0:T(1,128)}, f32[1,1024]{1,0:T(1,128)}, bf16[1024,512]{1,0:T(8...) custom-call(f32[256,1024]{1,0:T(8,128)} %bitcast.174, ...), custom_call_target="tpu_custom_call" | custom-call | tf_op jit(solution)/shard_map/norm_backward/pallas_call | solution.py:157
  265.4 5.8 %outer.14 = (bf16[256,2048]{1,0:T(8,128)(2,1)}, bf16[256,2048]{1,0:T(8,128)(2,1)}, bf16[256,2048]{1,0:T(8,128)(2,1)}, bf16[256,2048]{1,0:T(8,128)(2,1)}) custom-call(bf16[3,1024,256]{2,1,0:T(8,128)(2,1)} %pad_maximum_fusion.2.a_ref, bf16[256,4096]{1,0:T(8,128)(2,1)} %get-tuple-element.168.d_ref.dy_ref), custom_call_target="tpu_custom_call" | custom-call | tf_op jit(solution)/shard_map/outer/pallas_call | solution.py:866
  276.8 12.4 %ffn_backward.1 = (f32[256,1024]{1,0:T(8,128)}, bf16[256,4096]{1,0:T(8,128)(2,1)}, bf16[256,2048]{1,0:T(8,128)(2,1)}, bf16[256,2048]{1,0:T(8,128)(2,1)}, bf16[25...) custom-call(bf16[256,1024]{1,0:T(8,128)(2,1)} %get-tuple-element.148.dy_ref.branch_ref, ...), custom_call_target="tpu_custom_call" | custom-call | tf_op jit(solution)/shard_map/ffn_backward/pallas_call | solution.py:157
  291.9 5.0 outer.16
  306.0 4.5 all-to-all-start
  311.9 5.1 outer.19
  317.0 12.8 %attention_backward.1 = (f32[256,1024]{1,0:T(8,128)}, bf16[256,4096]{1,0:T(8,128)(2,1)}, f32[1,1024]{1,0:T(1,128)}, f32[1,1024]{1,0:T(1,128)}, bf16[256,2048]{1,...) custom-call(s32[18]{0:T(128)} %pad_add_fusion.info_ref, ...), custom_call_target="tpu_custom_call" | custom-call | tf_op jit(solution)/shard_map/attention_backward/pallas_call | solution.py:157
  336.3 5.3 all-to-all-start.1
  341.8 7.9 %embed_backward.1 = (bf16[256,1024]{1,0:T(8,128)(2,1)}, f32[256,1024]{1,0:T(8,128)}, f32[1,1024]{1,0:T(1,128)}, f32[1,1024]{1,0:T(1,128)}) custom-call(f32[256,1024]{1,0:T(8,128)} %get-tuple-element.142.grad_ref, bf16[256,4096]{1,0:T(8,128)(2,1)} %get-tuple-element.171.dp_ref.dy_ref, f32[256,1024]{1,0:T(8,128)} %get-tuple-element.151.n_ref, ...), custom_call_target="tpu_custom_call" | custom-call | tf_op jit(solution)/shard_map/embed_backward/pallas_call | solution.py:157
  356.5 5.0 outer.22
  365.2 5.0 outer.23
  378.3 5.6 %outer.27 = bf16[256,4096]{1,0:T(8,128)(2,1)} custom-call(bf16[1024,256]{1,0:T(8,128)(2,1)} %fusion.29.a_ref, bf16[256,4096]{1,0:T(8,128)(2,1)} %get-tuple-element.175.dy_ref, bf16[256,2048]{1,0:T(8,128)(2,1)} %copy-done.8, bf16[256,2048]{1,0:T(8,128)(2,1)} %copy-done.10, bf16[256,4096]{1,0:T(8,128)(2,1)} %collective-permute-done.44.refs_2_), custom_call_target="tpu_custom_call" | custom-call | tf_op jit(solution)/shard_map/outer/pallas_call | solution.py:866
  383.8 5.1 all-to-all-start.2
  391.1 24.1 %collective-permute-done.31 = bf16[128,4096]{1,0:T(8,128)(2,1)S(1)} collective-permute-done((bf16[128,4096]{1,0:T(8,128)(2,1)S(1)}, bf16[128,4096]{1,0:T(8,128)(2,1)S(1)}, u32[]{:S(2)}, u32[]{:S(2)}) %collective-permute-start.31) | collective-permute-done | bytes 1048608 | tf_op jit(solution)/shard_map/ppermute | solution.py:24
  416.4 20.7 %all-to-all-done.2 = bf16[4,64,4096]{2,1,0:T(8,128)(2,1)} async-done(((bf16[4,64,4096]{2,1,0:T(8,128)(2,1)}), bf16[4,64,4096]{2,1,0:T(8,128)(2,1)}, u32[]{:S(2)}, u32[]{:S(2)}) %all-to-all-start.2) | async-done | bytes 2097184 | tf_op jit(solution)/shard_map/all_to_all | solution.py:31
  445.0 13.6 %collective-permute-done.36.refs_2_ = bf16[256,4096]{1,0:T(8,128)(2,1)} collective-permute-done((bf16[256,4096]{1,0:T(8,128)(2,1)}, bf16[256,4096]{1,0:T(8,128)(2,1)}, u32[]{:S(2)}, u32[]{:S(2)}) %collective-permute-start.36) | collective-permute-done | bytes 2097184 | tf_op jit(solution)/shard_map/ppermute | solution.py:24
  458.6 5.5 %outer.24 = bf16[256,4096]{1,0:T(8,128)(2,1)} custom-call(bf16[2,1024,256]{2,1,0:T(8,128)(2,1)} %pad_maximum_fusion.4.a_ref, bf16[256,4096]{1,0:T(8,128)(2,1)} %get-tuple-element.171.dp_ref.dy_ref, bf16[256,2048]{1,0:T(8,128)(2,1)} %copy-done.11, bf16[256,2048]{1,0:T(8,128)(2,1)} %copy-done.12, bf16[256,4096]{1,0:T(8,128)(2,1)} %collective-permute-done.36.refs_2_), custom_call_target="tpu_custom_call" | custom-call | tf_op jit(solution)/shard_map/outer/pallas_call | solution.py:866
  474.1 9.5 %collective-permute-done.41.refs_2_ = bf16[256,1024]{1,0:T(8,128)(2,1)S(1)} collective-permute-done((bf16[256,1024]{1,0:T(8,128)(2,1)}, bf16[256,1024]{1,0:T(8,128)(2,1)S(1)}, u32[]{:S(2)}, u32[]{:S(2)}) %collective-permute-start.41) | collective-permute-done | bytes 524320 | tf_op jit(solution)/shard_map/ppermute | solution.py:24
  499.0 19.0 %all-to-all-done.4 = bf16[4,64,4096]{2,1,0:T(8,128)(2,1)S(1)} async-done(((bf16[4,64,4096]{2,1,0:T(8,128)(2,1)}), bf16[4,64,4096]{2,1,0:T(8,128)(2,1)S(1)}, u32[]{:S(2)}, u32[]{:S(2)}) %all-to-all-start.4) | async-done | bytes 2097184 | tf_op jit(solution)/shard_map/all_to_all | solution.py:31
  523.5 12.0 %all-to-all-done.5 = bf16[4,64,1024]{2,1,0:T(8,128)(2,1)S(1)} async-done(((bf16[4,64,1024]{2,1,0:T(8,128)(2,1)}), bf16[4,64,1024]{2,1,0:T(8,128)(2,1)S(1)}, u32[]{:S(2)}, u32[]{:S(2)}) %all-to-all-start.5) | async-done | bytes 524320 | tf_op jit(solution)/shard_map/all_to_all | solution.py:31
  (318 shorter events, 164.9 us)
Async XLA Ops:
  7.2 167.6 %all-gather.2.cloned.1.call-start = ((), (), s32[]{:S(2)}) async-start(), calls=%async_computation.6 | async-start | bytes 28966912 | tf_op jit(solution)/shard_map/all_gather | solution.py:920
  22.8 16.0 %collective-permute-start.1 = (bf16[4,32,1024]{2,1,0:T(8,128)(2,1)S(1)}, bf16[4,32,1024]{2,1,0:T(8,128)(2,1)S(1)}, u32[]{:S(2)}, u32[]{:S(2)}) collective-permute-start(bf16[4,32,1024]{2,1,0:T(8,128)(2,1)S(1)} %collective-permute-done), channel_id=1, source_target_pairs={{0,4},{1,5},{2,6},{3,7},{4,8},{5,9},{6,10},{7,11},{8,12},{9,13},{1... | collective-permute-start | bytes 786440 | tf_op jit(solution)/shard_map/ppermute | solution.py:36
  55.6 47.6 %collective-permute-start.4 = (bf16[4,4,32,1024]{3,2,1,0:T(8,128)(2,1)}, bf16[4,4,32,1024]{3,2,1,0:T(8,128)(2,1)}, u32[]{:S(2)}, u32[]{:S(2)}) collective-permute-start(bf16[4,4,32,1024]{3,2,1,0:T(8,128)(2,1)} %pad_maximum_fusion.3), channel_id=1, source_target_pairs={{0,2},{1,3},{2,0},{3,1},{4,6},{5,7},{6,4},{7,5},{8,10},{9,11},{10,... | collective-permute-start | bytes 3145736 | tf_op jit(solution)/shard_map/ppermute | solution.py:24
  57.0 72.0 %collective-permute-start.8 = (bf16[1,448]{1,0:T(2,128)(2,1)S(1)}, bf16[1,448]{1,0:T(2,128)(2,1)S(1)}, u32[]{:S(2)}, u32[]{:S(2)}) collective-permute-start(bf16[1,448]{1,0:T(2,128)(2,1)S(1)} %pad_maximum_fusion.14), channel_id=1, source_target_pairs={{0,4},{1,5},{2,6},{3,7},{4,8},{5,9},{6,10},{7,11},{8,12},{9,13},{1... | collective-permute-start | bytes 2696 | tf_op jit(solution)/shard_map/ppermute | solution.py:36
  57.2 55.2 %collective-permute-start.3 = (bf16[4,4,32,1024]{3,2,1,0:T(8,128)(2,1)}, bf16[4,4,32,1024]{3,2,1,0:T(8,128)(2,1)}, u32[]{:S(2)}, u32[]{:S(2)}) collective-permute-start(bf16[4,4,32,1024]{3,2,1,0:T(8,128)(2,1)} %pad_maximum_fusion.3), channel_id=1, source_target_pairs={{0,16},{1,17},{2,18},{3,19},{4,20},{5,21},{6,22},{7,23},{8,24},{9,... | collective-permute-start | bytes 3145736 | tf_op jit(solution)/shard_map/ppermute | solution.py:49
  103.3 22.4 %collective-permute-start.5 = (bf16[4,4,32,1024]{3,2,1,0:T(8,128)(2,1)}, bf16[4,4,32,1024]{3,2,1,0:T(8,128)(2,1)}, u32[]{:S(2)}, u32[]{:S(2)}) collective-permute-start(bf16[4,4,32,1024]{3,2,1,0:T(8,128)(2,1)} %collective-permute-done.4), channel_id=1, source_target_pairs={{0,16},{1,17},{2,18},{3,19},{4,20},{5,21},{6,22},{7,23},{8,24},{9,... | collective-permute-start | bytes 3145736 | tf_op jit(solution)/shard_map/ppermute | solution.py:49
  112.4 47.6 %collective-permute-start.7 = (bf16[4,2,4,32,1024]{4,3,2,1,0:T(8,128)(2,1)S(1)}, bf16[4,2,4,32,1024]{4,3,2,1,0:T(8,128)(2,1)}, u32[]{:S(2)}, u32[]{:S(2)}) collective-permute-start(bf16[4,2,4,32,1024]{4,3,2,1,0:T(8,128)(2,1)S(1)} %pad_maximum_fusion.1.refs_2_), channel_id=1, source_target_pairs={{0,1},{1,0},{2,3},{3,2},{4,5},{5,4},{6,7},{7,6},{8,9},{9,8},{10,11... | collective-permute-start | bytes 6291464 | tf_op jit(solution)/shard_map/ppermute | solution.py:19
  128.8 31.1 %collective-permute-start.6 = (bf16[4,2,4,32,1024]{4,3,2,0,1:T(8,128)(2,1)}, bf16[4,2,4,32,1024]{4,3,2,0,1:T(8,128)(2,1)}, u32[]{:S(2)}, u32[]{:S(2)}) collective-permute-start(bf16[4,2,4,32,1024]{4,3,2,0,1:T(8,128)(2,1)} %pad_maximum_fusion), channel_id=1, source_target_pairs={{0,1},{1,0},{2,3},{3,2},{4,5},{5,4},{6,7},{7,6},{8,9},{9,8},{10,11... | collective-permute-start | bytes 6291464 | tf_op jit(solution)/shard_map/ppermute | solution.py:19
  271.2 18.1 %collective-permute-start.18 = (bf16[256,2048]{1,0:T(8,128)(2,1)}, bf16[256,2048]{1,0:T(8,128)(2,1)S(1)}, u32[]{:S(2)}, u32[]{:S(2)}) collective-permute-start(bf16[256,2048]{1,0:T(8,128)(2,1)} %get-tuple-element.121), channel_id=1, source_target_pairs={{0,1},{1,0},{2,3},{3,2},{4,5},{5,4},{6,7},{7,6},{8,9},{9,8},{10,11... | collective-permute-start | bytes 3145736 | tf_op jit(solution)/shard_map/ppermute | solution.py:19
  271.6 18.5 %collective-permute-start.19 = (bf16[256,2048]{1,0:T(8,128)(2,1)}, bf16[256,2048]{1,0:T(8,128)(2,1)S(1)}, u32[]{:S(2)}, u32[]{:S(2)}) collective-permute-start(bf16[256,2048]{1,0:T(8,128)(2,1)} %get-tuple-element.122), channel_id=1, source_target_pairs={{0,1},{1,0},{2,3},{3,2},{4,5},{5,4},{6,7},{7,6},{8,9},{9,8},{10,11... | collective-permute-start | bytes 3145736 | tf_op jit(solution)/shard_map/ppermute | solution.py:19
  271.7 20.1 %collective-permute-start.20 = (bf16[1024,512]{1,0:T(8,128)(2,1)}, bf16[1024,512]{1,0:T(8,128)(2,1)}, u32[]{:S(2)}, u32[]{:S(2)}) collective-permute-start(bf16[1024,512]{1,0:T(8,128)(2,1)} %get-tuple-element.117), channel_id=1, source_target_pairs={{0,1},{1,0},{2,3},{3,2},{4,5},{5,4},{6,7},{7,6},{8,9},{9,8},{10,11... | collective-permute-start | bytes 3145736 | tf_op jit(solution)/shard_map/ppermute | solution.py:19
  276.0 25.3 %collective-permute-start.22 = (bf16[1024,512]{1,0:T(8,128)(2,1)}, bf16[1024,512]{1,0:T(8,128)(2,1)S(1)}, u32[]{:S(2)}, u32[]{:S(2)}) collective-permute-start(bf16[1024,512]{1,0:T(8,128)(2,1)} %outer.15), channel_id=1, source_target_pairs={{0,2},{1,3},{2,0},{3,1},{4,6},{5,7},{6,4},{7,5},{8,10},{9,11},{10,... | collective-permute-start | bytes 3145736 | tf_op jit(solution)/shard_map/ppermute | solution.py:24
  276.8 25.0 %collective-permute-start.21 = (bf16[1024,512]{1,0:T(8,128)(2,1)}, bf16[1024,512]{1,0:T(8,128)(2,1)}, u32[]{:S(2)}, u32[]{:S(2)}) collective-permute-start(bf16[1024,512]{1,0:T(8,128)(2,1)} %get-tuple-element.118), channel_id=1, source_target_pairs={{0,1},{1,0},{2,3},{3,2},{4,5},{5,4},{6,7},{7,6},{8,9},{9,8},{10,11... | collective-permute-start | bytes 3145736 | tf_op jit(solution)/shard_map/ppermute | solution.py:19
  289.3 21.2 %collective-permute-start.23 = (bf16[256,2048]{1,0:T(8,128)(2,1)}, bf16[256,2048]{1,0:T(8,128)(2,1)}, u32[]{:S(2)}, u32[]{:S(2)}) collective-permute-start(bf16[256,2048]{1,0:T(8,128)(2,1)} %get-tuple-element.130), channel_id=1, source_target_pairs={{0,1},{1,0},{2,3},{3,2},{4,5},{5,4},{6,7},{7,6},{8,9},{9,8},{10,11... | collective-permute-start | bytes 3145736 | tf_op jit(solution)/shard_map/ppermute | solution.py:19
  291.8 20.0 %collective-permute-start.24 = (bf16[256,2048]{1,0:T(8,128)(2,1)}, bf16[256,2048]{1,0:T(8,128)(2,1)}, u32[]{:S(2)}, u32[]{:S(2)}) collective-permute-start(bf16[256,2048]{1,0:T(8,128)(2,1)} %get-tuple-element.131), channel_id=1, source_target_pairs={{0,1},{1,0},{2,3},{3,2},{4,5},{5,4},{6,7},{7,6},{8,9},{9,8},{10,11... | collective-permute-start | bytes 3145736 | tf_op jit(solution)/shard_map/ppermute | solution.py:19
  301.3 28.5 %collective-permute-start.25 = (bf16[1024,512]{1,0:T(8,128)(2,1)}, bf16[1024,512]{1,0:T(8,128)(2,1)}, u32[]{:S(2)}, u32[]{:S(2)}) collective-permute-start(bf16[1024,512]{1,0:T(8,128)(2,1)} %get-tuple-element.119), channel_id=1, source_target_pairs={{0,1},{1,0},{2,3},{3,2},{4,5},{5,4},{6,7},{7,6},{8,9},{9,8},{10,11... | collective-permute-start | bytes 3145736 | tf_op jit(solution)/shard_map/ppermute | solution.py:19
  301.3 30.1 %collective-permute-start.28 = (bf16[256,2048]{1,0:T(8,128)(2,1)}, bf16[256,2048]{1,0:T(8,128)(2,1)}, u32[]{:S(2)}, u32[]{:S(2)}) collective-permute-start(bf16[256,2048]{1,0:T(8,128)(2,1)} %get-tuple-element.123), channel_id=1, source_target_pairs={{0,1},{1,0},{2,3},{3,2},{4,5},{5,4},{6,7},{7,6},{8,9},{9,8},{10,11... | collective-permute-start | bytes 3145736 | tf_op jit(solution)/shard_map/ppermute | solution.py:19
  301.9 29.8 %collective-permute-start.26 = (bf16[1024,512]{1,0:T(8,128)(2,1)}, bf16[1024,512]{1,0:T(8,128)(2,1)}, u32[]{:S(2)}, u32[]{:S(2)}) collective-permute-start(bf16[1024,512]{1,0:T(8,128)(2,1)} %outer.17), channel_id=1, source_target_pairs={{0,2},{1,3},{2,0},{3,1},{4,6},{5,7},{6,4},{7,5},{8,10},{9,11},{10,... | collective-permute-start | bytes 3145736 | tf_op jit(solution)/shard_map/ppermute | solution.py:24
  306.0 30.3 %all-to-all-start = ((bf16[4,256,512]{2,1,0:T(8,128)(2,1)}), bf16[4,256,512]{2,1,0:T(8,128)(2,1)S(1)}, u32[]{:S(2)}, u32[]{:S(2)}) async-start(bf16[4,256,512]{2,1,0:T(8,128)(2,1)} %bitcast.176), calls=%async_computation | async-start | bytes 2097152 | tf_op jit(solution)/shard_map/all_to_all | solution.py:31
  310.5 51.0 %collective-permute-start.30 = (bf16[256,4096]{1,0:T(8,128)(2,1)}, bf16[256,4096]{1,0:T(8,128)(2,1)S(1)}, u32[]{:S(2)}, u32[]{:S(2)}) collective-permute-start(bf16[256,4096]{1,0:T(8,128)(2,1)} %outer.16), channel_id=1, source_target_pairs={{16,0},{17,1},{18,2},{19,3},{20,4},{21,5},{22,6},{23,7},{24,8},{25... | collective-permute-start | bytes 6291464 | tf_op jit(solution)/shard_map/ppermute | solution.py:53
  311.8 44.6 %collective-permute-start.29 = (bf16[256,2048]{1,0:T(8,128)(2,1)}, bf16[256,2048]{1,0:T(8,128)(2,1)}, u32[]{:S(2)}, u32[]{:S(2)}) collective-permute-start(bf16[256,2048]{1,0:T(8,128)(2,1)} %get-tuple-element.124), channel_id=1, source_target_pairs={{0,1},{1,0},{2,3},{3,2},{4,5},{5,4},{6,7},{7,6},{8,9},{9,8},{10,11... | collective-permute-start | bytes 3145736 | tf_op jit(solution)/shard_map/ppermute | solution.py:19
  329.9 48.4 %collective-permute-start.44 = (bf16[256,4096]{1,0:T(8,128)(2,1)}, bf16[256,4096]{1,0:T(8,128)(2,1)}, u32[]{:S(2)}, u32[]{:S(2)}) collective-permute-start(bf16[256,4096]{1,0:T(8,128)(2,1)} %outer.19), channel_id=1, source_target_pairs={{0,2},{1,3},{2,0},{3,1},{4,6},{5,7},{6,4},{7,5},{8,10},{9,11},{10,... | collective-permute-start | bytes 6291464 | tf_op jit(solution)/shard_map/ppermute | solution.py:24
  331.5 30.6 %collective-permute-start.34 = (bf16[256,2048]{1,0:T(8,128)(2,1)}, bf16[256,2048]{1,0:T(8,128)(2,1)}, u32[]{:S(2)}, u32[]{:S(2)}) collective-permute-start(bf16[256,2048]{1,0:T(8,128)(2,1)} %get-tuple-element.144), channel_id=1, source_target_pairs={{0,1},{1,0},{2,3},{3,2},{4,5},{5,4},{6,7},{7,6},{8,9},{9,8},{10,11... | collective-permute-start | bytes 3145736 | tf_op jit(solution)/shard_map/ppermute | solution.py:19
  331.7 30.5 %collective-permute-start.35 = (bf16[256,2048]{1,0:T(8,128)(2,1)}, bf16[256,2048]{1,0:T(8,128)(2,1)}, u32[]{:S(2)}, u32[]{:S(2)}) collective-permute-start(bf16[256,2048]{1,0:T(8,128)(2,1)} %get-tuple-element.145), channel_id=1, source_target_pairs={{0,1},{1,0},{2,3},{3,2},{4,5},{5,4},{6,7},{7,6},{8,9},{9,8},{10,11... | collective-permute-start | bytes 3145736 | tf_op jit(solution)/shard_map/ppermute | solution.py:19
  336.3 47.5 %all-to-all-start.1 = ((bf16[4,256,512]{2,1,0:T(8,128)(2,1)}), bf16[4,256,512]{2,1,0:T(8,128)(2,1)}, u32[]{:S(2)}, u32[]{:S(2)}) async-start(bf16[4,256,512]{2,1,0:T(8,128)(2,1)} %bitcast.175), calls=%async_computation.1 | async-start | bytes 2097152 | tf_op jit(solution)/shard_map/all_to_all | solution.py:31
  356.4 17.6 %collective-permute-start.42 = (bf16[256,2048]{1,0:T(8,128)(2,1)}, bf16[256,2048]{1,0:T(8,128)(2,1)S(1)}, u32[]{:S(2)}, u32[]{:S(2)}) collective-permute-start(bf16[256,2048]{1,0:T(8,128)(2,1)} %get-tuple-element.132), channel_id=1, source_target_pairs={{0,1},{1,0},{2,3},{3,2},{4,5},{5,4},{6,7},{7,6},{8,9},{9,8},{10,11... | collective-permute-start | bytes 3145736 | tf_op jit(solution)/shard_map/ppermute | solution.py:19
  383.8 53.2 %all-to-all-start.2 = ((bf16[4,64,4096]{2,1,0:T(8,128)(2,1)}), bf16[4,64,4096]{2,1,0:T(8,128)(2,1)}, u32[]{:S(2)}, u32[]{:S(2)}) async-start(bf16[4,64,4096]{2,1,0:T(8,128)(2,1)} %bitcast.171), calls=%async_computation.2 | async-start | bytes 4194304 | tf_op jit(solution)/shard_map/all_to_all | solution.py:31
  389.0 26.2 %collective-permute-start.31 = (bf16[128,4096]{1,0:T(8,128)(2,1)S(1)}, bf16[128,4096]{1,0:T(8,128)(2,1)S(1)}, u32[]{:S(2)}, u32[]{:S(2)}) collective-permute-start(bf16[128,4096]{1,0:T(8,128)(2,1)S(1)} %slice.206), channel_id=1, source_target_pairs={{0,2},{1,3},{2,0},{3,1},{4,6},{5,7},{6,4},{7,5},{8,10},{9,11},{10,... | collective-permute-start | bytes 3145736 | tf_op jit(solution)/shard_map/ppermute | solution.py:24
  390.6 68.0 %collective-permute-start.36 = (bf16[256,4096]{1,0:T(8,128)(2,1)}, bf16[256,4096]{1,0:T(8,128)(2,1)}, u32[]{:S(2)}, u32[]{:S(2)}) collective-permute-start(bf16[256,4096]{1,0:T(8,128)(2,1)} %outer.23), channel_id=1, source_target_pairs={{0,2},{1,3},{2,0},{3,1},{4,6},{5,7},{6,4},{7,5},{8,10},{9,11},{10,... | collective-permute-start | bytes 6291464 | tf_op jit(solution)/shard_map/ppermute | solution.py:24
  437.1 28.7 %all-to-all-start.3 = ((bf16[4,32,4096]{2,1,0:T(8,128)(2,1)}), bf16[4,32,4096]{2,1,0:T(8,128)(2,1)S(1)}, u32[]{:S(2)}, u32[]{:S(2)}) async-start(bf16[4,32,4096]{2,1,0:T(8,128)(2,1)} %bitcast.83), calls=%async_computation.3 | async-start | bytes 2097152 | tf_op jit(solution)/shard_map/all_to_all | solution.py:31
  466.8 51.3 %all-to-all-start.4 = ((bf16[4,64,4096]{2,1,0:T(8,128)(2,1)}), bf16[4,64,4096]{2,1,0:T(8,128)(2,1)S(1)}, u32[]{:S(2)}, u32[]{:S(2)}) async-start(bf16[4,64,4096]{2,1,0:T(8,128)(2,1)} %bitcast.172), calls=%async_computation.4 | async-start | bytes 4194304 | tf_op jit(solution)/shard_map/all_to_all | solution.py:31
  518.1 17.4 %all-to-all-start.5 = ((bf16[4,64,1024]{2,1,0:T(8,128)(2,1)}), bf16[4,64,1024]{2,1,0:T(8,128)(2,1)S(1)}, u32[]{:S(2)}, u32[]{:S(2)}) async-start(bf16[4,64,1024]{2,1,0:T(8,128)(2,1)} %bitcast.85), calls=%async_computation.5 | async-start | bytes 1048576 | tf_op jit(solution)/shard_map/all_to_all | solution.py:31
  (66 other events, 594.5 us)
Sparse Core Ops, SparseCore 0:
  11.4 163.4 all-gather.1
